TPU v7x, 32 devices: a whole 2x2x4 slice. The times are simulated.
32 devices in a mesh: aux: 8 (over z, y), pair: 4 (over x, core).
Axes of the slice: x: 2, y: 2, z: 4, core: 2. Of those that a mesh axis runs over, the one named last changes fastest.
Arguments:
- half_ints: bfloat16 [24, 1408, 4096], P('pair', None, 'aux'), may hold values from -0.75 to 0.75
- vir_coeffs: bfloat16 [1408, 1280], P(None, 'aux'), may hold values from -0.15625 to 0.15625
- occ_energy: float32 [24], replicated, may hold values from -2 to -0.3
- vir_energy: float32 [1280], replicated, may hold values from 0.3 to 4
- roster: int32 [8, 2], replicated, may hold values from 0 to 3
Outputs:
- density: bfloat16 [1280, 24, 4096], P('pair', 'aux')
All inputs are finite; a program needn't handle non-finite values.
Results may differ from a plain program's by a relative error of at most 0.0058.
Values may be sent and summed in bfloat16 or wider, within the bound.
No kernel may reach another device: no remote copies, remote signals or barrier semaphores. Data moves between devices by JAX's collectives and lax.ppermute only.
A program may use at most 128 MiB of HBM per device.

v0:
```python
import jax
import jax.numpy as jnp
from jax import lax
from jax.sharding import PartitionSpec as P

spin_scale = 1.3


def broadcast(value, axis, source):
    kept = jnp.where(lax.axis_index(axis) == source, value, 0).astype(value.dtype)
    return lax.psum(kept, axis)


def per_device(half_ints, vir_coeffs, occ_energy, vir_energy, roster):
    occ_rows = half_ints.shape[0]
    aux_slice = half_ints.shape[2]
    half_flat = jnp.transpose(half_ints, (1, 0, 2)).reshape(
        half_ints.shape[1], occ_rows * aux_slice
    )
    columns = lax.all_gather(vir_coeffs, "aux", axis=1, tiled=True)
    product = jnp.dot(jnp.transpose(columns), half_flat, preferred_element_type=jnp.float32)
    vir_ints = product.astype(jnp.bfloat16).reshape(columns.shape[1], occ_rows, aux_slice)
    by_virtual = lax.all_to_all(vir_ints, "pair", split_axis=0, concat_axis=1, tiled=True)
    aux_count = lax.axis_size("aux")
    aux_index = lax.axis_index("aux")
    pair_index = lax.axis_index("pair")
    vir_width = by_virtual.shape[0]
    occ_width = by_virtual.shape[1] // aux_count
    step_count = roster.shape[1]
    block_plan = lax.dynamic_index_in_dim(roster, aux_index, 0, keepdims=False)
    sources = []
    for position in range(step_count):
        sources.append(lax.dynamic_index_in_dim(block_plan, position, 0, keepdims=False))
    own_block = lax.all_to_all(by_virtual, "aux", split_axis=1, concat_axis=2, tiled=True)
    remotes = [broadcast(own_block, "pair", source) for source in sources]
    aux_total = own_block.shape[2]
    flat_local = own_block.reshape(vir_width * occ_width, aux_total)
    occ_block = lax.dynamic_slice_in_dim(occ_energy, aux_index * occ_width, occ_width, 0)
    vir_block = lax.dynamic_slice_in_dim(vir_energy, pair_index * vir_width, vir_width, 0)
    energy_left = (vir_block[:, None] - occ_block[None, :]).reshape(-1)
    density = jnp.zeros((vir_width * occ_width, aux_total), jnp.float32)
    for position in range(step_count):
        flat_remote = remotes[position].reshape(vir_width * occ_width, aux_total)
        energy_block = lax.dynamic_slice_in_dim(
            vir_energy, sources[position] * vir_width, vir_width, 0
        )
        energy_right = (energy_block[:, None] - occ_block[None, :]).reshape(-1)
        integrals = jnp.dot(
            flat_local, jnp.transpose(flat_remote), preferred_element_type=jnp.float32
        )
        amplitudes = (
            spin_scale * integrals / (energy_left[:, None] + energy_right[None, :])
        ).astype(jnp.bfloat16)
        density = density + jnp.dot(amplitudes, flat_remote, preferred_element_type=jnp.float32)
    return density.astype(jnp.bfloat16).reshape(vir_width, occ_width, aux_total)


def solution(mesh):
    in_specs = (P("pair", None, "aux"), P(None, "aux"), P(), P(), P())
    out_specs = P("pair", "aux", None)
    return jax.shard_map(
        per_device, mesh=mesh, in_specs=in_specs, out_specs=out_specs, check_vma=False
    )
```

profile of v0, /device:TPU:0, one launch (start us, length us, event | category | flops | bytes accessed | tf_op | source)
XLA Modules:
  0.0 847.9 jit_solution(55702938888071626)
XLA Ops:
  6.5 0.7 all-gather.2.cloned.1.call-update
  7.3 11.5 %copy.22 = bf16[6,1408,512]{1,2,0:T(8,128)(2,1)} copy(bf16[6,1408,512]{2,1,0:T(8,128)(2,1)} %param.5) | data formatting | bytes 17301504 | tf_op args[0]
  18.8 59.5 %all-gather.2.cloned.1.call-done = bf16[1408,1280]{0,1:T(8,128)(2,1)} async-done(((bf16[1408,160]{0,1:T(8,128)(2,1)}), bf16[1408,1280]{0,1:T(8,128)(2,1)}) %all-gather.2.cloned.1.call-update) | async-done | bytes 3604496 | tf_op jit(solution)/shard_map/all_gather | solution.py:20
  78.3 17.9 %convolution_convert_fusion = bf16[1280,3072]{1,0:T(8,128)(2,1)} fusion(bf16[1408,1280]{0,1:T(8,128)(2,1)} %all-gather.2.cloned.1.call-done, bf16[1408,3072]{0,1:T(8,128)(2,1)} %bitcast.40), kind=kOutput, calls=%fused_computation.1 | convolution fusion | flops 11076894720 | bytes 20119552 | tf_op jit(solution)/shard_map/dot_general | solution.py:21
  96.2 10.5 %copy.23 = bf16[1280,3072]{0,1:T(8,128)(2,1)} copy(bf16[1280,3072]{1,0:T(8,128)(2,1)} %convolution_convert_fusion) | data formatting | bytes 15728640 | tf_op jit(solution)/shard_map/convert_element_type | solution.py:22
  106.7 15.4 %copy.24 = bf16[1280,6,512]{2,1,0:T(8,128)(2,1)} copy(bf16[1280,6,512]{0,2,1:T(8,128)(2,1)} %bitcast.36) | data formatting | bytes 15728640 | tf_op jit(solution)/shard_map/reshape | solution.py:22
  122.1 124.1 %all_to_all.33 = bf16[1280,6,512]{2,1,0:T(8,128)(2,1)} all-to-all(bf16[1280,6,512]{2,1,0:T(8,128)(2,1)} %copy.24), channel_id=1, replica_groups=mesh['aux'=8,'pair'=4] {'pair'}, dimensions={0} | all-to-all | bytes 15728640 | tf_op jit(solution)/shard_map/all_to_all | solution.py:23
  246.1 10.2 %copy.26 = bf16[320,4,6,512]{3,0,2,1:T(8,128)(2,1)} copy(bf16[320,4,6,512]{3,2,0,1:T(8,128)(2,1)} %bitcast.30) | data formatting | bytes 15728640 | tf_op jit(solution)/shard_map/all_to_all | solution.py:23
  256.4 4.9 all-to-all-start.1
  261.3 0.2 all-reduce.3.cloned.1.call-start
  261.6 0.5 fusion.10
  263.3 169.7 %all-to-all-done.1 = bf16[320,24,512]{2,0,1:T(8,128)(2,1)} async-done(((bf16[320,24,512]{2,0,1:T(8,128)(2,1)}), bf16[320,24,512]{2,0,1:T(8,128)(2,1)}, u32[]{:S(2)}, u32[]{:S(2)}) %all-to-all-start.1) | async-done | bytes 7864352 | tf_op jit(solution)/shard_map/all_to_all | solution.py:34
  433.0 10.0 %broadcast_select_fusion = (bf16[320,3,8,512]{3,0,1,2:T(8,128)(2,1)}, bf16[320,3,8,512]{3,0,1,2:T(8,128)(2,1)}) fusion(bf16[320,3,8,512]{3,0,1,2:T(8,128)(2,1)} %bitcast.8, pred[]{:T(512)S(6)} %eq.7, pred[]{:T(512)S(6)} %eq.6), kind=kLoop, calls=%fused_computation.2 | loop fusion | flops 7864320 | bytes 23592962 | tf_op jit(solution)/shard_map/jit(_where)/select_n | solution.py:10
  443.0 11.0 %copy.29 = bf16[320,3,8,512]{3,2,1,0:T(8,128)(2,1)} copy(bf16[320,3,8,512]{3,0,1,2:T(8,128)(2,1)} %get-tuple-element.7) | data formatting | bytes 15728640 | tf_op jit(solution)/shard_map/jit(_where)/select_n | solution.py:10
  454.0 11.8 %copy.34 = bf16[120,8,8,512]{3,1,2,0:T(8,128)(2,1)} copy(bf16[120,8,8,512]{3,2,1,0:T(8,128)(2,1)} %bitcast.37) | data formatting | bytes 15728640
  465.8 7.9 copy.28
  473.7 11.6 %copy.33 = bf16[120,8,8,512]{3,1,2,0:T(8,128)(2,1)} copy(bf16[120,8,8,512]{3,2,1,0:T(8,128)(2,1)} %bitcast.38) | data formatting | bytes 15728640
  487.5 9.5 %copy.27 = bf16[320,3,8,512]{3,2,1,0:T(8,128)(2,1)S(1)} copy(bf16[320,3,8,512]{3,0,1,2:T(8,128)(2,1)} %bitcast.8) | data formatting | bytes 15728640 | tf_op jit(solution)/shard_map/all_to_all | solution.py:34
  497.0 8.5 copy.32
  505.4 250.2 %all-reduce.3.cloned.1.call-done = (bf16[960,4096]{1,0:T(8,128)(2,1)}, bf16[960,4096]{1,0:T(8,128)(2,1)}) async-done(((bf16[960,4096]{1,0:T(8,128)(2,1)}, bf16[960,4096]{1,0:T(8,128)(2,1)}), (bf16[960,4096]{1,0:T(8,128)(2,1)}, bf16[960,4096]{1,0:T(8,128)(2,1)})) %all-reduce.3.cloned.1.call-update) | async-done | bytes 15728656 | tf_op jit(solution)/shard_map/psum | solution.py:11
  755.7 27.8 %fusion = f32[960,4096]{1,0:T(8,128)} fusion(bf16[960,4096]{1,0:T(8,128)(2,1)} %get-tuple-element.5, bf16[960,4096]{1,0:T(8,128)(2,1)} %bitcast.41, f32[960]{0:T(1024)S(1)} %sub.62, f32[960]{0:T(1024)S(1)} %sub.59), kind=kOutput, calls=%fused_computation.6 | convolution fusion | flops 15103180800 | bytes 31464960 | tf_op jit(solution)/shard_map/dot_general | solution.py:54
  783.5 28.5 %add_convert_fusion = bf16[960,4096]{1,0:T(8,128)(2,1)} fusion(f32[960,4096]{1,0:T(8,128)} %fusion, bf16[960,4096]{1,0:T(8,128)(2,1)} %get-tuple-element.6, bf16[960,4096]{1,0:T(8,128)(2,1)} %bitcast.42, f32[960]{0:T(1024)S(1)} %sub.65, f32[960]{0:T(1024)S(1)} %sub.59), kind=kOutput, calls=%fused_computation | convolution fusion | flops 15111045120 | bytes 39329280 | tf_op jit(solution)/shard_map/dot_general | solution.py:54
  812.0 16.0 %reshape.80 = bf16[320,3,4096]{2,1,0:T(4,128)(2,1)} reshape(bf16[960,4096]{1,0:T(8,128)(2,1)} %add_convert_fusion) | data formatting | bytes 15728640 | tf_op jit(solution)/shard_map/reshape | solution.py:55
  828.0 12.9 %copy.30 = bf16[320,3,4096]{2,0,1:T(8,128)(2,1)} copy(bf16[320,3,4096]{2,1,0:T(4,128)(2,1)} %reshape.80) | data formatting | bytes 15728640 | tf_op jit(solution)/shard_map/reshape | solution.py:55
  (22 shorter events, 1.1 us)
Async XLA Ops:
  6.5 255.0 %copy-start = (s32[8,2]{0,1:T(2,128)S(1)}, s32[8,2]{0,1:T(2,128)}, u32[]{:S(2)}) copy-start(s32[8,2]{0,1:T(2,128)} %param.9) | copy-start | bytes 196
  6.5 71.7 %all-gather.2.cloned.1.call-start = ((), (), s32[]{:S(2)}) async-start(), calls=%async_computation.2 | async-start | bytes 4055040 | tf_op jit(solution)/shard_map/all_gather | solution.py:20
  256.4 176.7 %all-to-all-start.1 = ((bf16[320,24,512]{2,0,1:T(8,128)(2,1)}), bf16[320,24,512]{2,0,1:T(8,128)(2,1)}, u32[]{:S(2)}, u32[]{:S(2)}) async-start(bf16[320,24,512]{2,0,1:T(8,128)(2,1)} %bitcast.33), calls=%async_computation.1 | async-start | bytes 15728640 | tf_op jit(solution)/shard_map/all_to_all | solution.py:34
  261.3 494.4 %all-reduce.3.cloned.1.call-start = ((), (), s32[]{:S(2)}) async-start(), calls=%async_computation.3 | async-start | bytes 31457280 | tf_op jit(solution)/shard_map/psum | solution.py:11
  443.0 22.8 %slice-start = ((s8[7864320]{0:T(1024)(128)(4,1)}), s8[4194304]{0:T(1024)(128)(4,1)S(1)}, s32[]{:S(2)}) async-start(s8[7864320]{0:T(1024)(128)(4,1)} %bitcast.34), calls=%async_computation.4 | async-start | bytes 8388608
  454.0 11.8 %slice-start.1 = ((s8[7864320]{0:T(1024)(128)(4,1)}), s8[3670016]{0:T(1024)(128)(4,1)S(1)}, s32[]{:S(2)}) async-start(s8[7864320]{0:T(1024)(128)(4,1)} %bitcast.34), calls=%async_computation.5 | async-start | bytes 7340032
  485.3 1.2 copy-start.3
  485.3 1.3 copy-start.2
  812.0 28.9 %copy-start.1 = (s32[8,2]{0,1:T(2,128)S(1)}, s32[8,2]{0,1:T(2,128)}, u32[]{:S(2)}) copy-start(s32[8,2]{0,1:T(2,128)} %param.9) | copy-start | bytes 196
Sparse Core Ops, SparseCore 0:
  9.5 68.6 all-gather.1
  485.4 270.1 all-reduce.2
where the time goes:
time: 856 us; the launch traced here: 848 us
  waiting for transfers between devices  480 us (56%)
  local copies, waits for them, and re-layouts  138 us (16%)
  blocking collectives  124 us (14%)
  matrix products  74.2 us (9%)
  between operations  16.1 us (2%)
  other arithmetic  10.2 us (1%)
    psum x1, waiting for transfers between devices, broadcast(): return lax.psum(kept, axis)  250 us
    all_to_all x1, waiting for transfers between devices, per_device(): lax.all_to_all(by_virtual, 'aux', split_axis=1, concat_axis=2, tiled=True)  170 us
    all_to_all x1, blocking collectives, per_device(): lax.all_to_all(vir_ints, 'pair', split_axis=0, concat_axis=1, tiled=True)  124 us
    all_gather x1, waiting for transfers between devices, per_device(): columns = lax.all_gather(vir_coeffs, 'aux', axis=1, tiled=True)  59.5 us
    dot_general x2, matrix products, per_device(): jnp.dot(amplitudes, flat_remote, preferred_element_type=jnp.float32)  56.3 us
    unnamed x16, local copies, waits for them, and re-layouts  43.4 us
    reshape x2, local copies, waits for them, and re-layouts, per_device(): return density.astype(jnp.bfloat16).reshape(vir_width, occ_width, aux_total)  28.9 us
    select_n x2, local copies, waits for them, and re-layouts, broadcast(): jnp.where(lax.axis_index(axis) == source, value, 0).astype(value.dtype)  18.9 us
  transfers between devices with their start and end apart: 3, of which 3 were waited for; matrix products, arithmetic and copies ran while one was open for 4% of the time, Pallas kernels for 0%

commit v1 on v0

v1 whole, which is shorter than its diff:
```python
import functools

import jax
import jax.numpy as jnp
from jax import lax
from jax.experimental import pallas as pl
from jax.experimental.pallas import tpu as pltpu
from jax.sharding import PartitionSpec as P

spin_scale = 1.3
VMEM_LIMIT = 56 * 1024 * 1024


def swap(value, distance):
    count = lax.axis_size("pair")
    pairs = [(source, source ^ distance) for source in range(count)]
    return lax.ppermute(value, "pair", pairs)


def transform_kernel(width, index_ref, coeff_ref, half_ref, *out_refs):
    half = half_ref[0, 0]
    for distance, out_ref in enumerate(out_refs):
        start = pl.multiple_of((index_ref[0] ^ distance) * width, width)
        product = jnp.dot(
            coeff_ref[pl.ds(start, width), :], half, preferred_element_type=jnp.float32
        )
        out_ref[0] = product.astype(out_ref.dtype)


def transform(coeff_rows, half, orbital, pair_index):
    pair_count = lax.axis_size("pair")
    blocks, _, depth, aux_slice = half.shape
    width = coeff_rows.shape[0] // pair_count
    grid_spec = pltpu.PrefetchScalarGridSpec(
        num_scalar_prefetch=1,
        grid=(blocks,),
        in_specs=[
            pl.BlockSpec(coeff_rows.shape, lambda b, index: (0, 0)),
            pl.BlockSpec((1, 1, depth, aux_slice), lambda b, index: (b, orbital, 0, 0)),
        ],
        out_specs=[
            pl.BlockSpec((1, width, aux_slice), lambda b, index: (b, 0, 0))
        ] * pair_count,
    )
    return pl.pallas_call(
        functools.partial(transform_kernel, width),
        grid_spec=grid_spec,
        out_shape=[jax.ShapeDtypeStruct((blocks, width, aux_slice), jnp.bfloat16)] * pair_count,
        compiler_params=pltpu.CompilerParams(vmem_limit_bytes=VMEM_LIMIT),
        cost_estimate=pl.CostEstimate(
            flops=2 * blocks * coeff_rows.size * aux_slice,
            bytes_accessed=2 * (coeff_rows.size + blocks * (depth + coeff_rows.shape[0]) * aux_slice),
            transcendentals=0,
        ),
        name="transform",
    )(pair_index.reshape(1), coeff_rows, half)


def density_kernel(occ_width, remote_count, slices, has_total, *refs):
    left_energy, right_energy = refs[:2]
    local_refs = refs[2 : 2 + occ_width]
    remote_refs = refs[2 + occ_width : 2 + occ_width + remote_count]
    total_ref = refs[2 + occ_width + remote_count] if has_total else None
    out_ref, integrals, amplitudes = refs[-3:]
    step = pl.program_id(0)
    remote = jnp.concatenate([ref[0] for ref in remote_refs], axis=0)

    @pl.when(step < slices)
    def _():
        local = jnp.concatenate([ref[0] for ref in local_refs], axis=0)
        product = lax.dot_general(
            local, remote, (((1,), (1,)), ((), ())), preferred_element_type=jnp.float32
        )

        @pl.when(step == 0)
        def _():
            integrals[...] = product

        @pl.when(step > 0)
        def _():
            integrals[...] += product

        @pl.when(step == slices - 1)
        def _():
            gap = left_energy[...] + right_energy[...]
            amplitudes[...] = (spin_scale * integrals[...] / gap).astype(jnp.bfloat16)

    @pl.when(step >= slices)
    def _():
        product = jnp.dot(amplitudes[...], remote, preferred_element_type=jnp.float32)
        if has_total:
            product = product + total_ref[...]
        out_ref[...] = product.astype(out_ref.dtype)


def add_density(locals_, remotes, left_energy, right_energy, total, out_dtype):
    occ_width = len(locals_)
    slices, width, aux_slice = locals_[0].shape
    rows = occ_width * width
    columns = sum(remote.shape[1] for remote in remotes)
    in_specs = [
        pl.BlockSpec((rows, 1), lambda t: (0, 0)),
        pl.BlockSpec((1, columns), lambda t: (0, 0)),
    ]
    in_specs += [
        pl.BlockSpec((1, width, aux_slice), lambda t: (jnp.minimum(t, slices - 1), 0, 0))
    ] * occ_width
    in_specs += [
        pl.BlockSpec((1, remote.shape[1], aux_slice), lambda t: (t % slices, 0, 0))
        for remote in remotes
    ]
    out_spec = pl.BlockSpec((rows, aux_slice), lambda t: (0, jnp.maximum(t - slices, 0)))
    operands = [left_energy, right_energy, *locals_, *remotes]
    moved = 2 * slices * aux_slice * (rows + 2 * columns)
    if total is not None:
        in_specs.append(out_spec)
        operands.append(total)
        moved += total.size * 4
    out_shape = jax.ShapeDtypeStruct((rows, slices * aux_slice), out_dtype)
    moved += out_shape.size * out_shape.dtype.itemsize
    return pl.pallas_call(
        functools.partial(density_kernel, occ_width, len(remotes), slices, total is not None),
        grid=(2 * slices,),
        in_specs=in_specs,
        out_specs=out_spec,
        out_shape=out_shape,
        scratch_shapes=[
            pltpu.VMEM((rows, columns), jnp.float32),
            pltpu.VMEM((rows, columns), jnp.bfloat16),
        ],
        compiler_params=pltpu.CompilerParams(vmem_limit_bytes=VMEM_LIMIT),
        cost_estimate=pl.CostEstimate(
            flops=4 * rows * columns * slices * aux_slice,
            bytes_accessed=moved,
            transcendentals=0,
        ),
        name="density",
    )(*operands)


def per_device(half_ints, vir_coeffs, occ_energy, vir_energy, roster):
    pair_count = lax.axis_size("pair")
    aux_count = lax.axis_size("aux")
    pair_index = lax.axis_index("pair")
    aux_index = lax.axis_index("aux")
    core = pair_index % 2
    occ_rows, depth, aux_slice = half_ints.shape
    row_blocks = aux_count // pair_count
    occ_width = occ_rows // row_blocks
    step_count = roster.shape[1]

    coeff_rows = lax.all_gather(jnp.transpose(vir_coeffs), "aux", axis=0, tiled=True)
    vir_width = coeff_rows.shape[0] // pair_count
    part = vir_width // 2
    half = half_ints.reshape(row_blocks, occ_width, depth, aux_slice)

    sources = lax.dynamic_index_in_dim(roster, aux_index, 0, keepdims=False)
    occ_block = lax.dynamic_slice_in_dim(occ_energy, aux_index * occ_width, occ_width, 0)
    vir_block = lax.dynamic_slice_in_dim(vir_energy, pair_index * vir_width, vir_width, 0)
    left_energy = (vir_block[None, :] - occ_block[:, None]).reshape(-1, 1)

    locals_ = []
    for orbital in range(occ_width):
        parts = transform(coeff_rows, half, orbital, pair_index)
        gathered = jnp.zeros((aux_count, vir_width, aux_slice), jnp.bfloat16)
        for distance, piece in enumerate(parts):
            if distance:
                piece = swap(piece, distance)
            start = (pair_index ^ distance) * row_blocks
            gathered = lax.dynamic_update_slice_in_dim(gathered, piece, start, 0)
        locals_.append(lax.all_to_all(gathered, "aux", split_axis=0, concat_axis=0, tiled=True))

    total = None
    for orbital in range(occ_width):
        local = locals_[orbital]
        own = lax.dynamic_slice_in_dim(local, core * part, part, 1)
        other = lax.dynamic_slice_in_dim(local, (1 - core) * part, part, 1)
        mate = swap(other, 1)
        remotes, energies = [], []
        for position in range(step_count):
            source = sources[position]
            held = jnp.where(source == pair_index, own, mate)
            distance = 2
            while distance < pair_count:
                arrived = swap(held, distance)
                near = (source // distance) % 2 == (pair_index // distance) % 2
                held = jnp.where(near, held, arrived)
                distance *= 2
            remotes += [held, swap(held, 1)]
            for side in (core, 1 - core):
                start = source * vir_width + side * part
                energy = lax.dynamic_slice_in_dim(vir_energy, start, part, 0)
                energies.append(energy - occ_block[orbital])
        right_energy = jnp.concatenate(energies).reshape(1, -1)
        last = orbital == occ_width - 1
        total = add_density(
            locals_, remotes, left_energy, right_energy, total, jnp.bfloat16 if last else jnp.float32
        )
    aux_total = total.shape[1]
    return jnp.transpose(total.reshape(occ_width, vir_width, aux_total), (1, 0, 2))


def solution(mesh):
    in_specs = (P("pair", None, "aux"), P(None, "aux"), P(), P(), P())
    out_specs = P("pair", "aux", None)
    return jax.shard_map(
        per_device, mesh=mesh, in_specs=in_specs, out_specs=out_specs, check_vma=False
    )
```

time: 856 us -> 578 us (0.68)
  blocking collectives: 124 us -> 0 us
  local copies, waits for them, and re-layouts: 138 us -> 27.3 us
  Pallas kernels: 0 us -> 103 us
  waiting for transfers between devices: 480 us -> 378 us
  matrix products: 74.2 us -> 0 us
  starting transfers between devices: 5.12 us -> 26.3 us
  other arithmetic: 10.2 us -> 21.2 us
    psum x1 -> x0, waiting for transfers between devices: 250 us -> none  [broadcast(): return lax.psum(kept, axis)]
    ppermute x0 -> x24, waiting for transfers between devices: none -> 217 us  [swap(): return lax.ppermute(value, 'pair', pairs)]
    all_to_all x1 -> x0, blocking collectives: 124 us -> none  [per_device(): lax.all_to_all(vir_ints, 'pair', split_axis=0, concat_axis=1, tiled=True)]
    pallas_call x0 -> x6, Pallas kernels: none -> 103 us  [the longest x3 79.8 us: add_density(): pl.pallas_call(functools.partial(density_kernel, occ_width, len(remotes),...]
    all_to_all x1 -> x3, waiting for transfers between devices: 170 us -> 89.4 us  [per_device(): lax.all_to_all(gathered, 'aux', split_axis=0, concat_axis=0, tiled=True)]
    dot_general x3 -> x0, matrix products: 74.2 us -> none  [the longest x2 56.3 us: per_device(): jnp.dot(amplitudes, flat_remote, preferred_element_type=jnp.float32)]
    reshape x3, local copies, waits for them, and re-layouts: 44.3 us -> 1.77 us  [per_device(): right_energy = jnp.concatenate(energies).reshape(1, -1)]
    unnamed x16 -> x26, local copies, waits for them, and re-layouts: 43.4 us -> 1.09 us
  transfers between devices with their start and end apart: 3 -> 28, of which waited for: 3 -> 16; matrix products, arithmetic and copies ran while one was open for 4% -> 8% of each run, Pallas kernels for 0% -> 12%
where the time goes in v1:
time: 578 us; the launch traced here: 576 us
  waiting for transfers between devices  378 us (65%)
  Pallas kernels  103 us (18%)
  local copies, waits for them, and re-layouts  27.3 us (5%)
  starting transfers between devices  26.3 us (5%)
  other arithmetic  21.2 us (4%)
  between operations  21.1 us (4%)
    ppermute x24, waiting for transfers between devices, swap(): return lax.ppermute(value, 'pair', pairs)  217 us
    all_to_all x3, waiting for transfers between devices, per_device(): lax.all_to_all(gathered, 'aux', split_axis=0, concat_axis=0, tiled=True)  89.4 us
    pallas_call x3, Pallas kernels, add_density(): pl.pallas_call(functools.partial(density_kernel, occ_width, len(remotes),...  79.8 us
    all_gather x1, waiting for transfers between devices, per_device(): lax.all_gather(jnp.transpose(vir_coeffs), 'aux', axis=0, tiled=True)  71 us
    pallas_call x3, Pallas kernels, transform(): pl.pallas_call(functools.partial(transform_kernel, width), grid_spec=grid...  22.9 us
    ppermute x24, starting transfers between devices, swap(): return lax.ppermute(value, 'pair', pairs)  13.7 us
    all_to_all x3, starting transfers between devices, per_device(): lax.all_to_all(gathered, 'aux', split_axis=0, concat_axis=0, tiled=True)  12.6 us
  transfers between devices with their start and end apart: 28, of which 16 were waited for; matrix products, arithmetic and copies ran while one was open for 8% of the time, Pallas kernels for 12%

profile of v1, /device:TPU:0, one launch (start us, length us, event | category | flops | bytes accessed | tf_op | source)
XLA Modules:
  0.0 576.3 jit_solution(7712306250780861084)
XLA Ops:
  7.3 71.0 %all-gather.2.cloned.1.call-done.coeff_ref = bf16[1280,1408]{1,0:T(8,128)(2,1)} async-done(((bf16[160,1408]{1,0:T(8,128)(2,1)}), bf16[1280,1408]{1,0:T(8,128)(2,1)}) %all-gather.2.cloned.1.call-update) | async-done | bytes 3604496 | tf_op jit(solution)/shard_map/all_gather | solution.py:152
  78.3 7.6 %transform.3 = (bf16[2,320,512]{2,1,0:T(8,128)(2,1)}, bf16[2,320,512]{2,1,0:T(8,128)(2,1)}, bf16[2,320,512]{2,1,0:T(8,128)(2,1)}, bf16[2,320,512]{2,1,0:T(8,128)(2,1)}) custom-call(s32[1]{0:T(128)} %bitcast.3.index_ref, bf16[1280,1408]{1,0:T(8,128)(2,1)} %all-gather.2.cloned.1.call-done.coeff_ref, bf16[2,3,1408,512]{3,2,1,0:T(8,128)(2,1)} %bitcast.12), custom_call_target="tpu_custom_call" | custom-call | flops 3690987520 | bytes 9109504 | tf_op jit(solution)/shard_map/transform/pallas_call | solution.py:45
  91.3 12.4 %collective-permute-done.1 = bf16[2,320,512]{2,1,0:T(8,128)(2,1)S(1)} collective-permute-done((bf16[2,320,512]{2,1,0:T(8,128)(2,1)}, bf16[2,320,512]{2,1,0:T(8,128)(2,1)S(1)}, u32[]{:S(2)}, u32[]{:S(2)}) %collective-permute-start.1) | collective-permute-done | bytes 655392 | tf_op jit(solution)/shard_map/ppermute | solution.py:17
  104.6 12.3 %collective-permute-done.2 = bf16[2,320,512]{2,1,0:T(8,128)(2,1)S(1)} collective-permute-done((bf16[2,320,512]{2,1,0:T(8,128)(2,1)}, bf16[2,320,512]{2,1,0:T(8,128)(2,1)S(1)}, u32[]{:S(2)}, u32[]{:S(2)}) %collective-permute-start.2) | collective-permute-done | bytes 655392 | tf_op jit(solution)/shard_map/ppermute | solution.py:17
  121.4 7.6 %transform.4 = (bf16[2,320,512]{2,1,0:T(8,128)(2,1)}, bf16[2,320,512]{2,1,0:T(8,128)(2,1)}, bf16[2,320,512]{2,1,0:T(8,128)(2,1)}, bf16[2,320,512]{2,1,0:T(8,128)(2,1)}) custom-call(s32[1]{0:T(128)} %bitcast.3.index_ref, bf16[1280,1408]{1,0:T(8,128)(2,1)} %all-gather.2.cloned.1.call-done.coeff_ref, bf16[2,3,1408,512]{3,2,1,0:T(8,128)(2,1)} %bitcast.13), custom_call_target="tpu_custom_call" | custom-call | flops 3690987520 | bytes 9109504 | tf_op jit(solution)/shard_map/transform/pallas_call | solution.py:45
  134.4 12.6 %collective-permute-done.4 = bf16[2,320,512]{2,1,0:T(8,128)(2,1)S(1)} collective-permute-done((bf16[2,320,512]{2,1,0:T(8,128)(2,1)}, bf16[2,320,512]{2,1,0:T(8,128)(2,1)S(1)}, u32[]{:S(2)}, u32[]{:S(2)}) %collective-permute-start.4) | collective-permute-done | bytes 655392 | tf_op jit(solution)/shard_map/ppermute | solution.py:17
  147.9 11.8 %collective-permute-done.5 = bf16[2,320,512]{2,1,0:T(8,128)(2,1)S(1)} collective-permute-done((bf16[2,320,512]{2,1,0:T(8,128)(2,1)}, bf16[2,320,512]{2,1,0:T(8,128)(2,1)S(1)}, u32[]{:S(2)}, u32[]{:S(2)}) %collective-permute-start.5) | collective-permute-done | bytes 655392 | tf_op jit(solution)/shard_map/ppermute | solution.py:17
  160.6 20.8 %all-to-all-done.refs_2_ = bf16[8,320,512]{2,1,0:T(8,128)(2,1)S(1)} async-done(((bf16[8,320,512]{2,1,0:T(8,128)(2,1)}), bf16[8,320,512]{2,1,0:T(8,128)(2,1)S(1)}, u32[]{:S(2)}, u32[]{:S(2)}) %all-to-all-start) | async-done | bytes 2621472 | tf_op jit(solution)/shard_map/all_to_all | solution.py:171
  181.5 4.4 all-to-all-start.1
  185.9 7.6 %transform.5 = (bf16[2,320,512]{2,1,0:T(8,128)(2,1)}, bf16[2,320,512]{2,1,0:T(8,128)(2,1)}, bf16[2,320,512]{2,1,0:T(8,128)(2,1)}, bf16[2,320,512]{2,1,0:T(8,128)(2,1)}) custom-call(s32[1]{0:T(128)} %bitcast.3.index_ref, bf16[1280,1408]{1,0:T(8,128)(2,1)} %all-gather.2.cloned.1.call-done.coeff_ref, bf16[2,3,1408,512]{3,2,1,0:T(8,128)(2,1)} %bitcast.14), custom_call_target="tpu_custom_call" | custom-call | flops 3690987520 | bytes 9109504 | tf_op jit(solution)/shard_map/transform/pallas_call | solution.py:45
  198.9 12.4 %collective-permute-done.7 = bf16[2,320,512]{2,1,0:T(8,128)(2,1)S(1)} collective-permute-done((bf16[2,320,512]{2,1,0:T(8,128)(2,1)}, bf16[2,320,512]{2,1,0:T(8,128)(2,1)S(1)}, u32[]{:S(2)}, u32[]{:S(2)}) %collective-permute-start.7) | collective-permute-done | bytes 655392 | tf_op jit(solution)/shard_map/ppermute | solution.py:17
  212.1 12.4 %collective-permute-done.8 = bf16[2,320,512]{2,1,0:T(8,128)(2,1)S(1)} collective-permute-done((bf16[2,320,512]{2,1,0:T(8,128)(2,1)}, bf16[2,320,512]{2,1,0:T(8,128)(2,1)S(1)}, u32[]{:S(2)}, u32[]{:S(2)}) %collective-permute-start.8) | collective-permute-done | bytes 655392 | tf_op jit(solution)/shard_map/ppermute | solution.py:17
  225.4 19.8 %all-to-all-done.1.refs_3_ = bf16[8,320,512]{2,1,0:T(8,128)(2,1)} async-done(((bf16[8,320,512]{2,1,0:T(8,128)(2,1)}), bf16[8,320,512]{2,1,0:T(8,128)(2,1)}, u32[]{:S(2)}, u32[]{:S(2)}) %all-to-all-start.1) | async-done | bytes 2621472 | tf_op jit(solution)/shard_map/all_to_all | solution.py:171
  245.2 4.6 all-to-all-start.2
  260.0 48.7 %all-to-all-done.2.refs_4_ = bf16[8,320,512]{2,1,0:T(8,128)(2,1)} async-done(((bf16[8,320,512]{2,1,0:T(8,128)(2,1)}), bf16[8,320,512]{2,1,0:T(8,128)(2,1)}, u32[]{:S(2)}, u32[]{:S(2)}) %all-to-all-start.2) | async-done | bytes 2621472 | tf_op jit(solution)/shard_map/all_to_all | solution.py:171
  331.2 15.2 %collective-permute-done.22 = bf16[8,160,512]{2,1,0:T(8,128)(2,1)} collective-permute-done((bf16[8,160,512]{2,1,0:T(8,128)(2,1)}, bf16[8,160,512]{2,1,0:T(8,128)(2,1)}, u32[]{:S(2)}, u32[]{:S(2)}) %collective-permute-start.22) | collective-permute-done | bytes 1310752 | tf_op jit(solution)/shard_map/ppermute | solution.py:17
  350.5 24.1 %collective-permute-done.20 = bf16[8,160,512]{2,1,0:T(8,128)(2,1)} collective-permute-done((bf16[8,160,512]{2,1,0:T(8,128)(2,1)}, bf16[8,160,512]{2,1,0:T(8,128)(2,1)}, u32[]{:S(2)}, u32[]{:S(2)}) %collective-permute-start.20) | collective-permute-done | bytes 1310752 | tf_op jit(solution)/shard_map/ppermute | solution.py:17
  377.1 25.5 %collective-permute-done.17 = bf16[8,160,512]{2,1,0:T(8,128)(2,1)} collective-permute-done((bf16[8,160,512]{2,1,0:T(8,128)(2,1)S(1)}, bf16[8,160,512]{2,1,0:T(8,128)(2,1)}, u32[]{:S(2)}, u32[]{:S(2)}) %collective-permute-start.17) | collective-permute-done | bytes 1310752 | tf_op jit(solution)/shard_map/ppermute | solution.py:17
  405.8 24.9 %collective-permute-done.15 = bf16[8,160,512]{2,1,0:T(8,128)(2,1)} collective-permute-done((bf16[8,160,512]{2,1,0:T(8,128)(2,1)S(1)}, bf16[8,160,512]{2,1,0:T(8,128)(2,1)}, u32[]{:S(2)}, u32[]{:S(2)}) %collective-permute-start.15) | collective-permute-done | bytes 1310752 | tf_op jit(solution)/shard_map/ppermute | solution.py:17
  432.2 26.6 %collective-permute-done.12 = bf16[8,160,512]{2,1,0:T(8,128)(2,1)} collective-permute-done((bf16[8,160,512]{2,1,0:T(8,128)(2,1)}, bf16[8,160,512]{2,1,0:T(8,128)(2,1)}, u32[]{:S(2)}, u32[]{:S(2)}) %collective-permute-start.12) | collective-permute-done | bytes 1310752 | tf_op jit(solution)/shard_map/ppermute | solution.py:17
  460.3 26.2 %collective-permute-done.10 = bf16[8,160,512]{2,1,0:T(8,128)(2,1)} collective-permute-done((bf16[8,160,512]{2,1,0:T(8,128)(2,1)}, bf16[8,160,512]{2,1,0:T(8,128)(2,1)}, u32[]{:S(2)}, u32[]{:S(2)}) %collective-permute-start.10) | collective-permute-done | bytes 1310752 | tf_op jit(solution)/shard_map/ppermute | solution.py:17
  488.6 24.7 %density.3.refs_9_ = f32[960,4096]{1,0:T(8,128)} custom-call(f32[960,1]{1,0:T(8,128)} %sub.130.refs_0_, f32[1,640]{1,0:T(1,128)} %reshape.53.refs_1_, bf16[8,320,512]{2,1,0:T(8,128)(2,1)} %copy-done.2, bf16[8,320,512]{2,1,0:T(8,128)(2,1)} %all-to-all-done.1.refs_3_, bf16[8,320,512]{2,1,0:T(8,128)(2,1)} %all-to-all-done.2.refs_4_, ...), custom_call_target="tpu_custom_call" | custom-call | flops 10066329600 | bytes 34078720 | tf_op jit(solution)/shard_map/density/pallas_call | solution.py:121
  514.3 28.3 %density.4.refs_9_ = f32[960,4096]{1,0:T(8,128)} custom-call(f32[960,1]{1,0:T(8,128)} %sub.130.refs_0_, f32[1,640]{1,0:T(1,128)} %reshape.52.refs_1_, bf16[8,320,512]{2,1,0:T(8,128)(2,1)} %copy-done.2, bf16[8,320,512]{2,1,0:T(8,128)(2,1)} %all-to-all-done.1.refs_3_, bf16[8,320,512]{2,1,0:T(8,128)(2,1)} %all-to-all-done.2.refs_4_, ...), custom_call_target="tpu_custom_call" | custom-call | flops 10066329600 | bytes 49807360 | tf_op jit(solution)/shard_map/density/pallas_call | solution.py:121
  542.6 26.8 %density.5 = bf16[960,4096]{1,0:T(8,128)(2,1)} custom-call(f32[960,1]{1,0:T(8,128)} %sub.130.refs_0_, f32[1,640]{1,0:T(1,128)} %reshape.49.refs_1_, bf16[8,320,512]{2,1,0:T(8,128)(2,1)} %copy-done.2, bf16[8,320,512]{2,1,0:T(8,128)(2,1)} %all-to-all-done.1.refs_3_, bf16[8,320,512]{2,1,0:T(8,128)(2,1)} %all-to-all-done.2.refs_4_, ...), custom_call_target="tpu_custom_call" | custom-call | flops 10066329600 | bytes 41943040 | tf_op jit(solution)/shard_map/density/pallas_call | solution.py:121
  (106 shorter events, 66.6 us)
Async XLA Ops:
  6.5 71.7 %all-gather.2.cloned.1.call-start = ((), (), s32[]{:S(2)}) async-start(), calls=%async_computation.3 | async-start | bytes 4055040 | tf_op jit(solution)/shard_map/all_gather | solution.py:152
  85.9 17.8 %collective-permute-start.1 = (bf16[2,320,512]{2,1,0:T(8,128)(2,1)}, bf16[2,320,512]{2,1,0:T(8,128)(2,1)S(1)}, u32[]{:S(2)}, u32[]{:S(2)}) collective-permute-start(bf16[2,320,512]{2,1,0:T(8,128)(2,1)} %get-tuple-element.19), channel_id=1, source_target_pairs={{0,2},{1,3},{2,0},{3,1},{4,6},{5,7},{6,4},{7,5},{8,10},{9,11},{10,... | collective-permute-start | bytes 1966088 | tf_op jit(solution)/shard_map/ppermute | solution.py:17
  87.4 29.5 %collective-permute-start.2 = (bf16[2,320,512]{2,1,0:T(8,128)(2,1)}, bf16[2,320,512]{2,1,0:T(8,128)(2,1)S(1)}, u32[]{:S(2)}, u32[]{:S(2)}) collective-permute-start(bf16[2,320,512]{2,1,0:T(8,128)(2,1)} %get-tuple-element.20), channel_id=1, source_target_pairs={{0,3},{1,2},{2,1},{3,0},{4,7},{5,6},{6,5},{7,4},{8,11},{9,10},{10,... | collective-permute-start | bytes 1966088 | tf_op jit(solution)/shard_map/ppermute | solution.py:17
  117.8 63.7 %all-to-all-start = ((bf16[8,320,512]{2,1,0:T(8,128)(2,1)}), bf16[8,320,512]{2,1,0:T(8,128)(2,1)S(1)}, u32[]{:S(2)}, u32[]{:S(2)}) async-start(bf16[8,320,512]{2,1,0:T(8,128)(2,1)} %constant_dynamic-update-slice_fusion.8), calls=%async_computation | async-start | bytes 5242880 | tf_op jit(solution)/shard_map/all_to_all | solution.py:171
  129.3 17.8 %collective-permute-start.4 = (bf16[2,320,512]{2,1,0:T(8,128)(2,1)}, bf16[2,320,512]{2,1,0:T(8,128)(2,1)S(1)}, u32[]{:S(2)}, u32[]{:S(2)}) collective-permute-start(bf16[2,320,512]{2,1,0:T(8,128)(2,1)} %get-tuple-element.23), channel_id=1, source_target_pairs={{0,2},{1,3},{2,0},{3,1},{4,6},{5,7},{6,4},{7,5},{8,10},{9,11},{10,... | collective-permute-start | bytes 1966088 | tf_op jit(solution)/shard_map/ppermute | solution.py:17
  130.7 29.0 %collective-permute-start.5 = (bf16[2,320,512]{2,1,0:T(8,128)(2,1)}, bf16[2,320,512]{2,1,0:T(8,128)(2,1)S(1)}, u32[]{:S(2)}, u32[]{:S(2)}) collective-permute-start(bf16[2,320,512]{2,1,0:T(8,128)(2,1)} %get-tuple-element.24), channel_id=1, source_target_pairs={{0,3},{1,2},{2,1},{3,0},{4,7},{5,6},{6,5},{7,4},{8,11},{9,10},{10,... | collective-permute-start | bytes 1966088 | tf_op jit(solution)/shard_map/ppermute | solution.py:17
  181.5 63.7 %all-to-all-start.1 = ((bf16[8,320,512]{2,1,0:T(8,128)(2,1)}), bf16[8,320,512]{2,1,0:T(8,128)(2,1)}, u32[]{:S(2)}, u32[]{:S(2)}) async-start(bf16[8,320,512]{2,1,0:T(8,128)(2,1)} %constant_dynamic-update-slice_fusion.4), calls=%async_computation.1 | async-start | bytes 5242880 | tf_op jit(solution)/shard_map/all_to_all | solution.py:171
  193.5 17.8 %collective-permute-start.7 = (bf16[2,320,512]{2,1,0:T(8,128)(2,1)}, bf16[2,320,512]{2,1,0:T(8,128)(2,1)S(1)}, u32[]{:S(2)}, u32[]{:S(2)}) collective-permute-start(bf16[2,320,512]{2,1,0:T(8,128)(2,1)} %get-tuple-element.27), channel_id=1, source_target_pairs={{0,2},{1,3},{2,0},{3,1},{4,6},{5,7},{6,4},{7,5},{8,10},{9,11},{10,... | collective-permute-start | bytes 1966088 | tf_op jit(solution)/shard_map/ppermute | solution.py:17
  195.0 29.5 %collective-permute-start.8 = (bf16[2,320,512]{2,1,0:T(8,128)(2,1)}, bf16[2,320,512]{2,1,0:T(8,128)(2,1)S(1)}, u32[]{:S(2)}, u32[]{:S(2)}) collective-permute-start(bf16[2,320,512]{2,1,0:T(8,128)(2,1)} %get-tuple-element.28), channel_id=1, source_target_pairs={{0,3},{1,2},{2,1},{3,0},{4,7},{5,6},{6,5},{7,4},{8,11},{9,10},{10,... | collective-permute-start | bytes 1966088 | tf_op jit(solution)/shard_map/ppermute | solution.py:17
  245.2 63.5 %all-to-all-start.2 = ((bf16[8,320,512]{2,1,0:T(8,128)(2,1)}), bf16[8,320,512]{2,1,0:T(8,128)(2,1)}, u32[]{:S(2)}, u32[]{:S(2)}) async-start(bf16[8,320,512]{2,1,0:T(8,128)(2,1)} %constant_dynamic-update-slice_fusion), calls=%async_computation.2 | async-start | bytes 5242880 | tf_op jit(solution)/shard_map/all_to_all | solution.py:171
  251.1 60.1 %collective-permute-start.19 = (bf16[8,160,512]{2,1,0:T(8,128)(2,1)}, bf16[8,160,512]{2,1,0:T(8,128)(2,1)}, u32[]{:S(2)}, u32[]{:S(2)}) collective-permute-start(bf16[8,160,512]{2,1,0:T(8,128)(2,1)} %constant_dynamic-slice_fusion), channel_id=1, source_target_pairs={{0,1},{1,0},{2,3},{3,2},{4,5},{5,4},{6,7},{7,6},{8,9},{9,8},{10,11... | collective-permute-start | bytes 3932168 | tf_op jit(solution)/shard_map/ppermute | solution.py:17
  253.5 65.6 %collective-permute-start.14 = (bf16[8,160,512]{2,1,0:T(8,128)(2,1)}, bf16[8,160,512]{2,1,0:T(8,128)(2,1)}, u32[]{:S(2)}, u32[]{:S(2)}) collective-permute-start(bf16[8,160,512]{2,1,0:T(8,128)(2,1)} %constant_dynamic-slice_fusion.1), channel_id=1, source_target_pairs={{0,1},{1,0},{2,3},{3,2},{4,5},{5,4},{6,7},{7,6},{8,9},{9,8},{10,11... | collective-permute-start | bytes 3932168 | tf_op jit(solution)/shard_map/ppermute | solution.py:17
  314.6 31.9 %collective-permute-start.22 = (bf16[8,160,512]{2,1,0:T(8,128)(2,1)}, bf16[8,160,512]{2,1,0:T(8,128)(2,1)}, u32[]{:S(2)}, u32[]{:S(2)}) collective-permute-start(bf16[8,160,512]{2,1,0:T(8,128)(2,1)} %get-tuple-element.29), channel_id=1, source_target_pairs={{0,2},{1,3},{2,0},{3,1},{4,6},{5,7},{6,4},{7,5},{8,10},{9,11},{10,... | collective-permute-start | bytes 3932168 | tf_op jit(solution)/shard_map/ppermute | solution.py:17
  318.6 56.0 %collective-permute-start.20 = (bf16[8,160,512]{2,1,0:T(8,128)(2,1)}, bf16[8,160,512]{2,1,0:T(8,128)(2,1)}, u32[]{:S(2)}, u32[]{:S(2)}) collective-permute-start(bf16[8,160,512]{2,1,0:T(8,128)(2,1)} %get-tuple-element.30), channel_id=1, source_target_pairs={{0,2},{1,3},{2,0},{3,1},{4,6},{5,7},{6,4},{7,5},{8,10},{9,11},{10,... | collective-permute-start | bytes 3932168 | tf_op jit(solution)/shard_map/ppermute | solution.py:17
  321.5 81.2 %collective-permute-start.17 = (bf16[8,160,512]{2,1,0:T(8,128)(2,1)S(1)}, bf16[8,160,512]{2,1,0:T(8,128)(2,1)}, u32[]{:S(2)}, u32[]{:S(2)}) collective-permute-start(bf16[8,160,512]{2,1,0:T(8,128)(2,1)S(1)} %get-tuple-element.31), channel_id=1, source_target_pairs={{0,2},{1,3},{2,0},{3,1},{4,6},{5,7},{6,4},{7,5},{8,10},{9,11},{10,... | collective-permute-start | bytes 3932168 | tf_op jit(solution)/shard_map/ppermute | solution.py:17
  325.5 105.3 %collective-permute-start.15 = (bf16[8,160,512]{2,1,0:T(8,128)(2,1)S(1)}, bf16[8,160,512]{2,1,0:T(8,128)(2,1)}, u32[]{:S(2)}, u32[]{:S(2)}) collective-permute-start(bf16[8,160,512]{2,1,0:T(8,128)(2,1)S(1)} %get-tuple-element.32), channel_id=1, source_target_pairs={{0,2},{1,3},{2,0},{3,1},{4,6},{5,7},{6,4},{7,5},{8,10},{9,11},{10,... | collective-permute-start | bytes 3932168 | tf_op jit(solution)/shard_map/ppermute | solution.py:17
  329.8 129.1 %collective-permute-start.12 = (bf16[8,160,512]{2,1,0:T(8,128)(2,1)}, bf16[8,160,512]{2,1,0:T(8,128)(2,1)}, u32[]{:S(2)}, u32[]{:S(2)}) collective-permute-start(bf16[8,160,512]{2,1,0:T(8,128)(2,1)} %get-tuple-element.33), channel_id=1, source_target_pairs={{0,2},{1,3},{2,0},{3,1},{4,6},{5,7},{6,4},{7,5},{8,10},{9,11},{10,... | collective-permute-start | bytes 3932168 | tf_op jit(solution)/shard_map/ppermute | solution.py:17
  346.5 140.0 %collective-permute-start.10 = (bf16[8,160,512]{2,1,0:T(8,128)(2,1)}, bf16[8,160,512]{2,1,0:T(8,128)(2,1)}, u32[]{:S(2)}, u32[]{:S(2)}) collective-permute-start(bf16[8,160,512]{2,1,0:T(8,128)(2,1)} %get-tuple-element.34), channel_id=1, source_target_pairs={{0,2},{1,3},{2,0},{3,1},{4,6},{5,7},{6,4},{7,5},{8,10},{9,11},{10,... | collective-permute-start | bytes 3932168 | tf_op jit(solution)/shard_map/ppermute | solution.py:17
  374.6 113.4 %collective-permute-start.23 = (bf16[8,160,512]{2,1,0:T(8,128)(2,1)}, bf16[8,160,512]{2,1,0:T(8,128)(2,1)}, u32[]{:S(2)}, u32[]{:S(2)}) collective-permute-start(bf16[8,160,512]{2,1,0:T(8,128)(2,1)} %broadcast_select_fusion.3.refs_7_), channel_id=1, source_target_pairs={{0,1},{1,0},{2,3},{3,2},{4,5},{5,4},{6,7},{7,6},{8,9},{9,8},{10,11... | collective-permute-start | bytes 3932168 | tf_op jit(solution)/shard_map/ppermute | solution.py:17
  402.6 85.9 %collective-permute-start.21 = (bf16[8,160,512]{2,1,0:T(8,128)(2,1)}, bf16[8,160,512]{2,1,0:T(8,128)(2,1)}, u32[]{:S(2)}, u32[]{:S(2)}) collective-permute-start(bf16[8,160,512]{2,1,0:T(8,128)(2,1)} %broadcast_select_fusion.9.refs_5_), channel_id=1, source_target_pairs={{0,1},{1,0},{2,3},{3,2},{4,5},{5,4},{6,7},{7,6},{8,9},{9,8},{10,11... | collective-permute-start | bytes 3932168 | tf_op jit(solution)/shard_map/ppermute | solution.py:17
  430.7 82.5 %collective-permute-start.18 = (bf16[8,160,512]{2,1,0:T(8,128)(2,1)S(1)}, bf16[8,160,512]{2,1,0:T(8,128)(2,1)S(1)}, u32[]{:S(2)}, u32[]{:S(2)}) collective-permute-start(bf16[8,160,512]{2,1,0:T(8,128)(2,1)S(1)} %broadcast_select_fusion.4.refs_7_), channel_id=1, source_target_pairs={{0,1},{1,0},{2,3},{3,2},{4,5},{5,4},{6,7},{7,6},{8,9},{9,8},{10,11... | collective-permute-start | bytes 3932168 | tf_op jit(solution)/shard_map/ppermute | solution.py:17
  458.8 54.5 %collective-permute-start.16 = (bf16[8,160,512]{2,1,0:T(8,128)(2,1)S(1)}, bf16[8,160,512]{2,1,0:T(8,128)(2,1)}, u32[]{:S(2)}, u32[]{:S(2)}) collective-permute-start(bf16[8,160,512]{2,1,0:T(8,128)(2,1)S(1)} %broadcast_select_fusion.10.refs_5_), channel_id=1, source_target_pairs={{0,1},{1,0},{2,3},{3,2},{4,5},{5,4},{6,7},{7,6},{8,9},{9,8},{10,11... | collective-permute-start | bytes 3932168 | tf_op jit(solution)/shard_map/ppermute | solution.py:17
  486.5 56.1 %collective-permute-start.13 = (bf16[8,160,512]{2,1,0:T(8,128)(2,1)S(1)}, bf16[8,160,512]{2,1,0:T(8,128)(2,1)}, u32[]{:S(2)}, u32[]{:S(2)}) collective-permute-start(bf16[8,160,512]{2,1,0:T(8,128)(2,1)S(1)} %broadcast_select_fusion.5.refs_7_), channel_id=1, source_target_pairs={{0,1},{1,0},{2,3},{3,2},{4,5},{5,4},{6,7},{7,6},{8,9},{9,8},{10,11... | collective-permute-start | bytes 3932168 | tf_op jit(solution)/shard_map/ppermute | solution.py:17
  488.0 54.6 %collective-permute-start.11 = (bf16[8,160,512]{2,1,0:T(8,128)(2,1)S(1)}, bf16[8,160,512]{2,1,0:T(8,128)(2,1)}, u32[]{:S(2)}, u32[]{:S(2)}) collective-permute-start(bf16[8,160,512]{2,1,0:T(8,128)(2,1)S(1)} %broadcast_select_fusion.11.refs_5_), channel_id=1, source_target_pairs={{0,1},{1,0},{2,3},{3,2},{4,5},{5,4},{6,7},{7,6},{8,9},{9,8},{10,11... | collective-permute-start | bytes 3932168 | tf_op jit(solution)/shard_map/ppermute | solution.py:17
  (17 other events, 560.4 us)
Sparse Core Ops, SparseCore 0:
  9.5 68.6 all-gather.1

commit v2 on v1

v2 whole, which is shorter than its diff:
```python
import functools

import jax
import jax.numpy as jnp
from jax import lax
from jax.experimental import pallas as pl
from jax.experimental.pallas import tpu as pltpu
from jax.sharding import PartitionSpec as P

spin_scale = 1.3
VMEM_LIMIT = 56 * 1024 * 1024
ANY = pl.BlockSpec(memory_space=pl.ANY)


def swap(value, distance, axis="pair"):
    count = lax.axis_size(axis)
    pairs = [(source, source ^ distance) for source in range(count)]
    return lax.ppermute(value, axis, pairs)


def along(value, step):
    count = lax.axis_size("aux")
    pairs = [(a, a + 2 * step) for a in range(count) if 0 <= a + 2 * step < count]
    return lax.ppermute(value, "aux", pairs)


def place_kernel(line, index_ref, *refs):
    count = 2 * line - 1
    own_refs, mate_refs, out_ref = refs[:count], refs[count:-1], refs[-1]
    here, side, core = index_ref[0], index_ref[1], index_ref[2]
    for half, piece_refs in ((core, own_refs), (1 - core, mate_refs)):
        for number, ref in enumerate(piece_refs):
            shift = (number + 1) // 2
            row = here - shift if number % 2 else here + shift

            @pl.when((row >= 0) & (row < line))
            def _():
                for slot in range(2):
                    out_ref[row, side ^ slot, half] = ref[slot]


def gather_coefficients(vir_coeffs):
    rows = jnp.transpose(vir_coeffs)
    part = rows.shape[0] // 2
    line = lax.axis_size("aux") // 2
    aux_index = lax.axis_index("aux")
    core = lax.axis_index("pair") % 2
    piece = lax.dynamic_slice_in_dim(rows, core * part, part, 0)
    both = jnp.stack([piece, swap(piece, 1, "aux")])
    own, mate = [both], [swap(both, 1)]
    below = above = both
    for _ in range(line - 1):
        below, above = along(below, 1), along(above, -1)
        own += [below, above]
        mate += [swap(below, 1), swap(above, 1)]
    depth = rows.shape[1]
    index = jnp.stack([aux_index // 2, aux_index % 2, core]).astype(jnp.int32)
    placed = pl.pallas_call(
        functools.partial(place_kernel, line),
        in_specs=[pl.BlockSpec(memory_space=pltpu.SMEM)]
        + [pl.BlockSpec(memory_space=pltpu.VMEM)] * (len(own) + len(mate)),
        out_specs=pl.BlockSpec(memory_space=pltpu.VMEM),
        out_shape=jax.ShapeDtypeStruct((line, 2, 2, part, depth), rows.dtype),
        compiler_params=pltpu.CompilerParams(vmem_limit_bytes=VMEM_LIMIT),
        cost_estimate=pl.CostEstimate(
            flops=0, bytes_accessed=4 * line * 4 * part * depth, transcendentals=0
        ),
        name="place",
    )(index, *own, *mate)
    return placed.reshape(line * 4 * part, depth)


def transform_kernel(width, index_ref, coeff_ref, half_ref, *out_refs):
    half = half_ref[0, 0]
    for distance, out_ref in enumerate(out_refs):
        start = pl.multiple_of((index_ref[0] ^ distance) * width, width)
        product = jnp.dot(
            coeff_ref[pl.ds(start, width), :], half, preferred_element_type=jnp.float32
        )
        out_ref[0] = product.astype(out_ref.dtype)


def transform(coeff_rows, half, orbital, pair_index, reach):
    blocks, _, depth, aux_slice = half.shape
    width = coeff_rows.shape[0] // lax.axis_size("pair")
    grid_spec = pltpu.PrefetchScalarGridSpec(
        num_scalar_prefetch=1,
        grid=(blocks,),
        in_specs=[
            pl.BlockSpec(coeff_rows.shape, lambda b, index: (0, 0)),
            pl.BlockSpec((1, 1, depth, aux_slice), lambda b, index: (b, orbital, 0, 0)),
        ],
        out_specs=[pl.BlockSpec((1, width, aux_slice), lambda b, index: (b, 0, 0))] * reach,
    )
    return pl.pallas_call(
        functools.partial(transform_kernel, width),
        grid_spec=grid_spec,
        out_shape=[jax.ShapeDtypeStruct((blocks, width, aux_slice), jnp.bfloat16)] * reach,
        compiler_params=pltpu.CompilerParams(vmem_limit_bytes=VMEM_LIMIT),
        cost_estimate=pl.CostEstimate(
            flops=2 * blocks * reach * width * depth * aux_slice,
            bytes_accessed=2 * (coeff_rows.size + blocks * (depth + reach * width) * aux_slice),
            transcendentals=0,
        ),
        name="transform",
    )(pair_index.reshape(1), coeff_rows, half)


def assemble_kernel(count, index_ref, *refs):
    piece_refs, out_ref = refs[:count], refs[-1]
    for number, ref in enumerate(piece_refs):
        @pl.when(pl.program_id(0) == number)
        def _():
            out_ref[...] = ref[...]


def assemble(pieces, pair_index, after):
    count = len(pieces)
    blocks, width, piece = pieces[0].shape
    whole = pl.BlockSpec((blocks, width, piece), lambda n, index: (0, 0, 0))
    return pl.pallas_call(
        functools.partial(assemble_kernel, count),
        grid_spec=pltpu.PrefetchScalarGridSpec(
            num_scalar_prefetch=1,
            grid=(count,),
            in_specs=[whole] * count + [ANY] * len(after),
            out_specs=pl.BlockSpec((blocks, width, piece), lambda n, index: (index[0] ^ n, 0, 0)),
        ),
        out_shape=jax.ShapeDtypeStruct((count * blocks, width, piece), pieces[0].dtype),
        cost_estimate=pl.CostEstimate(
            flops=0, bytes_accessed=4 * count * pieces[0].size, transcendentals=0
        ),
        name="assemble",
    )(pair_index.reshape(1), *pieces, *after)


def gate_kernel(value_ref, after_ref, out_ref):
    out_ref[...] = value_ref[...]


def gate(value, after):
    parts = 2 if value.shape[0] % 2 == 0 else 1
    spec = pl.BlockSpec((value.shape[0] // parts, *value.shape[1:]), lambda t: (t, 0, 0))
    return pl.pallas_call(
        gate_kernel,
        grid=(parts,),
        in_specs=[spec, ANY],
        out_specs=spec,
        out_shape=jax.ShapeDtypeStruct(value.shape, value.dtype),
        cost_estimate=pl.CostEstimate(flops=0, bytes_accessed=4 * value.size, transcendentals=0),
        name="gate",
    )(value, after)


GROUP = 2


def density_kernel(plan, distance_ref, *refs):
    occ_width, steps, slices, low, high, ends, segments, pair_count, starts, has_total = plan
    refs = list(refs)
    left_energy, right_energy = refs[:2]
    del refs[:2]
    local_refs = refs[:occ_width]
    del refs[:occ_width]
    held_refs = []
    for orbital in segments:
        held_refs.append([])
        for first, last in orbital:
            held_refs[-1].append((first, last, refs[:pair_count]))
            del refs[:pair_count]
    start_ref = refs.pop(0) if starts else None
    total_ref = refs.pop(0) if has_total else None
    out_ref = refs.pop(0)
    if ends:
        integrals, amplitudes, remote_ref, sems = refs
    else:
        remote_ref, sems = refs
        integrals = out_ref
    width = held_refs[0][0][2][0].shape[1]
    step = pl.program_id(0)
    turns = (high - low) // GROUP

    def copy_of(ref, first, number, t):
        return pltpu.make_async_copy(
            ref.at[t - first],
            remote_ref.at[t, pl.ds(number * width, width)],
            sems.at[number, t],
        )

    @pl.when(step == 0)
    def _():
        for orbital, parts in enumerate(held_refs):
            for first, last, blocks in parts:
                begin, end = (first, last) if ends else (max(first, low), min(last, high))

                @pl.loop(begin, end)
                def _(t):
                    for position in range(steps):
                        for distance, ref in enumerate(blocks):
                            @pl.when(distance_ref[position] == distance)
                            def _():
                                copy_of(ref, first, orbital * steps + position, t).start()

    def wait_for(t):
        for number in range(len(held_refs) * steps):
            copy_of(held_refs[0][0][2][0], t, number, t).wait()

    @pl.when(step < turns)
    def _():
        now = low + step * GROUP
        for ahead in range(GROUP):
            wait_for(now + ahead)
        local = jnp.concatenate(
            [
                jnp.concatenate([ref[ahead] for ahead in range(GROUP)], axis=1)
                for ref in local_refs
            ],
            axis=0,
        )
        remote = jnp.concatenate([remote_ref[now + ahead] for ahead in range(GROUP)], axis=1)
        product = lax.dot_general(
            local, remote, (((1,), (1,)), ((), ())), preferred_element_type=jnp.float32
        )

        @pl.when(step == 0)
        def _():
            integrals[...] = product + start_ref[...] if starts else product

        @pl.when(step > 0)
        def _():
            integrals[...] += product

        if ends:
            @pl.when(step == turns - 1)
            def _():
                gap = left_energy[...] + right_energy[...]
                amplitudes[...] = (spin_scale * integrals[...] / gap).astype(jnp.bfloat16)

    if ends:
        @pl.when(step >= turns)
        def _():
            now = step - turns

            @pl.when((now < low) | (now >= high))
            def _():
                wait_for(now)

            product = jnp.dot(amplitudes[...], remote_ref[now], preferred_element_type=jnp.float32)
            if has_total:
                product = product + total_ref[...]
            out_ref[...] = product.astype(out_ref.dtype)


def add_density(
    locals_, held, distances, left_energy, right_energy, span, ends, start=None, total=None,
    out_dtype=jnp.float32,
):
    occ_width, pair_count = len(locals_), len(held[0][0][2])
    steps = distances.shape[0]
    slices, width, aux_slice = locals_[0].shape
    rows, columns = occ_width * width, len(held) * steps * width
    low, high = span
    turns = (high - low) // GROUP
    base = low // GROUP
    in_specs = [
        pl.BlockSpec((rows, 1), lambda t, d: (0, 0)),
        pl.BlockSpec((1, columns), lambda t, d: (0, 0)),
    ]
    in_specs += [
        pl.BlockSpec(
            (GROUP, width, aux_slice), lambda t, d: (base + jnp.minimum(t, turns - 1), 0, 0)
        )
    ] * occ_width
    operands = [left_energy, right_energy, *locals_]
    for parts in held:
        for _, _, blocks in parts:
            operands += blocks
    in_specs += [ANY] * (len(operands) - len(in_specs))
    whole = pl.BlockSpec((rows, columns), lambda t, d: (0, 0))
    if start is not None:
        in_specs.append(whole)
        operands.append(start)
    moved = 2 * (high - low) * aux_slice * rows + 2 * slices * aux_slice * columns
    scratch = [
        pltpu.VMEM((slices, columns, aux_slice), jnp.bfloat16),
        pltpu.SemaphoreType.DMA((len(held) * steps, slices)),
    ]
    if ends:
        out_spec = pl.BlockSpec((rows, aux_slice), lambda t, d: (0, jnp.maximum(t - turns, 0)))
        out_shape = jax.ShapeDtypeStruct((rows, slices * aux_slice), out_dtype)
        scratch = [
            pltpu.VMEM((rows, columns), jnp.float32),
            pltpu.VMEM((rows, columns), jnp.bfloat16),
        ] + scratch
        if total is not None:
            in_specs.append(out_spec)
            operands.append(total)
            moved += total.size * 4
    else:
        out_spec = whole
        out_shape = jax.ShapeDtypeStruct((rows, columns), jnp.float32)
    moved += out_shape.size * out_shape.dtype.itemsize
    plan = (
        occ_width, steps, slices, low, high, ends,
        [[(first, last) for first, last, _ in parts] for parts in held],
        pair_count, start is not None, total is not None,
    )
    return pl.pallas_call(
        functools.partial(density_kernel, plan),
        grid_spec=pltpu.PrefetchScalarGridSpec(
            num_scalar_prefetch=1,
            grid=(turns + (slices if ends else 0),),
            in_specs=in_specs,
            out_specs=out_spec,
            scratch_shapes=scratch,
        ),
        out_shape=out_shape,
        compiler_params=pltpu.CompilerParams(vmem_limit_bytes=VMEM_LIMIT),
        cost_estimate=pl.CostEstimate(
            flops=2 * rows * columns * aux_slice * (high - low + (slices if ends else 0)),
            bytes_accessed=moved,
            transcendentals=0,
        ),
        name="density" if ends else "integrals",
    )(distances, *operands)


def per_device(half_ints, vir_coeffs, occ_energy, vir_energy, roster):
    pair_count = lax.axis_size("pair")
    aux_count = lax.axis_size("aux")
    pair_index = lax.axis_index("pair")
    aux_index = lax.axis_index("aux")
    occ_rows, depth, aux_slice = half_ints.shape
    row_blocks = aux_count // pair_count
    occ_width = occ_rows // row_blocks
    step_count = roster.shape[1]

    coeff_rows = gather_coefficients(vir_coeffs)
    vir_width = coeff_rows.shape[0] // pair_count
    half = half_ints.reshape(row_blocks, occ_width, depth, aux_slice)

    sources = lax.dynamic_index_in_dim(roster, aux_index, 0, keepdims=False)
    occ_block = lax.dynamic_slice_in_dim(occ_energy, aux_index * occ_width, occ_width, 0)
    vir_block = lax.dynamic_slice_in_dim(vir_energy, pair_index * vir_width, vir_width, 0)
    left_energy = (vir_block[None, :] - occ_block[:, None]).reshape(-1, 1)
    source_energy = [
        lax.dynamic_slice_in_dim(vir_energy, sources[position] * vir_width, vir_width, 0)
        for position in range(step_count)
    ]

    def spread(block):
        blocks = [block]
        distance = 2
        while distance < pair_count:
            blocks += [swap(b, distance) for b in blocks]
            distance *= 2
        return blocks

    def share(blocks, after=None):
        if after is not None and len(blocks) > 1:
            blocks = blocks[:-1] + [gate(blocks[-1], after)]
        return [b for block in blocks for b in (block, swap(block, 1))]

    first = []
    for raw in spread(half[:, :1]):
        own, other = transform(coeff_rows, raw, 0, pair_index, 2)
        first += [own, swap(other, 1)]
    parts = [
        transform(coeff_rows, half, orbital, pair_index, pair_count)
        for orbital in range(1, occ_width)
    ]
    moved = [first] + [
        [pieces[0]] + [swap(pieces[d], d) for d in range(1, pair_count)] for pieces in parts
    ]

    locals_, far = [], []
    middle = aux_count * 3 // 4
    for orbital in range(occ_width):
        after = [pieces[-1] for pieces in parts[1:]] if orbital == 1 else []
        if orbital > 1:
            after.append(far[orbital - 2][-1])
        if 0 < orbital < occ_width - 1:
            after += moved[orbital + 1][1:]
        sent = assemble(moved[orbital], pair_index, after)
        local = lax.all_to_all(sent, "aux", split_axis=0, concat_axis=0, tiled=True)
        locals_.append(local)
        if orbital < occ_width - 1:
            far.append(spread(local))
    halves = [spread(locals_[-1][:middle]), spread(locals_[-1][middle:])]

    distances = (sources ^ pair_index).astype(jnp.int32)

    def right_of(orbitals):
        return jnp.concatenate(
            [energy - occ_block[orbital] for orbital in orbitals for energy in source_energy]
        ).reshape(1, -1)

    total = None
    everything = (0, aux_count)
    if occ_width > 1:
        first = range(occ_width - 1)
        held = [[(0, aux_count, share(far[orbital]))] for orbital in first]
        total = add_density(
            locals_, held, distances, left_energy, right_of(first), everything, True
        )
    right_energy = right_of([occ_width - 1])
    lower = (0, middle, share(halves[0], total))
    start = add_density(
        locals_, [[lower]], distances, left_energy, right_energy, (0, middle), False
    )
    upper = (middle, aux_count, share(halves[1], start))
    total = add_density(
        locals_, [[lower, upper]], distances, left_energy, right_energy, (middle, aux_count), True,
        start=start, total=total, out_dtype=jnp.bfloat16,
    )
    return jnp.transpose(total.reshape(occ_width, vir_width, -1), (1, 0, 2))


def solution(mesh):
    in_specs = (P("pair", None, "aux"), P(None, "aux"), P(), P(), P())
    out_specs = P("pair", "aux", None)
    return jax.shard_map(
        per_device, mesh=mesh, in_specs=in_specs, out_specs=out_specs, check_vma=False
    )
```

time: 578 us -> 385 us (0.67)
  waiting for transfers between devices: 378 us -> 206 us
  starting transfers between devices: 26.3 us -> 48.9 us
  between operations: 21.1 us -> 1.81 us
  other arithmetic: 21.2 us -> 3.55 us
  local copies, waits for them, and re-layouts: 27.3 us -> 12.5 us
  Pallas kernels: 103 us -> 112 us
    ppermute x24 -> x35, waiting for transfers between devices: 217 us -> 143 us  [the longest x29 122 us: swap(): return lax.ppermute(value, axis, pairs)]
    all_gather x1 -> x0, waiting for transfers between devices: 71 us -> none  [per_device(): lax.all_gather(jnp.transpose(vir_coeffs), 'aux', axis=0, tiled=True)]
    all_to_all x3, waiting for transfers between devices: 89.4 us -> 62.6 us  [per_device(): local = lax.all_to_all(sent, 'aux', split_axis=0, concat_axis=0, tiled=True)]
    ppermute x24 -> x35, starting transfers between devices: 13.7 us -> 32.8 us  [the longest x6 17.8 us: along(): return lax.ppermute(value, 'aux', pairs)]
    select_n x9 -> x0, other arithmetic: 19 us -> none  [the longest x6 9.59 us: per_device(): held = jnp.where(near, held, arrived)]
    dynamic_update_slice x12 -> x0, local copies, waits for them, and re-layouts: 10.6 us -> none  [per_device(): gathered = lax.dynamic_update_slice_in_dim(gathered, piece, start, 0)]
    dynamic_slice x5 -> x0, local copies, waits for them, and re-layouts: 6.29 us -> none  [the longest x3 6.14 us: per_device(): other = lax.dynamic_slice_in_dim(local, (1 - core) * part, part, 1)]
    pallas_call x3 -> x9, Pallas kernels: 79.8 us -> 85.6 us  [the longest x3 65 us: add_density(): pl.pallas_call(functools.partial(density_kernel, plan), grid_spec=pltpu.P...]
  transfers between devices with their start and end apart: 28 -> 38, of which waited for: 16 -> 19; matrix products, arithmetic and copies ran while one was open for 8% -> 3% of each run, Pallas kernels for 12% -> 23%
where the time goes in v2:
time: 385 us; the launch traced here: 384 us
  waiting for transfers between devices  206 us (54%)
  Pallas kernels  112 us (29%)
  starting transfers between devices  48.9 us (13%)
  local copies, waits for them, and re-layouts  12.5 us (3%)
    ppermute x29, waiting for transfers between devices, swap(): return lax.ppermute(value, axis, pairs)  122 us
    pallas_call x3, Pallas kernels, add_density(): pl.pallas_call(functools.partial(density_kernel, plan), grid_spec=pltpu.P...  65 us
    all_to_all x3, waiting for transfers between devices, per_device(): local = lax.all_to_all(sent, 'aux', split_axis=0, concat_axis=0, tiled=True)  62.6 us
    pallas_call x4, Pallas kernels, transform(): pl.pallas_call(functools.partial(transform_kernel, width), grid_spec=grid...  26.4 us
    ppermute x6, waiting for transfers between devices, along(): return lax.ppermute(value, 'aux', pairs)  21.1 us
    ppermute x6, starting transfers between devices, along(): return lax.ppermute(value, 'aux', pairs)  17.8 us
    all_to_all x3, starting transfers between devices, per_device(): local = lax.all_to_all(sent, 'aux', split_axis=0, concat_axis=0, tiled=True)  16 us
    ppermute x29, starting transfers between devices, swap(): return lax.ppermute(value, axis, pairs)  15 us
  transfers between devices with their start and end apart: 38, of which 19 were waited for; matrix products, arithmetic and copies ran while one was open for 3% of the time, Pallas kernels for 23%

profile of v2, /device:TPU:0, one launch (start us, length us, event | category | flops | bytes accessed | tf_op | source)
XLA Modules:
  0.0 384.4 jit_solution(18153900954566756514)
XLA Ops:
  6.7 5.5 %collective-permute-done = bf16[80,1408]{1,0:T(8,128)(2,1)S(1)} collective-permute-done((bf16[80,1408]{1,0:T(8,128)(2,1)S(1)}, bf16[80,1408]{1,0:T(8,128)(2,1)S(1)}, u32[]{:S(2)}, u32[]{:S(2)}) %collective-permute-start) | collective-permute-done | bytes 225312 | tf_op jit(solution)/shard_map/ppermute | solution.py:18
  17.1 7.1 %collective-permute-done.1.refs_1_ = bf16[2,80,1408]{2,1,0:T(8,128)(2,1)S(1)} collective-permute-done((bf16[2,80,1408]{2,1,0:T(8,128)(2,1)S(1)}, bf16[2,80,1408]{2,1,0:T(8,128)(2,1)S(1)}, u32[]{:S(2)}, u32[]{:S(2)}) %collective-permute-start.1) | collective-permute-done | bytes 450592 | tf_op jit(solution)/shard_map/ppermute | solution.py:24
  24.2 5.2 %collective-permute-start.3 = (bf16[2,80,1408]{2,1,0:T(8,128)(2,1)S(1)}, bf16[2,80,1408]{2,1,0:T(8,128)(2,1)}, u32[]{:S(2)}, u32[]{:S(2)}) collective-permute-start(bf16[2,80,1408]{2,1,0:T(8,128)(2,1)S(1)} %collective-permute-done.1.refs_1_), channel_id=1, source_target_pairs={{0,8},{4,12},{8,16},{12,20},{16,24},{20,28},{1,9},{5,13},{9,17},{1... | collective-permute-start | bytes 1351688 | tf_op jit(solution)/shard_map/ppermute | solution.py:24
  31.3 4.9 %collective-permute-done.3.refs_3_ = bf16[2,80,1408]{2,1,0:T(8,128)(2,1)} collective-permute-done((bf16[2,80,1408]{2,1,0:T(8,128)(2,1)S(1)}, bf16[2,80,1408]{2,1,0:T(8,128)(2,1)}, u32[]{:S(2)}, u32[]{:S(2)}) %collective-permute-start.3) | collective-permute-done | bytes 450592 | tf_op jit(solution)/shard_map/ppermute | solution.py:24
  36.3 5.3 %collective-permute-start.5 = (bf16[2,80,1408]{2,1,0:T(8,128)(2,1)}, bf16[2,80,1408]{2,1,0:T(8,128)(2,1)}, u32[]{:S(2)}, u32[]{:S(2)}) collective-permute-start(bf16[2,80,1408]{2,1,0:T(8,128)(2,1)} %collective-permute-done.3.refs_3_), channel_id=1, source_target_pairs={{0,8},{4,12},{8,16},{12,20},{16,24},{20,28},{1,9},{5,13},{9,17},{1... | collective-permute-start | bytes 1351688 | tf_op jit(solution)/shard_map/ppermute | solution.py:24
  47.8 4.9 %collective-permute-done.6.refs_6_ = bf16[2,80,1408]{2,1,0:T(8,128)(2,1)} collective-permute-done((bf16[2,80,1408]{2,1,0:T(8,128)(2,1)}, bf16[2,80,1408]{2,1,0:T(8,128)(2,1)}, u32[]{:S(2)}, u32[]{:S(2)}) %collective-permute-start.6) | collective-permute-done | bytes 450592 | tf_op jit(solution)/shard_map/ppermute | solution.py:24
  54.9 4.9 %place.1 = bf16[4,2,2,80,1408]{4,3,2,1,0:T(8,128)(2,1)} custom-call(s32[3]{0:T(128)} %pad_add_fusion.index_ref, bf16[2,80,1408]{2,1,0:T(8,128)(2,1)} %copy-done.6, bf16[2,80,1408]{2,1,0:T(8,128)(2,1)} %copy-done.11, bf16[2,80,1408]{2,1,0:T(8,128)(2,1)} %copy-done.12, bf16[2,80,1408]{2,1,0:T(8,128)(2,1)} %collective-permute-done.3.refs_3_, ...), custom_call_target="tpu_custom_call" | custom-call | bytes 7208960 | tf_op jit(solution)/shard_map/place/pallas_call | solution.py:58
  59.8 5.6 %transform.4 = (bf16[2,320,512]{2,1,0:T(8,128)(2,1)}, bf16[2,320,512]{2,1,0:T(8,128)(2,1)}) custom-call(s32[1]{0:T(128)} %bitcast.3.index_ref, bf16[1280,1408]{1,0:T(8,128)(2,1)} %bitcast.20, bf16[2,1,1408,512]{3,2,1,0:T(8,128)(2,1)} %copy-done.3), custom_call_target="tpu_custom_call" | custom-call | flops 1845493760 | bytes 7798784 | tf_op jit(solution)/shard_map/transform/pallas_call | solution.py:95
  67.7 5.6 %transform.5 = (bf16[2,320,512]{2,1,0:T(8,128)(2,1)}, bf16[2,320,512]{2,1,0:T(8,128)(2,1)}) custom-call(s32[1]{0:T(128)} %bitcast.3.index_ref, bf16[1280,1408]{1,0:T(8,128)(2,1)} %bitcast.21, bf16[2,1,1408,512]{3,2,1,0:T(8,128)(2,1)} %collective-permute-done.15.half_ref), custom_call_target="tpu_custom_call" | custom-call | flops 1845493760 | bytes 7798784 | tf_op jit(solution)/shard_map/transform/pallas_call | solution.py:95
  80.1 6.1 %all-to-all-start = ((bf16[8,320,512]{2,1,0:T(8,128)(2,1)}), bf16[8,320,512]{2,1,0:T(8,128)(2,1)S(1)}, u32[]{:S(2)}, u32[]{:S(2)}) async-start(bf16[8,320,512]{2,1,0:T(8,128)(2,1)} %assemble.3), calls=%async_computation | async-start | bytes 5242880 | tf_op jit(solution)/shard_map/all_to_all | solution.py:385
  86.2 7.6 %transform.7 = (bf16[2,320,512]{2,1,0:T(8,128)(2,1)}, bf16[2,320,512]{2,1,0:T(8,128)(2,1)}, bf16[2,320,512]{2,1,0:T(8,128)(2,1)}, bf16[2,320,512]{2,1,0:T(8,128)(2,1)}) custom-call(s32[1]{0:T(128)} %bitcast.3.index_ref, bf16[1280,1408]{1,0:T(8,128)(2,1)} %bitcast.22, bf16[2,3,1408,512]{3,2,1,0:T(8,128)(2,1)} %bitcast.25), custom_call_target="tpu_custom_call" | custom-call | flops 3690987520 | bytes 9109504 | tf_op jit(solution)/shard_map/transform/pallas_call | solution.py:95
  95.7 7.6 %transform.6 = (bf16[2,320,512]{2,1,0:T(8,128)(2,1)}, bf16[2,320,512]{2,1,0:T(8,128)(2,1)}, bf16[2,320,512]{2,1,0:T(8,128)(2,1)}, bf16[2,320,512]{2,1,0:T(8,128)(2,1)}) custom-call(s32[1]{0:T(128)} %bitcast.3.index_ref, bf16[1280,1408]{1,0:T(8,128)(2,1)} %bitcast.23, bf16[2,3,1408,512]{3,2,1,0:T(8,128)(2,1)} %bitcast.26), custom_call_target="tpu_custom_call" | custom-call | flops 3690987520 | bytes 9109504 | tf_op jit(solution)/shard_map/transform/pallas_call | solution.py:95
  105.2 6.5 %collective-permute-done.21.refs_6_.refs_2_ = bf16[2,320,512]{2,1,0:T(8,128)(2,1)} collective-permute-done((bf16[2,320,512]{2,1,0:T(8,128)(2,1)}, bf16[2,320,512]{2,1,0:T(8,128)(2,1)}, u32[]{:S(2)}, u32[]{:S(2)}) %collective-permute-start.21) | collective-permute-done | bytes 655392 | tf_op jit(solution)/shard_map/ppermute | solution.py:18
  111.7 13.3 %collective-permute-done.22.refs_7_.refs_3_ = bf16[2,320,512]{2,1,0:T(8,128)(2,1)} collective-permute-done((bf16[2,320,512]{2,1,0:T(8,128)(2,1)}, bf16[2,320,512]{2,1,0:T(8,128)(2,1)}, u32[]{:S(2)}, u32[]{:S(2)}) %collective-permute-start.22) | collective-permute-done | bytes 655392 | tf_op jit(solution)/shard_map/ppermute | solution.py:18
  125.0 14.8 %collective-permute-done.18.refs_2_ = bf16[2,320,512]{2,1,0:T(8,128)(2,1)} collective-permute-done((bf16[2,320,512]{2,1,0:T(8,128)(2,1)}, bf16[2,320,512]{2,1,0:T(8,128)(2,1)}, u32[]{:S(2)}, u32[]{:S(2)}) %collective-permute-start.18) | collective-permute-done | bytes 655392 | tf_op jit(solution)/shard_map/ppermute | solution.py:18
  139.8 13.3 %collective-permute-done.19.refs_3_ = bf16[2,320,512]{2,1,0:T(8,128)(2,1)} collective-permute-done((bf16[2,320,512]{2,1,0:T(8,128)(2,1)}, bf16[2,320,512]{2,1,0:T(8,128)(2,1)}, u32[]{:S(2)}, u32[]{:S(2)}) %collective-permute-start.19) | collective-permute-done | bytes 655392 | tf_op jit(solution)/shard_map/ppermute | solution.py:18
  156.7 6.0 %all-to-all-start.1 = ((bf16[8,320,512]{2,1,0:T(8,128)(2,1)}), bf16[8,320,512]{2,1,0:T(8,128)(2,1)}, u32[]{:S(2)}, u32[]{:S(2)}) async-start(bf16[8,320,512]{2,1,0:T(8,128)(2,1)} %assemble.4), calls=%async_computation.1 | async-start | bytes 5242880 | tf_op jit(solution)/shard_map/all_to_all | solution.py:385
  164.3 58.4 %all-to-all-done.1.refs_3_.refs_9_ = bf16[8,320,512]{2,1,0:T(8,128)(2,1)} async-done(((bf16[8,320,512]{2,1,0:T(8,128)(2,1)}), bf16[8,320,512]{2,1,0:T(8,128)(2,1)}, u32[]{:S(2)}, u32[]{:S(2)}) %all-to-all-start.1) | async-done | bytes 2621472 | tf_op jit(solution)/shard_map/all_to_all | solution.py:385
  232.4 48.5 %collective-permute-done.29.refs_11_ = bf16[8,320,512]{2,1,0:T(8,128)(2,1)} collective-permute-done((bf16[8,320,512]{2,1,0:T(8,128)(2,1)}, bf16[8,320,512]{2,1,0:T(8,128)(2,1)}, u32[]{:S(2)}, u32[]{:S(2)}) %collective-permute-start.29) | collective-permute-done | bytes 2621472 | tf_op jit(solution)/shard_map/ppermute | solution.py:18
  286.8 4.2 %all-to-all-done.2.refs_4_ = bf16[8,320,512]{2,1,0:T(8,128)(2,1)S(1)} async-done(((bf16[8,320,512]{2,1,0:T(8,128)(2,1)}), bf16[8,320,512]{2,1,0:T(8,128)(2,1)S(1)}, u32[]{:S(2)}, u32[]{:S(2)}) %all-to-all-start.2) | async-done | bytes 2621472 | tf_op jit(solution)/shard_map/all_to_all | solution.py:385
  295.0 32.5 %density.2.after_ref.refs_14_ = f32[960,4096]{1,0:T(8,128)} custom-call(s32[2]{0:T(128)} %get-tuple-element.29.distance_ref, f32[960,1]{1,0:T(8,128)} %sub.71.refs_0_, f32[1,1280]{1,0:T(1,128)} %reshape.63.refs_1_, bf16[8,320,512]{2,1,0:T(8,128)(2,1)} %copy-done.1, bf16[8,320,512]{2,1,0:T(8,128)(2,1)} %all-to-all-done.1.refs_3_.refs_9_, ...), custom_call_target="tpu_custom_call" | custom-call | flops 20132659200 | bytes 34078720 | tf_op jit(solution)/shard_map/density/pallas_call | solution.py:308
  327.5 8.7 %collective-permute-done.25.value_ref = bf16[6,320,512]{2,1,0:T(8,128)(2,1)} collective-permute-done((bf16[6,320,512]{2,1,0:T(8,128)(2,1)}, bf16[6,320,512]{2,1,0:T(8,128)(2,1)}, u32[]{:S(2)}, u32[]{:S(2)}) %collective-permute-start.25) | collective-permute-done | bytes 1966112 | tf_op jit(solution)/shard_map/ppermute | solution.py:18
  344.3 11.5 %integrals.1.after_ref.refs_13_ = f32[960,640]{1,0:T(8,128)} custom-call(s32[2]{0:T(128)} %get-tuple-element.29.distance_ref, f32[960,1]{1,0:T(8,128)} %sub.71.refs_0_, f32[1,640]{1,0:T(1,128)} %reshape.59.refs_1_, bf16[8,320,512]{2,1,0:T(8,128)(2,1)} %copy-done.1, bf16[8,320,512]{2,1,0:T(8,128)(2,1)} %all-to-all-done.1.refs_3_.refs_9_, ...), custom_call_target="tpu_custom_call" | custom-call | flops 3774873600 | bytes 13598720 | tf_op jit(solution)/shard_map/integrals/pallas_call | solution.py:308
  363.1 21.1 %density.3 = bf16[960,4096]{1,0:T(8,128)(2,1)} custom-call(s32[2]{0:T(128)} %get-tuple-element.29.distance_ref, f32[960,1]{1,0:T(8,128)} %sub.71.refs_0_, f32[1,640]{1,0:T(1,128)} %reshape.59.refs_1_, bf16[8,320,512]{2,1,0:T(8,128)(2,1)} %copy-done.1, bf16[8,320,512]{2,1,0:T(8,128)(2,1)} %all-to-all-done.1.refs_3_.refs_9_, bf16[8,320,512]{2,1,0:T(8,128)(2,1)} %copy-done, ...), custom_call_target="tpu_custom_call" | custom-call | flops 6291456000 | bytes 30801920 | tf_op jit(solution)/shard_map/density/pallas_call | solution.py:308
  (122 shorter events, 73.5 us)
Async XLA Ops:
  2.1 65.6 %collective-permute-start.15 = (bf16[2,1,1408,512]{3,2,1,0:T(8,128)(2,1)S(1)}, bf16[2,1,1408,512]{3,2,1,0:T(8,128)(2,1)}, u32[]{:S(2)}, u32[]{:S(2)}) collective-permute-start(bf16[2,1,1408,512]{3,2,1,0:T(8,128)(2,1)S(1)} %slice.37.half_ref), channel_id=1, source_target_pairs={{0,2},{1,3},{2,0},{3,1},{4,6},{5,7},{6,4},{7,5},{8,10},{9,11},{10,... | collective-permute-start | bytes 8650760 | tf_op jit(solution)/shard_map/ppermute | solution.py:18
  15.7 13.7 %collective-permute-start.2 = (bf16[2,80,1408]{2,1,0:T(8,128)(2,1)S(1)}, bf16[2,80,1408]{2,1,0:T(8,128)(2,1)S(1)}, u32[]{:S(2)}, u32[]{:S(2)}) collective-permute-start(bf16[2,80,1408]{2,1,0:T(8,128)(2,1)S(1)} %pad_maximum_fusion.refs_0_), channel_id=1, source_target_pairs={{8,0},{12,4},{16,8},{20,12},{24,16},{28,20},{9,1},{13,5},{17,9},{2... | collective-permute-start | bytes 1351688 | tf_op jit(solution)/shard_map/ppermute | solution.py:24
  17.0 13.8 %collective-permute-start.7 = (bf16[2,80,1408]{2,1,0:T(8,128)(2,1)S(1)}, bf16[2,80,1408]{2,1,0:T(8,128)(2,1)S(1)}, u32[]{:S(2)}, u32[]{:S(2)}) collective-permute-start(bf16[2,80,1408]{2,1,0:T(8,128)(2,1)S(1)} %pad_maximum_fusion.refs_0_), channel_id=1, source_target_pairs={{0,1},{1,0},{2,3},{3,2},{4,5},{5,4},{6,7},{7,6},{8,9},{9,8},{10,11... | collective-permute-start | bytes 1351688 | tf_op jit(solution)/shard_map/ppermute | solution.py:18
  29.4 12.1 %collective-permute-start.4 = (bf16[2,80,1408]{2,1,0:T(8,128)(2,1)S(1)}, bf16[2,80,1408]{2,1,0:T(8,128)(2,1)}, u32[]{:S(2)}, u32[]{:S(2)}) collective-permute-start(bf16[2,80,1408]{2,1,0:T(8,128)(2,1)S(1)} %collective-permute-done.2.refs_2_), channel_id=1, source_target_pairs={{8,0},{12,4},{16,8},{20,12},{24,16},{28,20},{9,1},{13,5},{17,9},{2... | collective-permute-start | bytes 1351688 | tf_op jit(solution)/shard_map/ppermute | solution.py:24
  30.7 12.2 %collective-permute-start.8 = (bf16[2,80,1408]{2,1,0:T(8,128)(2,1)S(1)}, bf16[2,80,1408]{2,1,0:T(8,128)(2,1)S(1)}, u32[]{:S(2)}, u32[]{:S(2)}) collective-permute-start(bf16[2,80,1408]{2,1,0:T(8,128)(2,1)S(1)} %collective-permute-done.1.refs_1_), channel_id=1, source_target_pairs={{0,1},{1,0},{2,3},{3,2},{4,5},{5,4},{6,7},{7,6},{8,9},{9,8},{10,11... | collective-permute-start | bytes 1351688 | tf_op jit(solution)/shard_map/ppermute | solution.py:18
  30.8 12.2 %collective-permute-start.9 = (bf16[2,80,1408]{2,1,0:T(8,128)(2,1)S(1)}, bf16[2,80,1408]{2,1,0:T(8,128)(2,1)S(1)}, u32[]{:S(2)}, u32[]{:S(2)}) collective-permute-start(bf16[2,80,1408]{2,1,0:T(8,128)(2,1)S(1)} %collective-permute-done.2.refs_2_), channel_id=1, source_target_pairs={{0,1},{1,0},{2,3},{3,2},{4,5},{5,4},{6,7},{7,6},{8,9},{9,8},{10,11... | collective-permute-start | bytes 1351688 | tf_op jit(solution)/shard_map/ppermute | solution.py:18
  80.1 76.6 %all-to-all-start = ((bf16[8,320,512]{2,1,0:T(8,128)(2,1)}), bf16[8,320,512]{2,1,0:T(8,128)(2,1)S(1)}, u32[]{:S(2)}, u32[]{:S(2)}) async-start(bf16[8,320,512]{2,1,0:T(8,128)(2,1)} %assemble.3), calls=%async_computation | async-start | bytes 5242880 | tf_op jit(solution)/shard_map/all_to_all | solution.py:385
  93.8 17.9 %collective-permute-start.21 = (bf16[2,320,512]{2,1,0:T(8,128)(2,1)}, bf16[2,320,512]{2,1,0:T(8,128)(2,1)}, u32[]{:S(2)}, u32[]{:S(2)}) collective-permute-start(bf16[2,320,512]{2,1,0:T(8,128)(2,1)} %get-tuple-element.27), channel_id=1, source_target_pairs={{0,2},{1,3},{2,0},{3,1},{4,6},{5,7},{6,4},{7,5},{8,10},{9,11},{10,... | collective-permute-start | bytes 1966088 | tf_op jit(solution)/shard_map/ppermute | solution.py:18
  95.3 29.6 %collective-permute-start.22 = (bf16[2,320,512]{2,1,0:T(8,128)(2,1)}, bf16[2,320,512]{2,1,0:T(8,128)(2,1)}, u32[]{:S(2)}, u32[]{:S(2)}) collective-permute-start(bf16[2,320,512]{2,1,0:T(8,128)(2,1)} %get-tuple-element.25.refs_4_), channel_id=1, source_target_pairs={{0,3},{1,2},{2,1},{3,0},{4,7},{5,6},{6,5},{7,4},{8,11},{9,10},{10,... | collective-permute-start | bytes 1966088 | tf_op jit(solution)/shard_map/ppermute | solution.py:18
  103.3 21.6 %collective-permute-start.17 = (bf16[2,320,512]{2,1,0:T(8,128)(2,1)}, bf16[2,320,512]{2,1,0:T(8,128)(2,1)}, u32[]{:S(2)}, u32[]{:S(2)}) collective-permute-start(bf16[2,320,512]{2,1,0:T(8,128)(2,1)} %get-tuple-element.22), channel_id=1, source_target_pairs={{0,1},{1,0},{2,3},{3,2},{4,5},{5,4},{6,7},{7,6},{8,9},{9,8},{10,11... | collective-permute-start | bytes 1966088 | tf_op jit(solution)/shard_map/ppermute | solution.py:18
  103.6 36.2 %collective-permute-start.18 = (bf16[2,320,512]{2,1,0:T(8,128)(2,1)}, bf16[2,320,512]{2,1,0:T(8,128)(2,1)}, u32[]{:S(2)}, u32[]{:S(2)}) collective-permute-start(bf16[2,320,512]{2,1,0:T(8,128)(2,1)} %get-tuple-element.23), channel_id=1, source_target_pairs={{0,2},{1,3},{2,0},{3,1},{4,6},{5,7},{6,4},{7,5},{8,10},{9,11},{10,... | collective-permute-start | bytes 1966088 | tf_op jit(solution)/shard_map/ppermute | solution.py:18
  105.1 48.0 %collective-permute-start.19 = (bf16[2,320,512]{2,1,0:T(8,128)(2,1)}, bf16[2,320,512]{2,1,0:T(8,128)(2,1)}, u32[]{:S(2)}, u32[]{:S(2)}) collective-permute-start(bf16[2,320,512]{2,1,0:T(8,128)(2,1)} %get-tuple-element.24), channel_id=1, source_target_pairs={{0,3},{1,2},{2,1},{3,0},{4,7},{5,6},{6,5},{7,4},{8,11},{9,10},{10,... | collective-permute-start | bytes 1966088 | tf_op jit(solution)/shard_map/ppermute | solution.py:18
  156.7 66.0 %all-to-all-start.1 = ((bf16[8,320,512]{2,1,0:T(8,128)(2,1)}), bf16[8,320,512]{2,1,0:T(8,128)(2,1)}, u32[]{:S(2)}, u32[]{:S(2)}) async-start(bf16[8,320,512]{2,1,0:T(8,128)(2,1)} %assemble.4), calls=%async_computation.1 | async-start | bytes 5242880 | tf_op jit(solution)/shard_map/all_to_all | solution.py:385
  162.7 61.4 %collective-permute-start.23 = (bf16[8,320,512]{2,1,0:T(8,128)(2,1)S(1)}, bf16[8,320,512]{2,1,0:T(8,128)(2,1)}, u32[]{:S(2)}, u32[]{:S(2)}) collective-permute-start(bf16[8,320,512]{2,1,0:T(8,128)(2,1)S(1)} %all-to-all-done.refs_2_.refs_5_), channel_id=1, source_target_pairs={{0,2},{1,3},{2,0},{3,1},{4,6},{5,7},{6,4},{7,5},{8,10},{9,11},{10,... | collective-permute-start | bytes 7864328 | tf_op jit(solution)/shard_map/ppermute | solution.py:18
  222.7 58.2 %collective-permute-start.29 = (bf16[8,320,512]{2,1,0:T(8,128)(2,1)}, bf16[8,320,512]{2,1,0:T(8,128)(2,1)}, u32[]{:S(2)}, u32[]{:S(2)}) collective-permute-start(bf16[8,320,512]{2,1,0:T(8,128)(2,1)} %all-to-all-done.1.refs_3_.refs_9_), channel_id=1, source_target_pairs={{0,2},{1,3},{2,0},{3,1},{4,6},{5,7},{6,4},{7,5},{8,10},{9,11},{10,... | collective-permute-start | bytes 7864328 | tf_op jit(solution)/shard_map/ppermute | solution.py:18
  227.9 63.2 %all-to-all-start.2 = ((bf16[8,320,512]{2,1,0:T(8,128)(2,1)}), bf16[8,320,512]{2,1,0:T(8,128)(2,1)S(1)}, u32[]{:S(2)}, u32[]{:S(2)}) async-start(bf16[8,320,512]{2,1,0:T(8,128)(2,1)} %assemble.5), calls=%async_computation.2 | async-start | bytes 5242880 | tf_op jit(solution)/shard_map/all_to_all | solution.py:385
  231.8 63.2 %collective-permute-start.28 = (bf16[8,320,512]{2,1,0:T(8,128)(2,1)}, bf16[8,320,512]{2,1,0:T(8,128)(2,1)}, u32[]{:S(2)}, u32[]{:S(2)}) collective-permute-start(bf16[8,320,512]{2,1,0:T(8,128)(2,1)} %all-to-all-done.1.refs_3_.refs_9_), channel_id=1, source_target_pairs={{0,1},{1,0},{2,3},{3,2},{4,5},{5,4},{6,7},{7,6},{8,9},{9,8},{10,11... | collective-permute-start | bytes 7864328 | tf_op jit(solution)/shard_map/ppermute | solution.py:18
  231.9 63.1 %collective-permute-start.26 = (bf16[8,320,512]{2,1,0:T(8,128)(2,1)}, bf16[8,320,512]{2,1,0:T(8,128)(2,1)}, u32[]{:S(2)}, u32[]{:S(2)}) collective-permute-start(bf16[8,320,512]{2,1,0:T(8,128)(2,1)} %copy-done.1), channel_id=1, source_target_pairs={{0,1},{1,0},{2,3},{3,2},{4,5},{5,4},{6,7},{7,6},{8,9},{9,8},{10,11... | collective-permute-start | bytes 7864328 | tf_op jit(solution)/shard_map/ppermute | solution.py:18
  280.9 14.1 %collective-permute-start.30 = (bf16[8,320,512]{2,1,0:T(8,128)(2,1)}, bf16[8,320,512]{2,1,0:T(8,128)(2,1)}, u32[]{:S(2)}, u32[]{:S(2)}) collective-permute-start(bf16[8,320,512]{2,1,0:T(8,128)(2,1)} %collective-permute-done.29.refs_11_), channel_id=1, source_target_pairs={{0,1},{1,0},{2,3},{3,2},{4,5},{5,4},{6,7},{7,6},{8,9},{9,8},{10,11... | collective-permute-start | bytes 7864328 | tf_op jit(solution)/shard_map/ppermute | solution.py:18
  280.9 14.1 %collective-permute-start.27 = (bf16[8,320,512]{2,1,0:T(8,128)(2,1)}, bf16[8,320,512]{2,1,0:T(8,128)(2,1)}, u32[]{:S(2)}, u32[]{:S(2)}) collective-permute-start(bf16[8,320,512]{2,1,0:T(8,128)(2,1)} %collective-permute-done.23.refs_4_.refs_7_), channel_id=1, source_target_pairs={{0,1},{1,0},{2,3},{3,2},{4,5},{5,4},{6,7},{7,6},{8,9},{9,8},{10,11... | collective-permute-start | bytes 7864328 | tf_op jit(solution)/shard_map/ppermute | solution.py:18
  292.6 43.6 %collective-permute-start.25 = (bf16[6,320,512]{2,1,0:T(8,128)(2,1)}, bf16[6,320,512]{2,1,0:T(8,128)(2,1)}, u32[]{:S(2)}, u32[]{:S(2)}) collective-permute-start(bf16[6,320,512]{2,1,0:T(8,128)(2,1)} %slice.38.refs_5_), channel_id=1, source_target_pairs={{0,2},{1,3},{2,0},{3,1},{4,6},{5,7},{6,4},{7,5},{8,10},{9,11},{10,... | collective-permute-start | bytes 5898248 | tf_op jit(solution)/shard_map/ppermute | solution.py:18
  295.0 46.3 %collective-permute-start.24 = (bf16[6,320,512]{2,1,0:T(8,128)(2,1)}, bf16[6,320,512]{2,1,0:T(8,128)(2,1)}, u32[]{:S(2)}, u32[]{:S(2)}) collective-permute-start(bf16[6,320,512]{2,1,0:T(8,128)(2,1)} %slice.38.refs_5_), channel_id=1, source_target_pairs={{0,1},{1,0},{2,3},{3,2},{4,5},{5,4},{6,7},{7,6},{8,9},{9,8},{10,11... | collective-permute-start | bytes 5898248 | tf_op jit(solution)/shard_map/ppermute | solution.py:18
  340.0 17.2 %collective-permute-start.33 = (bf16[2,320,512]{2,1,0:T(8,128)(2,1)S(1)}, bf16[2,320,512]{2,1,0:T(8,128)(2,1)S(1)}, u32[]{:S(2)}, u32[]{:S(2)}) collective-permute-start(bf16[2,320,512]{2,1,0:T(8,128)(2,1)S(1)} %slice.39.refs_9_), channel_id=1, source_target_pairs={{0,2},{1,3},{2,0},{3,1},{4,6},{5,7},{6,4},{7,5},{8,10},{9,11},{10,... | collective-permute-start | bytes 1966088 | tf_op jit(solution)/shard_map/ppermute | solution.py:18
  341.0 18.9 %collective-permute-start.32 = (bf16[2,320,512]{2,1,0:T(8,128)(2,1)S(1)}, bf16[2,320,512]{2,1,0:T(8,128)(2,1)}, u32[]{:S(2)}, u32[]{:S(2)}) collective-permute-start(bf16[2,320,512]{2,1,0:T(8,128)(2,1)S(1)} %slice.39.refs_9_), channel_id=1, source_target_pairs={{0,1},{1,0},{2,3},{3,2},{4,5},{5,4},{6,7},{7,6},{8,9},{9,8},{10,11... | collective-permute-start | bytes 1966088 | tf_op jit(solution)/shard_map/ppermute | solution.py:18
  (34 other events, 500.2 us)

commit v3 on v2

--- a/solution.py
+++ b/solution.py
@@ -70,63 +70,85 @@
     return placed.reshape(line * 4 * part, depth)
 
 
-def transform_kernel(width, index_ref, coeff_ref, half_ref, *out_refs):
+def transform_kernel(width, distances, index_ref, coeff_ref, half_ref, *refs):
     half = half_ref[0, 0]
-    for distance, out_ref in enumerate(out_refs):
-        start = pl.multiple_of((index_ref[0] ^ distance) * width, width)
+    out_refs = refs[-len(distances) :]
+    for distance, out_ref in zip(distances, out_refs):
+        place = (index_ref[0] ^ distance) % (coeff_ref.shape[0] // width)
+        start = pl.multiple_of(place * width, width)
         product = jnp.dot(
             coeff_ref[pl.ds(start, width), :], half, preferred_element_type=jnp.float32
         )
         out_ref[0] = product.astype(out_ref.dtype)
 
 
-def transform(coeff_rows, half, orbital, pair_index, reach):
+def transform(coeff_rows, half, orbital, pair_index, distances, after=()):
+    pair_count = lax.axis_size("pair")
     blocks, _, depth, aux_slice = half.shape
-    width = coeff_rows.shape[0] // lax.axis_size("pair")
+    width = coeff_rows.shape[0] // pair_count
+    near = 2 if max(distances) < 2 else pair_count
+    count = len(distances)
     grid_spec = pltpu.PrefetchScalarGridSpec(
         num_scalar_prefetch=1,
         grid=(blocks,),
         in_specs=[
-            pl.BlockSpec(coeff_rows.shape, lambda b, index: (0, 0)),
+            pl.BlockSpec((near * width, depth), lambda b, index: (index[0] // near, 0)),
             pl.BlockSpec((1, 1, depth, aux_slice), lambda b, index: (b, orbital, 0, 0)),
-        ],
-        out_specs=[pl.BlockSpec((1, width, aux_slice), lambda b, index: (b, 0, 0))] * reach,
+        ]
+        + [ANY] * len(after),
+        out_specs=[pl.BlockSpec((1, width, aux_slice), lambda b, index: (b, 0, 0))] * count,
     )
     return pl.pallas_call(
-        functools.partial(transform_kernel, width),
+        functools.partial(transform_kernel, width, distances),
         grid_spec=grid_spec,
-        out_shape=[jax.ShapeDtypeStruct((blocks, width, aux_slice), jnp.bfloat16)] * reach,
+        out_shape=[jax.ShapeDtypeStruct((blocks, width, aux_slice), jnp.bfloat16)] * count,
         compiler_params=pltpu.CompilerParams(vmem_limit_bytes=VMEM_LIMIT),
         cost_estimate=pl.CostEstimate(
-            flops=2 * blocks * reach * width * depth * aux_slice,
-            bytes_accessed=2 * (coeff_rows.size + blocks * (depth + reach * width) * aux_slice),
+            flops=2 * blocks * count * width * depth * aux_slice,
+            bytes_accessed=2 * (near * width * depth + blocks * (depth + count * width) * aux_slice),
             transcendentals=0,
         ),
         name="transform",
-    )(pair_index.reshape(1), coeff_rows, half)
+    )(pair_index.reshape(1), coeff_rows, half, *after)
 
 
 def assemble_kernel(count, index_ref, *refs):
-    piece_refs, out_ref = refs[:count], refs[-1]
-    for number, ref in enumerate(piece_refs):
-        @pl.when(pl.program_id(0) == number)
-        def _():
-            out_ref[...] = ref[...]
+    piece_refs, (out_ref, held, arrived, left) = refs[:count], refs[-4:]
+    blocks = held.shape[1]
+    inward = [
+        pltpu.make_async_copy(ref, held.at[number], arrived.at[number])
+        for number, ref in enumerate(piece_refs)
+    ]
+    outward = [
+        pltpu.make_async_copy(
+            held.at[number],
+            out_ref.at[pl.ds((index_ref[0] ^ number) * blocks, blocks)],
+            left.at[number],
+        )
+        for number in range(count)
+    ]
+    for copy in inward:
+        copy.start()
+    for come, go in zip(inward, outward):
+        come.wait()
+        go.start()
+    for copy in outward:
+        copy.wait()
 
 
 def assemble(pieces, pair_index, after):
     count = len(pieces)
-    blocks, width, piece = pieces[0].shape
-    whole = pl.BlockSpec((blocks, width, piece), lambda n, index: (0, 0, 0))
+    shape, dtype = pieces[0].shape, pieces[0].dtype
     return pl.pallas_call(
         functools.partial(assemble_kernel, count),
-        grid_spec=pltpu.PrefetchScalarGridSpec(
-            num_scalar_prefetch=1,
-            grid=(count,),
-            in_specs=[whole] * count + [ANY] * len(after),
-            out_specs=pl.BlockSpec((blocks, width, piece), lambda n, index: (index[0] ^ n, 0, 0)),
-        ),
-        out_shape=jax.ShapeDtypeStruct((count * blocks, width, piece), pieces[0].dtype),
+        in_specs=[pl.BlockSpec(memory_space=pltpu.SMEM)] + [ANY] * (count + len(after)),
+        out_specs=ANY,
+        out_shape=jax.ShapeDtypeStruct((count * shape[0], *shape[1:]), dtype),
+        scratch_shapes=[
+            pltpu.VMEM((count, *shape), dtype),
+            pltpu.SemaphoreType.DMA((count,)),
+            pltpu.SemaphoreType.DMA((count,)),
+        ],
         cost_estimate=pl.CostEstimate(
             flops=0, bytes_accessed=4 * count * pieces[0].size, transcendentals=0
         ),
@@ -189,9 +211,17 @@
 
     @pl.when(step == 0)
     def _():
+        wanted = []
         for orbital, parts in enumerate(held_refs):
             for first, last, blocks in parts:
-                begin, end = (first, last) if ends else (max(first, low), min(last, high))
+                wanted.append((orbital, first, blocks, max(first, low), min(last, high)))
+        if ends:
+            for orbital, parts in enumerate(held_refs):
+                for first, last, blocks in parts:
+                    wanted.append((orbital, first, blocks, first, min(last, low)))
+                    wanted.append((orbital, first, blocks, max(first, high), last))
+        for orbital, first, blocks, begin, end in wanted:
+            if begin < end:
 
                 @pl.loop(begin, end)
                 def _(t):
@@ -239,21 +269,21 @@
     if ends:
         @pl.when(step >= turns)
         def _():
-            now = step - turns
-
-            @pl.when((now < low) | (now >= high))
-            def _():
-                wait_for(now)
-
-            product = jnp.dot(amplitudes[...], remote_ref[now], preferred_element_type=jnp.float32)
+            now = (step - turns) * GROUP
+            for ahead in range(GROUP):
+                @pl.when((now + ahead < low) | (now + ahead >= high))
+                def _():
+                    wait_for(now + ahead)
+
+            remote = jnp.concatenate([remote_ref[now + ahead] for ahead in range(GROUP)], axis=1)
+            product = jnp.dot(amplitudes[...], remote, preferred_element_type=jnp.float32)
             if has_total:
                 product = product + total_ref[...]
             out_ref[...] = product.astype(out_ref.dtype)
 
 
 def add_density(
-    locals_, held, distances, left_energy, right_energy, span, ends, start=None, total=None,
-    out_dtype=jnp.float32,
+    locals_, held, distances, left_energy, right_energy, span, ends, start=None, total=None
 ):
     occ_width, pair_count = len(locals_), len(held[0][0][2])
     steps = distances.shape[0]
@@ -286,8 +316,8 @@
         pltpu.SemaphoreType.DMA((len(held) * steps, slices)),
     ]
     if ends:
-        out_spec = pl.BlockSpec((rows, aux_slice), lambda t, d: (0, jnp.maximum(t - turns, 0)))
-        out_shape = jax.ShapeDtypeStruct((rows, slices * aux_slice), out_dtype)
+        out_spec = pl.BlockSpec((rows, GROUP * aux_slice), lambda t, d: (0, jnp.maximum(t - turns, 0)))
+        out_shape = jax.ShapeDtypeStruct((rows, slices * aux_slice), jnp.bfloat16)
         scratch = [
             pltpu.VMEM((rows, columns), jnp.float32),
             pltpu.VMEM((rows, columns), jnp.bfloat16),
@@ -295,7 +325,7 @@
         if total is not None:
             in_specs.append(out_spec)
             operands.append(total)
-            moved += total.size * 4
+            moved += total.size * 2
     else:
         out_spec = whole
         out_shape = jax.ShapeDtypeStruct((rows, columns), jnp.float32)
@@ -309,7 +339,7 @@
         functools.partial(density_kernel, plan),
         grid_spec=pltpu.PrefetchScalarGridSpec(
             num_scalar_prefetch=1,
-            grid=(turns + (slices if ends else 0),),
+            grid=(turns + (slices // GROUP if ends else 0),),
             in_specs=in_specs,
             out_specs=out_spec,
             scratch_shapes=scratch,
@@ -363,20 +393,25 @@
 
     first = []
     for raw in spread(half[:, :1]):
-        own, other = transform(coeff_rows, raw, 0, pair_index, 2)
+        own, other = transform(coeff_rows, raw, 0, pair_index, (0, 1))
         first += [own, swap(other, 1)]
+    distant = tuple(range(2, pair_count))
     parts = [
-        transform(coeff_rows, half, orbital, pair_index, pair_count)
+        transform(coeff_rows, half, orbital, pair_index, distant)
         for orbital in range(1, occ_width)
     ]
-    moved = [first] + [
-        [pieces[0]] + [swap(pieces[d], d) for d in range(1, pair_count)] for pieces in parts
-    ]
+    moved = [first] + [[swap(piece, d) for piece, d in zip(pieces, distant)] for pieces in parts]
+    for orbital in range(1, occ_width):
+        own, other = transform(coeff_rows, half, orbital, pair_index, (0, 1), moved[1][:1])
+        moved[orbital] = [own, swap(other, 1)] + moved[orbital]
 
     locals_, far = [], []
+    final = occ_width - 1
     middle = aux_count * 3 // 4
     for orbital in range(occ_width):
         after = [pieces[-1] for pieces in parts[1:]] if orbital == 1 else []
+        if orbital == 0 and final:
+            after.append(parts[0][-1])
         if orbital > 1:
             after.append(far[orbital - 2][-1])
         if 0 < orbital < occ_width - 1:
@@ -411,7 +446,7 @@
     upper = (middle, aux_count, share(halves[1], start))
     total = add_density(
         locals_, [[lower, upper]], distances, left_energy, right_energy, (middle, aux_count), True,
-        start=start, total=total, out_dtype=jnp.bfloat16,
+        start=start, total=total,
     )
     return jnp.transpose(total.reshape(occ_width, vir_width, -1), (1, 0, 2))
 

time: 385 us -> 374 us (0.971)
  waiting for transfers between devices: 206 us -> 196 us
  Pallas kernels: 112 us -> 108 us
    ppermute x29, waiting for transfers between devices: 122 us -> 113 us  [swap(): return lax.ppermute(value, axis, pairs)]
    pallas_call x3, Pallas kernels: 65 us -> 59.6 us  [add_density(): pl.pallas_call(functools.partial(density_kernel, plan), grid_spec=pltpu.P...]
    pallas_call x7 -> x9, Pallas kernels: 37.4 us -> 39.4 us  [the longest x6 31.5 us: transform(): pl.pallas_call(functools.partial(transform_kernel, width, distances), gri...]
  transfers between devices with their start and end apart: 38 -> 38, of which waited for: 19 -> 17; matrix products, arithmetic and copies ran while one was open for 3% -> 3% of each run, Pallas kernels for 23% -> 24%
where the time goes in v3:
time: 374 us; the launch traced here: 373 us
  waiting for transfers between devices  196 us (52%)
  Pallas kernels  108 us (29%)
  starting transfers between devices  48.8 us (13%)
  local copies, waits for them, and re-layouts  15.3 us (4%)
    ppermute x29, waiting for transfers between devices, swap(): return lax.ppermute(value, axis, pairs)  113 us
    all_to_all x3, waiting for transfers between devices, per_device(): local = lax.all_to_all(sent, 'aux', split_axis=0, concat_axis=0, tiled=True)  61.9 us
    pallas_call x3, Pallas kernels, add_density(): pl.pallas_call(functools.partial(density_kernel, plan), grid_spec=pltpu.P...  59.6 us
    pallas_call x6, Pallas kernels, transform(): pl.pallas_call(functools.partial(transform_kernel, width, distances), gri...  31.5 us
    ppermute x6, waiting for transfers between devices, along(): return lax.ppermute(value, 'aux', pairs)  21.1 us
    ppermute x6, starting transfers between devices, along(): return lax.ppermute(value, 'aux', pairs)  17.8 us
    all_to_all x3, starting transfers between devices, per_device(): local = lax.all_to_all(sent, 'aux', split_axis=0, concat_axis=0, tiled=True)  15.5 us
    ppermute x29, starting transfers between devices, swap(): return lax.ppermute(value, axis, pairs)  15.4 us
  transfers between devices with their start and end apart: 38, of which 17 were waited for; matrix products, arithmetic and copies ran while one was open for 3% of the time, Pallas kernels for 24%

profile of v3, /device:TPU:0, one launch (start us, length us, event | category | flops | bytes accessed | tf_op | source)
XLA Modules:
  0.0 373.2 jit_solution(3991213131575157439)
XLA Ops:
  6.7 5.5 %collective-permute-done = bf16[80,1408]{1,0:T(8,128)(2,1)S(1)} collective-permute-done((bf16[80,1408]{1,0:T(8,128)(2,1)S(1)}, bf16[80,1408]{1,0:T(8,128)(2,1)S(1)}, u32[]{:S(2)}, u32[]{:S(2)}) %collective-permute-start) | collective-permute-done | bytes 225312 | tf_op jit(solution)/shard_map/ppermute | solution.py:18
  17.1 7.1 %collective-permute-done.1.refs_1_ = bf16[2,80,1408]{2,1,0:T(8,128)(2,1)S(1)} collective-permute-done((bf16[2,80,1408]{2,1,0:T(8,128)(2,1)S(1)}, bf16[2,80,1408]{2,1,0:T(8,128)(2,1)S(1)}, u32[]{:S(2)}, u32[]{:S(2)}) %collective-permute-start.1) | collective-permute-done | bytes 450592 | tf_op jit(solution)/shard_map/ppermute | solution.py:24
  24.2 5.2 %collective-permute-start.3 = (bf16[2,80,1408]{2,1,0:T(8,128)(2,1)S(1)}, bf16[2,80,1408]{2,1,0:T(8,128)(2,1)}, u32[]{:S(2)}, u32[]{:S(2)}) collective-permute-start(bf16[2,80,1408]{2,1,0:T(8,128)(2,1)S(1)} %collective-permute-done.1.refs_1_), channel_id=1, source_target_pairs={{0,8},{4,12},{8,16},{12,20},{16,24},{20,28},{1,9},{5,13},{9,17},{1... | collective-permute-start | bytes 1351688 | tf_op jit(solution)/shard_map/ppermute | solution.py:24
  31.3 4.9 %collective-permute-done.3.refs_3_ = bf16[2,80,1408]{2,1,0:T(8,128)(2,1)} collective-permute-done((bf16[2,80,1408]{2,1,0:T(8,128)(2,1)S(1)}, bf16[2,80,1408]{2,1,0:T(8,128)(2,1)}, u32[]{:S(2)}, u32[]{:S(2)}) %collective-permute-start.3) | collective-permute-done | bytes 450592 | tf_op jit(solution)/shard_map/ppermute | solution.py:24
  36.3 5.3 %collective-permute-start.5 = (bf16[2,80,1408]{2,1,0:T(8,128)(2,1)}, bf16[2,80,1408]{2,1,0:T(8,128)(2,1)}, u32[]{:S(2)}, u32[]{:S(2)}) collective-permute-start(bf16[2,80,1408]{2,1,0:T(8,128)(2,1)} %collective-permute-done.3.refs_3_), channel_id=1, source_target_pairs={{0,8},{4,12},{8,16},{12,20},{16,24},{20,28},{1,9},{5,13},{9,17},{1... | collective-permute-start | bytes 1351688 | tf_op jit(solution)/shard_map/ppermute | solution.py:24
  47.8 4.9 %collective-permute-done.6.refs_6_ = bf16[2,80,1408]{2,1,0:T(8,128)(2,1)} collective-permute-done((bf16[2,80,1408]{2,1,0:T(8,128)(2,1)}, bf16[2,80,1408]{2,1,0:T(8,128)(2,1)}, u32[]{:S(2)}, u32[]{:S(2)}) %collective-permute-start.6) | collective-permute-done | bytes 450592 | tf_op jit(solution)/shard_map/ppermute | solution.py:24
  54.9 4.9 %place.1 = bf16[4,2,2,80,1408]{4,3,2,1,0:T(8,128)(2,1)} custom-call(s32[3]{0:T(128)} %pad_add_fusion.index_ref, bf16[2,80,1408]{2,1,0:T(8,128)(2,1)} %copy-done.7, bf16[2,80,1408]{2,1,0:T(8,128)(2,1)} %copy-done.13, bf16[2,80,1408]{2,1,0:T(8,128)(2,1)} %copy-done.14, bf16[2,80,1408]{2,1,0:T(8,128)(2,1)} %collective-permute-done.3.refs_3_, ...), custom_call_target="tpu_custom_call" | custom-call | bytes 7208960 | tf_op jit(solution)/shard_map/place/pallas_call | solution.py:58
  59.8 5.1 %transform.6 = (bf16[2,320,512]{2,1,0:T(8,128)(2,1)}, bf16[2,320,512]{2,1,0:T(8,128)(2,1)}) custom-call(s32[1]{0:T(128)} %bitcast.3.index_ref, bf16[1280,1408]{1,0:T(8,128)(2,1)} %bitcast.25, bf16[2,1,1408,512]{3,2,1,0:T(8,128)(2,1)} %copy-done.3), custom_call_target="tpu_custom_call" | custom-call | flops 1845493760 | bytes 5996544 | tf_op jit(solution)/shard_map/transform/pallas_call | solution.py:101
  67.7 5.0 %transform.7 = (bf16[2,320,512]{2,1,0:T(8,128)(2,1)}, bf16[2,320,512]{2,1,0:T(8,128)(2,1)}) custom-call(s32[1]{0:T(128)} %bitcast.3.index_ref, bf16[1280,1408]{1,0:T(8,128)(2,1)} %bitcast.26, bf16[2,1,1408,512]{3,2,1,0:T(8,128)(2,1)} %collective-permute-done.15.half_ref), custom_call_target="tpu_custom_call" | custom-call | flops 1845493760 | bytes 5996544 | tf_op jit(solution)/shard_map/transform/pallas_call | solution.py:101
  72.7 5.6 %transform.8 = (bf16[2,320,512]{2,1,0:T(8,128)(2,1)}, bf16[2,320,512]{2,1,0:T(8,128)(2,1)}) custom-call(s32[1]{0:T(128)} %bitcast.3.index_ref, bf16[1280,1408]{1,0:T(8,128)(2,1)} %bitcast.27, bf16[2,3,1408,512]{3,2,1,0:T(8,128)(2,1)} %bitcast.21), custom_call_target="tpu_custom_call" | custom-call | flops 1845493760 | bytes 7798784 | tf_op jit(solution)/shard_map/transform/pallas_call | solution.py:101
  82.1 6.1 %all-to-all-start = ((bf16[8,320,512]{2,1,0:T(8,128)(2,1)}), bf16[8,320,512]{2,1,0:T(8,128)(2,1)S(1)}, u32[]{:S(2)}, u32[]{:S(2)}) async-start(bf16[8,320,512]{2,1,0:T(8,128)(2,1)} %assemble.3), calls=%async_computation | async-start | bytes 5242880 | tf_op jit(solution)/shard_map/all_to_all | solution.py:420
  89.8 5.6 %transform.10 = (bf16[2,320,512]{2,1,0:T(8,128)(2,1)}, bf16[2,320,512]{2,1,0:T(8,128)(2,1)}) custom-call(s32[1]{0:T(128)} %bitcast.3.index_ref, bf16[1280,1408]{1,0:T(8,128)(2,1)} %bitcast.28, bf16[2,3,1408,512]{3,2,1,0:T(8,128)(2,1)} %bitcast.22), custom_call_target="tpu_custom_call" | custom-call | flops 1845493760 | bytes 7798784 | tf_op jit(solution)/shard_map/transform/pallas_call | solution.py:101
  97.3 8.7 %collective-permute-done.17.refs_0_.refs_2_ = bf16[2,320,512]{2,1,0:T(8,128)(2,1)S(1)} collective-permute-done((bf16[2,320,512]{2,1,0:T(8,128)(2,1)}, bf16[2,320,512]{2,1,0:T(8,128)(2,1)S(1)}, u32[]{:S(2)}, u32[]{:S(2)}) %collective-permute-start.17) | collective-permute-done | bytes 655392 | tf_op jit(solution)/shard_map/ppermute | solution.py:18
  106.8 5.1 %transform.9 = (bf16[2,320,512]{2,1,0:T(8,128)(2,1)}, bf16[2,320,512]{2,1,0:T(8,128)(2,1)}) custom-call(s32[1]{0:T(128)} %bitcast.3.index_ref, bf16[1280,1408]{1,0:T(8,128)(2,1)} %bitcast.29, bf16[2,3,1408,512]{3,2,1,0:T(8,128)(2,1)} %bitcast.23, bf16[2,320,512]{2,1,0:T(8,128)(2,1)} %copy-done.4), custom_call_target="tpu_custom_call" | custom-call | flops 1845493760 | bytes 5996544 | tf_op jit(solution)/shard_map/transform/pallas_call | solution.py:101
  111.9 5.1 %transform.11 = (bf16[2,320,512]{2,1,0:T(8,128)(2,1)}, bf16[2,320,512]{2,1,0:T(8,128)(2,1)}) custom-call(s32[1]{0:T(128)} %bitcast.3.index_ref, bf16[1280,1408]{1,0:T(8,128)(2,1)} %bitcast.30, bf16[2,3,1408,512]{3,2,1,0:T(8,128)(2,1)} %bitcast.24, bf16[2,320,512]{2,1,0:T(8,128)(2,1)} %get-tuple-element.23.refs_0_), custom_call_target="tpu_custom_call" | custom-call | flops 1845493760 | bytes 5996544 | tf_op jit(solution)/shard_map/transform/pallas_call | solution.py:101
  117.5 16.7 %collective-permute-done.21.refs_6_.refs_2_ = bf16[2,320,512]{2,1,0:T(8,128)(2,1)} collective-permute-done((bf16[2,320,512]{2,1,0:T(8,128)(2,1)}, bf16[2,320,512]{2,1,0:T(8,128)(2,1)}, u32[]{:S(2)}, u32[]{:S(2)}) %collective-permute-start.21) | collective-permute-done | bytes 655392 | tf_op jit(solution)/shard_map/ppermute | solution.py:18
  134.2 12.6 %collective-permute-done.22.refs_7_.refs_3_ = bf16[2,320,512]{2,1,0:T(8,128)(2,1)} collective-permute-done((bf16[2,320,512]{2,1,0:T(8,128)(2,1)}, bf16[2,320,512]{2,1,0:T(8,128)(2,1)}, u32[]{:S(2)}, u32[]{:S(2)}) %collective-permute-start.22) | collective-permute-done | bytes 655392 | tf_op jit(solution)/shard_map/ppermute | solution.py:18
  151.2 5.5 %all-to-all-start.1 = ((bf16[8,320,512]{2,1,0:T(8,128)(2,1)}), bf16[8,320,512]{2,1,0:T(8,128)(2,1)}, u32[]{:S(2)}, u32[]{:S(2)}) async-start(bf16[8,320,512]{2,1,0:T(8,128)(2,1)} %assemble.4), calls=%async_computation.1 | async-start | bytes 5242880 | tf_op jit(solution)/shard_map/all_to_all | solution.py:420
  158.2 59.0 %all-to-all-done.1.refs_3_.refs_9_ = bf16[8,320,512]{2,1,0:T(8,128)(2,1)} async-done(((bf16[8,320,512]{2,1,0:T(8,128)(2,1)}), bf16[8,320,512]{2,1,0:T(8,128)(2,1)}, u32[]{:S(2)}, u32[]{:S(2)}) %all-to-all-start.1) | async-done | bytes 2621472 | tf_op jit(solution)/shard_map/all_to_all | solution.py:420
  226.0 50.1 %collective-permute-done.29.refs_11_ = bf16[8,320,512]{2,1,0:T(8,128)(2,1)} collective-permute-done((bf16[8,320,512]{2,1,0:T(8,128)(2,1)}, bf16[8,320,512]{2,1,0:T(8,128)(2,1)}, u32[]{:S(2)}, u32[]{:S(2)}) %collective-permute-start.29) | collective-permute-done | bytes 2621472 | tf_op jit(solution)/shard_map/ppermute | solution.py:18
  288.7 31.7 %density.2.after_ref.refs_14_ = bf16[960,4096]{1,0:T(8,128)(2,1)} custom-call(s32[2]{0:T(128)} %get-tuple-element.29.distance_ref, f32[960,1]{1,0:T(8,128)} %sub.71.refs_0_, f32[1,1280]{1,0:T(1,128)} %reshape.65.refs_1_, bf16[8,320,512]{2,1,0:T(8,128)(2,1)} %copy-done.1, bf16[8,320,512]{2,1,0:T(8,128)(2,1)} %all-to-all-done.1.refs_3_.refs_9_, ...), custom_call_target="tpu_custom_call" | custom-call | flops 20132659200 | bytes 26214400 | tf_op jit(solution)/shard_map/density/pallas_call | solution.py:338
  320.4 9.4 %collective-permute-done.25.value_ref = bf16[6,320,512]{2,1,0:T(8,128)(2,1)} collective-permute-done((bf16[6,320,512]{2,1,0:T(8,128)(2,1)}, bf16[6,320,512]{2,1,0:T(8,128)(2,1)}, u32[]{:S(2)}, u32[]{:S(2)}) %collective-permute-start.25) | collective-permute-done | bytes 1966112 | tf_op jit(solution)/shard_map/ppermute | solution.py:18
  337.9 11.5 %integrals.1.after_ref.refs_13_ = f32[960,640]{1,0:T(8,128)} custom-call(s32[2]{0:T(128)} %get-tuple-element.29.distance_ref, f32[960,1]{1,0:T(8,128)} %sub.71.refs_0_, f32[1,640]{1,0:T(1,128)} %reshape.61.refs_1_, bf16[8,320,512]{2,1,0:T(8,128)(2,1)} %copy-done.1, bf16[8,320,512]{2,1,0:T(8,128)(2,1)} %all-to-all-done.1.refs_3_.refs_9_, ...), custom_call_target="tpu_custom_call" | custom-call | flops 3774873600 | bytes 13598720 | tf_op jit(solution)/shard_map/integrals/pallas_call | solution.py:338
  356.6 16.4 %density.3 = bf16[960,4096]{1,0:T(8,128)(2,1)} custom-call(s32[2]{0:T(128)} %get-tuple-element.29.distance_ref, f32[960,1]{1,0:T(8,128)} %sub.71.refs_0_, f32[1,640]{1,0:T(1,128)} %reshape.61.refs_1_, bf16[8,320,512]{2,1,0:T(8,128)(2,1)} %copy-done.1, bf16[8,320,512]{2,1,0:T(8,128)(2,1)} %all-to-all-done.1.refs_3_.refs_9_, bf16[8,320,512]{2,1,0:T(8,128)(2,1)} %copy-done, ...), custom_call_target="tpu_custom_call" | custom-call | flops 6291456000 | bytes 22937600 | tf_op jit(solution)/shard_map/density/pallas_call | solution.py:338
  (130 shorter events, 74.5 us)
Async XLA Ops:
  2.1 65.6 %collective-permute-start.15 = (bf16[2,1,1408,512]{3,2,1,0:T(8,128)(2,1)S(1)}, bf16[2,1,1408,512]{3,2,1,0:T(8,128)(2,1)}, u32[]{:S(2)}, u32[]{:S(2)}) collective-permute-start(bf16[2,1,1408,512]{3,2,1,0:T(8,128)(2,1)S(1)} %slice.37.half_ref), channel_id=1, source_target_pairs={{0,2},{1,3},{2,0},{3,1},{4,6},{5,7},{6,4},{7,5},{8,10},{9,11},{10,... | collective-permute-start | bytes 8650760 | tf_op jit(solution)/shard_map/ppermute | solution.py:18
  15.7 13.7 %collective-permute-start.2 = (bf16[2,80,1408]{2,1,0:T(8,128)(2,1)S(1)}, bf16[2,80,1408]{2,1,0:T(8,128)(2,1)S(1)}, u32[]{:S(2)}, u32[]{:S(2)}) collective-permute-start(bf16[2,80,1408]{2,1,0:T(8,128)(2,1)S(1)} %pad_maximum_fusion.refs_0_), channel_id=1, source_target_pairs={{8,0},{12,4},{16,8},{20,12},{24,16},{28,20},{9,1},{13,5},{17,9},{2... | collective-permute-start | bytes 1351688 | tf_op jit(solution)/shard_map/ppermute | solution.py:24
  17.0 13.7 %collective-permute-start.7 = (bf16[2,80,1408]{2,1,0:T(8,128)(2,1)S(1)}, bf16[2,80,1408]{2,1,0:T(8,128)(2,1)S(1)}, u32[]{:S(2)}, u32[]{:S(2)}) collective-permute-start(bf16[2,80,1408]{2,1,0:T(8,128)(2,1)S(1)} %pad_maximum_fusion.refs_0_), channel_id=1, source_target_pairs={{0,1},{1,0},{2,3},{3,2},{4,5},{5,4},{6,7},{7,6},{8,9},{9,8},{10,11... | collective-permute-start | bytes 1351688 | tf_op jit(solution)/shard_map/ppermute | solution.py:18
  30.8 12.2 %collective-permute-start.9 = (bf16[2,80,1408]{2,1,0:T(8,128)(2,1)S(1)}, bf16[2,80,1408]{2,1,0:T(8,128)(2,1)S(1)}, u32[]{:S(2)}, u32[]{:S(2)}) collective-permute-start(bf16[2,80,1408]{2,1,0:T(8,128)(2,1)S(1)} %collective-permute-done.2.refs_2_), channel_id=1, source_target_pairs={{0,1},{1,0},{2,3},{3,2},{4,5},{5,4},{6,7},{7,6},{8,9},{9,8},{10,11... | collective-permute-start | bytes 1351688 | tf_op jit(solution)/shard_map/ppermute | solution.py:18
  64.9 13.4 %collective-permute-start.14 = (bf16[2,320,512]{2,1,0:T(8,128)(2,1)}, bf16[2,320,512]{2,1,0:T(8,128)(2,1)S(1)}, u32[]{:S(2)}, u32[]{:S(2)}) collective-permute-start(bf16[2,320,512]{2,1,0:T(8,128)(2,1)} %get-tuple-element.18), channel_id=1, source_target_pairs={{0,1},{1,0},{2,3},{3,2},{4,5},{5,4},{6,7},{7,6},{8,9},{9,8},{10,11... | collective-permute-start | bytes 1966088 | tf_op jit(solution)/shard_map/ppermute | solution.py:18
  82.1 69.1 %all-to-all-start = ((bf16[8,320,512]{2,1,0:T(8,128)(2,1)}), bf16[8,320,512]{2,1,0:T(8,128)(2,1)S(1)}, u32[]{:S(2)}, u32[]{:S(2)}) async-start(bf16[8,320,512]{2,1,0:T(8,128)(2,1)} %assemble.3), calls=%async_computation | async-start | bytes 5242880 | tf_op jit(solution)/shard_map/all_to_all | solution.py:420
  88.2 17.8 %collective-permute-start.17 = (bf16[2,320,512]{2,1,0:T(8,128)(2,1)}, bf16[2,320,512]{2,1,0:T(8,128)(2,1)S(1)}, u32[]{:S(2)}, u32[]{:S(2)}) collective-permute-start(bf16[2,320,512]{2,1,0:T(8,128)(2,1)} %get-tuple-element.22), channel_id=1, source_target_pairs={{0,2},{1,3},{2,0},{3,1},{4,6},{5,7},{6,4},{7,5},{8,10},{9,11},{10,... | collective-permute-start | bytes 1966088 | tf_op jit(solution)/shard_map/ppermute | solution.py:18
  89.7 57.1 %collective-permute-start.19 = (bf16[2,320,512]{2,1,0:T(8,128)(2,1)}, bf16[2,320,512]{2,1,0:T(8,128)(2,1)S(1)}, u32[]{:S(2)}, u32[]{:S(2)}) collective-permute-start(bf16[2,320,512]{2,1,0:T(8,128)(2,1)} %get-tuple-element.21.refs_4_), channel_id=1, source_target_pairs={{0,3},{1,2},{2,1},{3,0},{4,7},{5,6},{6,5},{7,4},{8,11},{9,10},{10,... | collective-permute-start | bytes 1966088 | tf_op jit(solution)/shard_map/ppermute | solution.py:18
  95.4 38.8 %collective-permute-start.21 = (bf16[2,320,512]{2,1,0:T(8,128)(2,1)}, bf16[2,320,512]{2,1,0:T(8,128)(2,1)}, u32[]{:S(2)}, u32[]{:S(2)}) collective-permute-start(bf16[2,320,512]{2,1,0:T(8,128)(2,1)} %get-tuple-element.27), channel_id=1, source_target_pairs={{0,2},{1,3},{2,0},{3,1},{4,6},{5,7},{6,4},{7,5},{8,10},{9,11},{10,... | collective-permute-start | bytes 1966088 | tf_op jit(solution)/shard_map/ppermute | solution.py:18
  96.9 49.9 %collective-permute-start.22 = (bf16[2,320,512]{2,1,0:T(8,128)(2,1)}, bf16[2,320,512]{2,1,0:T(8,128)(2,1)}, u32[]{:S(2)}, u32[]{:S(2)}) collective-permute-start(bf16[2,320,512]{2,1,0:T(8,128)(2,1)} %get-tuple-element.25.refs_4_), channel_id=1, source_target_pairs={{0,3},{1,2},{2,1},{3,0},{4,7},{5,6},{6,5},{7,4},{8,11},{9,10},{10,... | collective-permute-start | bytes 1966088 | tf_op jit(solution)/shard_map/ppermute | solution.py:18
  117.0 29.8 %collective-permute-start.20 = (bf16[2,320,512]{2,1,0:T(8,128)(2,1)}, bf16[2,320,512]{2,1,0:T(8,128)(2,1)S(1)}, u32[]{:S(2)}, u32[]{:S(2)}) collective-permute-start(bf16[2,320,512]{2,1,0:T(8,128)(2,1)} %get-tuple-element.26), channel_id=1, source_target_pairs={{0,1},{1,0},{2,3},{3,2},{4,5},{5,4},{6,7},{7,6},{8,9},{9,8},{10,11... | collective-permute-start | bytes 1966088 | tf_op jit(solution)/shard_map/ppermute | solution.py:18
  117.0 30.7 %collective-permute-start.18 = (bf16[2,320,512]{2,1,0:T(8,128)(2,1)S(1)}, bf16[2,320,512]{2,1,0:T(8,128)(2,1)}, u32[]{:S(2)}, u32[]{:S(2)}) collective-permute-start(bf16[2,320,512]{2,1,0:T(8,128)(2,1)S(1)} %copy-done.21), channel_id=1, source_target_pairs={{0,1},{1,0},{2,3},{3,2},{4,5},{5,4},{6,7},{7,6},{8,9},{9,8},{10,11... | collective-permute-start | bytes 1966088 | tf_op jit(solution)/shard_map/ppermute | solution.py:18
  151.2 66.0 %all-to-all-start.1 = ((bf16[8,320,512]{2,1,0:T(8,128)(2,1)}), bf16[8,320,512]{2,1,0:T(8,128)(2,1)}, u32[]{:S(2)}, u32[]{:S(2)}) async-start(bf16[8,320,512]{2,1,0:T(8,128)(2,1)} %assemble.4), calls=%async_computation.1 | async-start | bytes 5242880 | tf_op jit(solution)/shard_map/all_to_all | solution.py:420
  156.7 62.1 %collective-permute-start.23 = (bf16[8,320,512]{2,1,0:T(8,128)(2,1)S(1)}, bf16[8,320,512]{2,1,0:T(8,128)(2,1)}, u32[]{:S(2)}, u32[]{:S(2)}) collective-permute-start(bf16[8,320,512]{2,1,0:T(8,128)(2,1)S(1)} %all-to-all-done.refs_2_.refs_5_), channel_id=1, source_target_pairs={{0,2},{1,3},{2,0},{3,1},{4,6},{5,7},{6,4},{7,5},{8,10},{9,11},{10,... | collective-permute-start | bytes 7864328 | tf_op jit(solution)/shard_map/ppermute | solution.py:18
  217.2 58.8 %collective-permute-start.29 = (bf16[8,320,512]{2,1,0:T(8,128)(2,1)}, bf16[8,320,512]{2,1,0:T(8,128)(2,1)}, u32[]{:S(2)}, u32[]{:S(2)}) collective-permute-start(bf16[8,320,512]{2,1,0:T(8,128)(2,1)} %all-to-all-done.1.refs_3_.refs_9_), channel_id=1, source_target_pairs={{0,2},{1,3},{2,0},{3,1},{4,6},{5,7},{6,4},{7,5},{8,10},{9,11},{10,... | collective-permute-start | bytes 7864328 | tf_op jit(solution)/shard_map/ppermute | solution.py:18
  221.4 63.2 %all-to-all-start.2 = ((bf16[8,320,512]{2,1,0:T(8,128)(2,1)}), bf16[8,320,512]{2,1,0:T(8,128)(2,1)S(1)}, u32[]{:S(2)}, u32[]{:S(2)}) async-start(bf16[8,320,512]{2,1,0:T(8,128)(2,1)} %assemble.5), calls=%async_computation.2 | async-start | bytes 5242880 | tf_op jit(solution)/shard_map/all_to_all | solution.py:420
  225.4 63.3 %collective-permute-start.28 = (bf16[8,320,512]{2,1,0:T(8,128)(2,1)}, bf16[8,320,512]{2,1,0:T(8,128)(2,1)}, u32[]{:S(2)}, u32[]{:S(2)}) collective-permute-start(bf16[8,320,512]{2,1,0:T(8,128)(2,1)} %all-to-all-done.1.refs_3_.refs_9_), channel_id=1, source_target_pairs={{0,1},{1,0},{2,3},{3,2},{4,5},{5,4},{6,7},{7,6},{8,9},{9,8},{10,11... | collective-permute-start | bytes 7864328 | tf_op jit(solution)/shard_map/ppermute | solution.py:18
  225.5 63.2 %collective-permute-start.26 = (bf16[8,320,512]{2,1,0:T(8,128)(2,1)}, bf16[8,320,512]{2,1,0:T(8,128)(2,1)}, u32[]{:S(2)}, u32[]{:S(2)}) collective-permute-start(bf16[8,320,512]{2,1,0:T(8,128)(2,1)} %copy-done.1), channel_id=1, source_target_pairs={{0,1},{1,0},{2,3},{3,2},{4,5},{5,4},{6,7},{7,6},{8,9},{9,8},{10,11... | collective-permute-start | bytes 7864328 | tf_op jit(solution)/shard_map/ppermute | solution.py:18
  276.1 12.6 %collective-permute-start.30 = (bf16[8,320,512]{2,1,0:T(8,128)(2,1)}, bf16[8,320,512]{2,1,0:T(8,128)(2,1)}, u32[]{:S(2)}, u32[]{:S(2)}) collective-permute-start(bf16[8,320,512]{2,1,0:T(8,128)(2,1)} %collective-permute-done.29.refs_11_), channel_id=1, source_target_pairs={{0,1},{1,0},{2,3},{3,2},{4,5},{5,4},{6,7},{7,6},{8,9},{9,8},{10,11... | collective-permute-start | bytes 7864328 | tf_op jit(solution)/shard_map/ppermute | solution.py:18
  276.1 12.6 %collective-permute-start.27 = (bf16[8,320,512]{2,1,0:T(8,128)(2,1)}, bf16[8,320,512]{2,1,0:T(8,128)(2,1)}, u32[]{:S(2)}, u32[]{:S(2)}) collective-permute-start(bf16[8,320,512]{2,1,0:T(8,128)(2,1)} %collective-permute-done.23.refs_4_.refs_7_), channel_id=1, source_target_pairs={{0,1},{1,0},{2,3},{3,2},{4,5},{5,4},{6,7},{7,6},{8,9},{9,8},{10,11... | collective-permute-start | bytes 7864328 | tf_op jit(solution)/shard_map/ppermute | solution.py:18
  286.1 43.7 %collective-permute-start.25 = (bf16[6,320,512]{2,1,0:T(8,128)(2,1)}, bf16[6,320,512]{2,1,0:T(8,128)(2,1)}, u32[]{:S(2)}, u32[]{:S(2)}) collective-permute-start(bf16[6,320,512]{2,1,0:T(8,128)(2,1)} %slice.38.refs_5_), channel_id=1, source_target_pairs={{0,2},{1,3},{2,0},{3,1},{4,6},{5,7},{6,4},{7,5},{8,10},{9,11},{10,... | collective-permute-start | bytes 5898248 | tf_op jit(solution)/shard_map/ppermute | solution.py:18
  288.7 46.2 %collective-permute-start.24 = (bf16[6,320,512]{2,1,0:T(8,128)(2,1)}, bf16[6,320,512]{2,1,0:T(8,128)(2,1)}, u32[]{:S(2)}, u32[]{:S(2)}) collective-permute-start(bf16[6,320,512]{2,1,0:T(8,128)(2,1)} %slice.38.refs_5_), channel_id=1, source_target_pairs={{0,1},{1,0},{2,3},{3,2},{4,5},{5,4},{6,7},{7,6},{8,9},{9,8},{10,11... | collective-permute-start | bytes 5898248 | tf_op jit(solution)/shard_map/ppermute | solution.py:18
  333.5 17.2 %collective-permute-start.33 = (bf16[2,320,512]{2,1,0:T(8,128)(2,1)S(1)}, bf16[2,320,512]{2,1,0:T(8,128)(2,1)S(1)}, u32[]{:S(2)}, u32[]{:S(2)}) collective-permute-start(bf16[2,320,512]{2,1,0:T(8,128)(2,1)S(1)} %slice.39.refs_9_), channel_id=1, source_target_pairs={{0,2},{1,3},{2,0},{3,1},{4,6},{5,7},{6,4},{7,5},{8,10},{9,11},{10,... | collective-permute-start | bytes 1966088 | tf_op jit(solution)/shard_map/ppermute | solution.py:18
  334.5 18.9 %collective-permute-start.32 = (bf16[2,320,512]{2,1,0:T(8,128)(2,1)S(1)}, bf16[2,320,512]{2,1,0:T(8,128)(2,1)}, u32[]{:S(2)}, u32[]{:S(2)}) collective-permute-start(bf16[2,320,512]{2,1,0:T(8,128)(2,1)S(1)} %slice.39.refs_9_), channel_id=1, source_target_pairs={{0,1},{1,0},{2,3},{3,2},{4,5},{5,4},{6,7},{7,6},{8,9},{9,8},{10,11... | collective-permute-start | bytes 1966088 | tf_op jit(solution)/shard_map/ppermute | solution.py:18
  (37 other events, 471.3 us)

commit v4 on v3

--- a/solution.py
+++ b/solution.py
@@ -156,22 +156,20 @@
     )(pair_index.reshape(1), *pieces, *after)
 
 
-def gate_kernel(value_ref, after_ref, out_ref):
-    out_ref[...] = value_ref[...]
+def gate_kernel(*refs):
+    del refs
 
 
 def gate(value, after):
-    parts = 2 if value.shape[0] % 2 == 0 else 1
-    spec = pl.BlockSpec((value.shape[0] // parts, *value.shape[1:]), lambda t: (t, 0, 0))
     return pl.pallas_call(
         gate_kernel,
-        grid=(parts,),
-        in_specs=[spec, ANY],
-        out_specs=spec,
+        in_specs=[ANY] * (1 + len(after)),
+        out_specs=ANY,
         out_shape=jax.ShapeDtypeStruct(value.shape, value.dtype),
-        cost_estimate=pl.CostEstimate(flops=0, bytes_accessed=4 * value.size, transcendentals=0),
+        input_output_aliases={0: 0},
+        cost_estimate=pl.CostEstimate(flops=0, bytes_accessed=0, transcendentals=0),
         name="gate",
-    )(value, after)
+    )(value, *after)
 
 
 GROUP = 2
@@ -388,7 +386,7 @@
 
     def share(blocks, after=None):
         if after is not None and len(blocks) > 1:
-            blocks = blocks[:-1] + [gate(blocks[-1], after)]
+            blocks = blocks[:-1] + [gate(blocks[-1], [after])]
         return [b for block in blocks for b in (block, swap(block, 1))]
 
     first = []
@@ -409,14 +407,15 @@
     final = occ_width - 1
     middle = aux_count * 3 // 4
     for orbital in range(occ_width):
-        after = [pieces[-1] for pieces in parts[1:]] if orbital == 1 else []
-        if orbital == 0 and final:
-            after.append(parts[0][-1])
+        early = [parts[0][-1]] if orbital == 0 and final else []
+        sent = assemble(moved[orbital], pair_index, early)
+        after = []
+        if 0 < orbital < final:
+            after += moved[orbital + 1][1:]
         if orbital > 1:
             after.append(far[orbital - 2][-1])
-        if 0 < orbital < occ_width - 1:
-            after += moved[orbital + 1][1:]
-        sent = assemble(moved[orbital], pair_index, after)
+        if after:
+            sent = gate(sent, after)
         local = lax.all_to_all(sent, "aux", split_axis=0, concat_axis=0, tiled=True)
         locals_.append(local)
         if orbital < occ_width - 1:

time: 374 us -> 366 us (0.979)
  Pallas kernels: 108 us -> 104 us
    pallas_call x2 -> x4, Pallas kernels: 4.41 us -> 0.01 us  [gate(): pl.pallas_call(gate_kernel, in_specs=[ANY] * (1 + len(after)), out_specs=...]
  transfers between devices with their start and end apart: 38 -> 38, of which waited for: 17 -> 19; matrix products, arithmetic and copies ran while one was open for 3% -> 3% of each run, Pallas kernels for 24% -> 23%
where the time goes in v4:
time: 366 us; the launch traced here: 365 us
  waiting for transfers between devices  193 us (53%)
  Pallas kernels  104 us (28%)
  starting transfers between devices  48.1 us (13%)
  local copies, waits for them, and re-layouts  14.5 us (4%)
    ppermute x29, waiting for transfers between devices, swap(): return lax.ppermute(value, axis, pairs)  110 us
    all_to_all x3, waiting for transfers between devices, per_device(): local = lax.all_to_all(sent, 'aux', split_axis=0, concat_axis=0, tiled=True)  62.5 us
    pallas_call x3, Pallas kernels, add_density(): pl.pallas_call(functools.partial(density_kernel, plan), grid_spec=pltpu.P...  59.6 us
    pallas_call x6, Pallas kernels, transform(): pl.pallas_call(functools.partial(transform_kernel, width, distances), gri...  31.4 us
    ppermute x6, waiting for transfers between devices, along(): return lax.ppermute(value, 'aux', pairs)  21.1 us
    ppermute x6, starting transfers between devices, along(): return lax.ppermute(value, 'aux', pairs)  17.8 us
    ppermute x29, starting transfers between devices, swap(): return lax.ppermute(value, axis, pairs)  15.4 us
    all_to_all x3, starting transfers between devices, per_device(): local = lax.all_to_all(sent, 'aux', split_axis=0, concat_axis=0, tiled=True)  14.9 us
  transfers between devices with their start and end apart: 38, of which 19 were waited for; matrix products, arithmetic and copies ran while one was open for 3% of the time, Pallas kernels for 23%

profile of v4, /device:TPU:0, one launch (start us, length us, event | category | flops | bytes accessed | tf_op | source)
XLA Modules:
  0.0 365.3 jit_solution(3633235818364937030)
XLA Ops:
  6.7 5.5 %collective-permute-done = bf16[80,1408]{1,0:T(8,128)(2,1)S(1)} collective-permute-done((bf16[80,1408]{1,0:T(8,128)(2,1)S(1)}, bf16[80,1408]{1,0:T(8,128)(2,1)S(1)}, u32[]{:S(2)}, u32[]{:S(2)}) %collective-permute-start) | collective-permute-done | bytes 225312 | tf_op jit(solution)/shard_map/ppermute | solution.py:18
  17.1 7.1 %collective-permute-done.1.refs_1_ = bf16[2,80,1408]{2,1,0:T(8,128)(2,1)S(1)} collective-permute-done((bf16[2,80,1408]{2,1,0:T(8,128)(2,1)S(1)}, bf16[2,80,1408]{2,1,0:T(8,128)(2,1)S(1)}, u32[]{:S(2)}, u32[]{:S(2)}) %collective-permute-start.1) | collective-permute-done | bytes 450592 | tf_op jit(solution)/shard_map/ppermute | solution.py:24
  24.2 5.2 %collective-permute-start.3 = (bf16[2,80,1408]{2,1,0:T(8,128)(2,1)S(1)}, bf16[2,80,1408]{2,1,0:T(8,128)(2,1)}, u32[]{:S(2)}, u32[]{:S(2)}) collective-permute-start(bf16[2,80,1408]{2,1,0:T(8,128)(2,1)S(1)} %collective-permute-done.1.refs_1_), channel_id=1, source_target_pairs={{0,8},{4,12},{8,16},{12,20},{16,24},{20,28},{1,9},{5,13},{9,17},{1... | collective-permute-start | bytes 1351688 | tf_op jit(solution)/shard_map/ppermute | solution.py:24
  31.3 4.9 %collective-permute-done.3.refs_3_ = bf16[2,80,1408]{2,1,0:T(8,128)(2,1)} collective-permute-done((bf16[2,80,1408]{2,1,0:T(8,128)(2,1)S(1)}, bf16[2,80,1408]{2,1,0:T(8,128)(2,1)}, u32[]{:S(2)}, u32[]{:S(2)}) %collective-permute-start.3) | collective-permute-done | bytes 450592 | tf_op jit(solution)/shard_map/ppermute | solution.py:24
  36.3 5.3 %collective-permute-start.5 = (bf16[2,80,1408]{2,1,0:T(8,128)(2,1)}, bf16[2,80,1408]{2,1,0:T(8,128)(2,1)}, u32[]{:S(2)}, u32[]{:S(2)}) collective-permute-start(bf16[2,80,1408]{2,1,0:T(8,128)(2,1)} %collective-permute-done.3.refs_3_), channel_id=1, source_target_pairs={{0,8},{4,12},{8,16},{12,20},{16,24},{20,28},{1,9},{5,13},{9,17},{1... | collective-permute-start | bytes 1351688 | tf_op jit(solution)/shard_map/ppermute | solution.py:24
  47.8 4.9 %collective-permute-done.6.refs_6_ = bf16[2,80,1408]{2,1,0:T(8,128)(2,1)} collective-permute-done((bf16[2,80,1408]{2,1,0:T(8,128)(2,1)}, bf16[2,80,1408]{2,1,0:T(8,128)(2,1)}, u32[]{:S(2)}, u32[]{:S(2)}) %collective-permute-start.6) | collective-permute-done | bytes 450592 | tf_op jit(solution)/shard_map/ppermute | solution.py:24
  54.9 4.9 %place.1 = bf16[4,2,2,80,1408]{4,3,2,1,0:T(8,128)(2,1)} custom-call(s32[3]{0:T(128)} %pad_add_fusion.index_ref, bf16[2,80,1408]{2,1,0:T(8,128)(2,1)} %copy-done.8, bf16[2,80,1408]{2,1,0:T(8,128)(2,1)} %copy-done.12, bf16[2,80,1408]{2,1,0:T(8,128)(2,1)} %copy-done.13, bf16[2,80,1408]{2,1,0:T(8,128)(2,1)} %collective-permute-done.3.refs_3_, ...), custom_call_target="tpu_custom_call" | custom-call | bytes 7208960 | tf_op jit(solution)/shard_map/place/pallas_call | solution.py:58
  59.8 5.1 %transform.6 = (bf16[2,320,512]{2,1,0:T(8,128)(2,1)}, bf16[2,320,512]{2,1,0:T(8,128)(2,1)}) custom-call(s32[1]{0:T(128)} %bitcast.3.index_ref, bf16[1280,1408]{1,0:T(8,128)(2,1)} %bitcast.25, bf16[2,1,1408,512]{3,2,1,0:T(8,128)(2,1)} %copy-done.3), custom_call_target="tpu_custom_call" | custom-call | flops 1845493760 | bytes 5996544 | tf_op jit(solution)/shard_map/transform/pallas_call | solution.py:101
  67.7 5.1 %transform.7 = (bf16[2,320,512]{2,1,0:T(8,128)(2,1)}, bf16[2,320,512]{2,1,0:T(8,128)(2,1)}) custom-call(s32[1]{0:T(128)} %bitcast.3.index_ref, bf16[1280,1408]{1,0:T(8,128)(2,1)} %bitcast.26, bf16[2,1,1408,512]{3,2,1,0:T(8,128)(2,1)} %collective-permute-done.15.half_ref), custom_call_target="tpu_custom_call" | custom-call | flops 1845493760 | bytes 5996544 | tf_op jit(solution)/shard_map/transform/pallas_call | solution.py:101
  72.8 5.6 %transform.8 = (bf16[2,320,512]{2,1,0:T(8,128)(2,1)}, bf16[2,320,512]{2,1,0:T(8,128)(2,1)}) custom-call(s32[1]{0:T(128)} %bitcast.3.index_ref, bf16[1280,1408]{1,0:T(8,128)(2,1)} %bitcast.27, bf16[2,3,1408,512]{3,2,1,0:T(8,128)(2,1)} %bitcast.21), custom_call_target="tpu_custom_call" | custom-call | flops 1845493760 | bytes 7798784 | tf_op jit(solution)/shard_map/transform/pallas_call | solution.py:101
  82.2 6.1 %all-to-all-start = ((bf16[8,320,512]{2,1,0:T(8,128)(2,1)}), bf16[8,320,512]{2,1,0:T(8,128)(2,1)S(1)}, u32[]{:S(2)}, u32[]{:S(2)}) async-start(bf16[8,320,512]{2,1,0:T(8,128)(2,1)} %assemble.3), calls=%async_computation | async-start | bytes 5242880 | tf_op jit(solution)/shard_map/all_to_all | solution.py:419
  89.8 5.6 %transform.11 = (bf16[2,320,512]{2,1,0:T(8,128)(2,1)}, bf16[2,320,512]{2,1,0:T(8,128)(2,1)}) custom-call(s32[1]{0:T(128)} %bitcast.3.index_ref, bf16[1280,1408]{1,0:T(8,128)(2,1)} %bitcast.28, bf16[2,3,1408,512]{3,2,1,0:T(8,128)(2,1)} %bitcast.22), custom_call_target="tpu_custom_call" | custom-call | flops 1845493760 | bytes 7798784 | tf_op jit(solution)/shard_map/transform/pallas_call | solution.py:101
  97.3 8.7 %collective-permute-done.17.refs_0_.refs_2_ = bf16[2,320,512]{2,1,0:T(8,128)(2,1)S(1)} collective-permute-done((bf16[2,320,512]{2,1,0:T(8,128)(2,1)}, bf16[2,320,512]{2,1,0:T(8,128)(2,1)S(1)}, u32[]{:S(2)}, u32[]{:S(2)}) %collective-permute-start.17) | collective-permute-done | bytes 655392 | tf_op jit(solution)/shard_map/ppermute | solution.py:18
  106.9 5.0 %transform.9 = (bf16[2,320,512]{2,1,0:T(8,128)(2,1)}, bf16[2,320,512]{2,1,0:T(8,128)(2,1)}) custom-call(s32[1]{0:T(128)} %bitcast.3.index_ref, bf16[1280,1408]{1,0:T(8,128)(2,1)} %bitcast.29, bf16[2,3,1408,512]{3,2,1,0:T(8,128)(2,1)} %bitcast.23, bf16[2,320,512]{2,1,0:T(8,128)(2,1)} %copy-done.4), custom_call_target="tpu_custom_call" | custom-call | flops 1845493760 | bytes 5996544 | tf_op jit(solution)/shard_map/transform/pallas_call | solution.py:101
  112.0 5.1 %transform.10 = (bf16[2,320,512]{2,1,0:T(8,128)(2,1)}, bf16[2,320,512]{2,1,0:T(8,128)(2,1)}) custom-call(s32[1]{0:T(128)} %bitcast.3.index_ref, bf16[1280,1408]{1,0:T(8,128)(2,1)} %bitcast.30, bf16[2,3,1408,512]{3,2,1,0:T(8,128)(2,1)} %bitcast.24, bf16[2,320,512]{2,1,0:T(8,128)(2,1)} %get-tuple-element.23.refs_0_), custom_call_target="tpu_custom_call" | custom-call | flops 1845493760 | bytes 5996544 | tf_op jit(solution)/shard_map/transform/pallas_call | solution.py:101
  121.8 12.4 %collective-permute-done.21.refs_2_ = bf16[2,320,512]{2,1,0:T(8,128)(2,1)} collective-permute-done((bf16[2,320,512]{2,1,0:T(8,128)(2,1)}, bf16[2,320,512]{2,1,0:T(8,128)(2,1)}, u32[]{:S(2)}, u32[]{:S(2)}) %collective-permute-start.21) | collective-permute-done | bytes 655392 | tf_op jit(solution)/shard_map/ppermute | solution.py:18
  134.2 12.6 %collective-permute-done.22.refs_3_ = bf16[2,320,512]{2,1,0:T(8,128)(2,1)} collective-permute-done((bf16[2,320,512]{2,1,0:T(8,128)(2,1)}, bf16[2,320,512]{2,1,0:T(8,128)(2,1)}, u32[]{:S(2)}, u32[]{:S(2)}) %collective-permute-start.22) | collective-permute-done | bytes 655392 | tf_op jit(solution)/shard_map/ppermute | solution.py:18
  148.4 4.8 %all-to-all-start.1 = ((bf16[8,320,512]{2,1,0:T(8,128)(2,1)}), bf16[8,320,512]{2,1,0:T(8,128)(2,1)}, u32[]{:S(2)}, u32[]{:S(2)}) async-start(bf16[8,320,512]{2,1,0:T(8,128)(2,1)} %gate.4), calls=%async_computation.1 | async-start | bytes 5242880 | tf_op jit(solution)/shard_map/all_to_all | solution.py:419
  154.7 59.0 %all-to-all-done.1.refs_3_.refs_9_ = bf16[8,320,512]{2,1,0:T(8,128)(2,1)} async-done(((bf16[8,320,512]{2,1,0:T(8,128)(2,1)}), bf16[8,320,512]{2,1,0:T(8,128)(2,1)}, u32[]{:S(2)}, u32[]{:S(2)}) %all-to-all-start.1) | async-done | bytes 2621472 | tf_op jit(solution)/shard_map/all_to_all | solution.py:419
  222.5 50.0 %collective-permute-done.29.refs_11_ = bf16[8,320,512]{2,1,0:T(8,128)(2,1)} collective-permute-done((bf16[8,320,512]{2,1,0:T(8,128)(2,1)}, bf16[8,320,512]{2,1,0:T(8,128)(2,1)}, u32[]{:S(2)}, u32[]{:S(2)}) %collective-permute-start.29) | collective-permute-done | bytes 2621472 | tf_op jit(solution)/shard_map/ppermute | solution.py:18
  285.1 31.7 %density.2.refs_1_.refs_14_ = bf16[960,4096]{1,0:T(8,128)(2,1)} custom-call(s32[2]{0:T(128)} %get-tuple-element.29.distance_ref, f32[960,1]{1,0:T(8,128)} %sub.71.refs_0_, f32[1,1280]{1,0:T(1,128)} %reshape.65.refs_1_, bf16[8,320,512]{2,1,0:T(8,128)(2,1)} %copy-done.1, bf16[8,320,512]{2,1,0:T(8,128)(2,1)} %all-to-all-done.1.refs_3_.refs_9_, ...), custom_call_target="tpu_custom_call" | custom-call | flops 20132659200 | bytes 26214400 | tf_op jit(solution)/shard_map/density/pallas_call | solution.py:336
  316.8 9.5 %collective-permute-done.25.refs_0_ = bf16[6,320,512]{2,1,0:T(8,128)(2,1)} collective-permute-done((bf16[6,320,512]{2,1,0:T(8,128)(2,1)}, bf16[6,320,512]{2,1,0:T(8,128)(2,1)}, u32[]{:S(2)}, u32[]{:S(2)}) %collective-permute-start.25) | collective-permute-done | bytes 1966112 | tf_op jit(solution)/shard_map/ppermute | solution.py:18
  331.8 11.5 %integrals.1.refs_1_.refs_13_ = f32[960,640]{1,0:T(8,128)} custom-call(s32[2]{0:T(128)} %get-tuple-element.29.distance_ref, f32[960,1]{1,0:T(8,128)} %sub.71.refs_0_, f32[1,640]{1,0:T(1,128)} %reshape.61.refs_1_, bf16[8,320,512]{2,1,0:T(8,128)(2,1)} %copy-done.1, bf16[8,320,512]{2,1,0:T(8,128)(2,1)} %all-to-all-done.1.refs_3_.refs_9_, ...), custom_call_target="tpu_custom_call" | custom-call | flops 3774873600 | bytes 13598720 | tf_op jit(solution)/shard_map/integrals/pallas_call | solution.py:336
  348.7 16.4 %density.3 = bf16[960,4096]{1,0:T(8,128)(2,1)} custom-call(s32[2]{0:T(128)} %get-tuple-element.29.distance_ref, f32[960,1]{1,0:T(8,128)} %sub.71.refs_0_, f32[1,640]{1,0:T(1,128)} %reshape.61.refs_1_, bf16[8,320,512]{2,1,0:T(8,128)(2,1)} %copy-done.1, bf16[8,320,512]{2,1,0:T(8,128)(2,1)} %all-to-all-done.1.refs_3_.refs_9_, bf16[8,320,512]{2,1,0:T(8,128)(2,1)} %copy-done, ...), custom_call_target="tpu_custom_call" | custom-call | flops 6291456000 | bytes 22937600 | tf_op jit(solution)/shard_map/density/pallas_call | solution.py:336
  (128 shorter events, 71.6 us)
Async XLA Ops:
  2.1 65.6 %collective-permute-start.15 = (bf16[2,1,1408,512]{3,2,1,0:T(8,128)(2,1)S(1)}, bf16[2,1,1408,512]{3,2,1,0:T(8,128)(2,1)}, u32[]{:S(2)}, u32[]{:S(2)}) collective-permute-start(bf16[2,1,1408,512]{3,2,1,0:T(8,128)(2,1)S(1)} %slice.37.half_ref), channel_id=1, source_target_pairs={{0,2},{1,3},{2,0},{3,1},{4,6},{5,7},{6,4},{7,5},{8,10},{9,11},{10,... | collective-permute-start | bytes 8650760 | tf_op jit(solution)/shard_map/ppermute | solution.py:18
  15.7 13.7 %collective-permute-start.2 = (bf16[2,80,1408]{2,1,0:T(8,128)(2,1)S(1)}, bf16[2,80,1408]{2,1,0:T(8,128)(2,1)S(1)}, u32[]{:S(2)}, u32[]{:S(2)}) collective-permute-start(bf16[2,80,1408]{2,1,0:T(8,128)(2,1)S(1)} %pad_maximum_fusion.refs_0_), channel_id=1, source_target_pairs={{8,0},{12,4},{16,8},{20,12},{24,16},{28,20},{9,1},{13,5},{17,9},{2... | collective-permute-start | bytes 1351688 | tf_op jit(solution)/shard_map/ppermute | solution.py:24
  17.0 13.7 %collective-permute-start.7 = (bf16[2,80,1408]{2,1,0:T(8,128)(2,1)S(1)}, bf16[2,80,1408]{2,1,0:T(8,128)(2,1)S(1)}, u32[]{:S(2)}, u32[]{:S(2)}) collective-permute-start(bf16[2,80,1408]{2,1,0:T(8,128)(2,1)S(1)} %pad_maximum_fusion.refs_0_), channel_id=1, source_target_pairs={{0,1},{1,0},{2,3},{3,2},{4,5},{5,4},{6,7},{7,6},{8,9},{9,8},{10,11... | collective-permute-start | bytes 1351688 | tf_op jit(solution)/shard_map/ppermute | solution.py:18
  30.7 12.2 %collective-permute-start.8 = (bf16[2,80,1408]{2,1,0:T(8,128)(2,1)S(1)}, bf16[2,80,1408]{2,1,0:T(8,128)(2,1)S(1)}, u32[]{:S(2)}, u32[]{:S(2)}) collective-permute-start(bf16[2,80,1408]{2,1,0:T(8,128)(2,1)S(1)} %collective-permute-done.1.refs_1_), channel_id=1, source_target_pairs={{0,1},{1,0},{2,3},{3,2},{4,5},{5,4},{6,7},{7,6},{8,9},{9,8},{10,11... | collective-permute-start | bytes 1351688 | tf_op jit(solution)/shard_map/ppermute | solution.py:18
  30.8 12.2 %collective-permute-start.9 = (bf16[2,80,1408]{2,1,0:T(8,128)(2,1)S(1)}, bf16[2,80,1408]{2,1,0:T(8,128)(2,1)S(1)}, u32[]{:S(2)}, u32[]{:S(2)}) collective-permute-start(bf16[2,80,1408]{2,1,0:T(8,128)(2,1)S(1)} %collective-permute-done.2.refs_2_), channel_id=1, source_target_pairs={{0,1},{1,0},{2,3},{3,2},{4,5},{5,4},{6,7},{7,6},{8,9},{9,8},{10,11... | collective-permute-start | bytes 1351688 | tf_op jit(solution)/shard_map/ppermute | solution.py:18
  64.9 13.5 %collective-permute-start.14 = (bf16[2,320,512]{2,1,0:T(8,128)(2,1)}, bf16[2,320,512]{2,1,0:T(8,128)(2,1)S(1)}, u32[]{:S(2)}, u32[]{:S(2)}) collective-permute-start(bf16[2,320,512]{2,1,0:T(8,128)(2,1)} %get-tuple-element.18), channel_id=1, source_target_pairs={{0,1},{1,0},{2,3},{3,2},{4,5},{5,4},{6,7},{7,6},{8,9},{9,8},{10,11... | collective-permute-start | bytes 1966088 | tf_op jit(solution)/shard_map/ppermute | solution.py:18
  82.2 66.2 %all-to-all-start = ((bf16[8,320,512]{2,1,0:T(8,128)(2,1)}), bf16[8,320,512]{2,1,0:T(8,128)(2,1)S(1)}, u32[]{:S(2)}, u32[]{:S(2)}) async-start(bf16[8,320,512]{2,1,0:T(8,128)(2,1)} %assemble.3), calls=%async_computation | async-start | bytes 5242880 | tf_op jit(solution)/shard_map/all_to_all | solution.py:419
  88.3 17.8 %collective-permute-start.17 = (bf16[2,320,512]{2,1,0:T(8,128)(2,1)}, bf16[2,320,512]{2,1,0:T(8,128)(2,1)S(1)}, u32[]{:S(2)}, u32[]{:S(2)}) collective-permute-start(bf16[2,320,512]{2,1,0:T(8,128)(2,1)} %get-tuple-element.22), channel_id=1, source_target_pairs={{0,2},{1,3},{2,0},{3,1},{4,6},{5,7},{6,4},{7,5},{8,10},{9,11},{10,... | collective-permute-start | bytes 1966088 | tf_op jit(solution)/shard_map/ppermute | solution.py:18
  89.8 29.4 %collective-permute-start.19 = (bf16[2,320,512]{2,1,0:T(8,128)(2,1)}, bf16[2,320,512]{2,1,0:T(8,128)(2,1)}, u32[]{:S(2)}, u32[]{:S(2)}) collective-permute-start(bf16[2,320,512]{2,1,0:T(8,128)(2,1)} %get-tuple-element.21.refs_4_), channel_id=1, source_target_pairs={{0,3},{1,2},{2,1},{3,0},{4,7},{5,6},{6,5},{7,4},{8,11},{9,10},{10,... | collective-permute-start | bytes 1966088 | tf_op jit(solution)/shard_map/ppermute | solution.py:18
  95.4 38.8 %collective-permute-start.21 = (bf16[2,320,512]{2,1,0:T(8,128)(2,1)}, bf16[2,320,512]{2,1,0:T(8,128)(2,1)}, u32[]{:S(2)}, u32[]{:S(2)}) collective-permute-start(bf16[2,320,512]{2,1,0:T(8,128)(2,1)} %get-tuple-element.26), channel_id=1, source_target_pairs={{0,2},{1,3},{2,0},{3,1},{4,6},{5,7},{6,4},{7,5},{8,10},{9,11},{10,... | collective-permute-start | bytes 1966088 | tf_op jit(solution)/shard_map/ppermute | solution.py:18
  96.9 49.9 %collective-permute-start.22 = (bf16[2,320,512]{2,1,0:T(8,128)(2,1)}, bf16[2,320,512]{2,1,0:T(8,128)(2,1)}, u32[]{:S(2)}, u32[]{:S(2)}) collective-permute-start(bf16[2,320,512]{2,1,0:T(8,128)(2,1)} %get-tuple-element.27), channel_id=1, source_target_pairs={{0,3},{1,2},{2,1},{3,0},{4,7},{5,6},{6,5},{7,4},{8,11},{9,10},{10,... | collective-permute-start | bytes 1966088 | tf_op jit(solution)/shard_map/ppermute | solution.py:18
  117.0 29.8 %collective-permute-start.20 = (bf16[2,320,512]{2,1,0:T(8,128)(2,1)}, bf16[2,320,512]{2,1,0:T(8,128)(2,1)S(1)}, u32[]{:S(2)}, u32[]{:S(2)}) collective-permute-start(bf16[2,320,512]{2,1,0:T(8,128)(2,1)} %get-tuple-element.25), channel_id=1, source_target_pairs={{0,1},{1,0},{2,3},{3,2},{4,5},{5,4},{6,7},{7,6},{8,9},{9,8},{10,11... | collective-permute-start | bytes 1966088 | tf_op jit(solution)/shard_map/ppermute | solution.py:18
  148.4 65.3 %all-to-all-start.1 = ((bf16[8,320,512]{2,1,0:T(8,128)(2,1)}), bf16[8,320,512]{2,1,0:T(8,128)(2,1)}, u32[]{:S(2)}, u32[]{:S(2)}) async-start(bf16[8,320,512]{2,1,0:T(8,128)(2,1)} %gate.4), calls=%async_computation.1 | async-start | bytes 5242880 | tf_op jit(solution)/shard_map/all_to_all | solution.py:419
  153.2 64.7 %collective-permute-start.23 = (bf16[8,320,512]{2,1,0:T(8,128)(2,1)S(1)}, bf16[8,320,512]{2,1,0:T(8,128)(2,1)}, u32[]{:S(2)}, u32[]{:S(2)}) collective-permute-start(bf16[8,320,512]{2,1,0:T(8,128)(2,1)S(1)} %all-to-all-done.refs_2_.refs_5_), channel_id=1, source_target_pairs={{0,2},{1,3},{2,0},{3,1},{4,6},{5,7},{6,4},{7,5},{8,10},{9,11},{10,... | collective-permute-start | bytes 7864328 | tf_op jit(solution)/shard_map/ppermute | solution.py:18
  213.7 58.8 %collective-permute-start.29 = (bf16[8,320,512]{2,1,0:T(8,128)(2,1)}, bf16[8,320,512]{2,1,0:T(8,128)(2,1)}, u32[]{:S(2)}, u32[]{:S(2)}) collective-permute-start(bf16[8,320,512]{2,1,0:T(8,128)(2,1)} %all-to-all-done.1.refs_3_.refs_9_), channel_id=1, source_target_pairs={{0,2},{1,3},{2,0},{3,1},{4,6},{5,7},{6,4},{7,5},{8,10},{9,11},{10,... | collective-permute-start | bytes 7864328 | tf_op jit(solution)/shard_map/ppermute | solution.py:18
  218.0 63.2 %all-to-all-start.2 = ((bf16[8,320,512]{2,1,0:T(8,128)(2,1)}), bf16[8,320,512]{2,1,0:T(8,128)(2,1)S(1)}, u32[]{:S(2)}, u32[]{:S(2)}) async-start(bf16[8,320,512]{2,1,0:T(8,128)(2,1)} %gate.5), calls=%async_computation.2 | async-start | bytes 5242880 | tf_op jit(solution)/shard_map/all_to_all | solution.py:419
  221.9 63.2 %collective-permute-start.28 = (bf16[8,320,512]{2,1,0:T(8,128)(2,1)}, bf16[8,320,512]{2,1,0:T(8,128)(2,1)}, u32[]{:S(2)}, u32[]{:S(2)}) collective-permute-start(bf16[8,320,512]{2,1,0:T(8,128)(2,1)} %all-to-all-done.1.refs_3_.refs_9_), channel_id=1, source_target_pairs={{0,1},{1,0},{2,3},{3,2},{4,5},{5,4},{6,7},{7,6},{8,9},{9,8},{10,11... | collective-permute-start | bytes 7864328 | tf_op jit(solution)/shard_map/ppermute | solution.py:18
  222.0 63.1 %collective-permute-start.26 = (bf16[8,320,512]{2,1,0:T(8,128)(2,1)}, bf16[8,320,512]{2,1,0:T(8,128)(2,1)}, u32[]{:S(2)}, u32[]{:S(2)}) collective-permute-start(bf16[8,320,512]{2,1,0:T(8,128)(2,1)} %copy-done.1), channel_id=1, source_target_pairs={{0,1},{1,0},{2,3},{3,2},{4,5},{5,4},{6,7},{7,6},{8,9},{9,8},{10,11... | collective-permute-start | bytes 7864328 | tf_op jit(solution)/shard_map/ppermute | solution.py:18
  272.5 12.6 %collective-permute-start.30 = (bf16[8,320,512]{2,1,0:T(8,128)(2,1)}, bf16[8,320,512]{2,1,0:T(8,128)(2,1)}, u32[]{:S(2)}, u32[]{:S(2)}) collective-permute-start(bf16[8,320,512]{2,1,0:T(8,128)(2,1)} %collective-permute-done.29.refs_11_), channel_id=1, source_target_pairs={{0,1},{1,0},{2,3},{3,2},{4,5},{5,4},{6,7},{7,6},{8,9},{9,8},{10,11... | collective-permute-start | bytes 7864328 | tf_op jit(solution)/shard_map/ppermute | solution.py:18
  272.5 12.6 %collective-permute-start.27 = (bf16[8,320,512]{2,1,0:T(8,128)(2,1)}, bf16[8,320,512]{2,1,0:T(8,128)(2,1)}, u32[]{:S(2)}, u32[]{:S(2)}) collective-permute-start(bf16[8,320,512]{2,1,0:T(8,128)(2,1)} %collective-permute-done.23.refs_1_.refs_7_), channel_id=1, source_target_pairs={{0,1},{1,0},{2,3},{3,2},{4,5},{5,4},{6,7},{7,6},{8,9},{9,8},{10,11... | collective-permute-start | bytes 7864328 | tf_op jit(solution)/shard_map/ppermute | solution.py:18
  282.7 43.7 %collective-permute-start.25 = (bf16[6,320,512]{2,1,0:T(8,128)(2,1)}, bf16[6,320,512]{2,1,0:T(8,128)(2,1)}, u32[]{:S(2)}, u32[]{:S(2)}) collective-permute-start(bf16[6,320,512]{2,1,0:T(8,128)(2,1)} %slice.38.refs_5_), channel_id=1, source_target_pairs={{0,2},{1,3},{2,0},{3,1},{4,6},{5,7},{6,4},{7,5},{8,10},{9,11},{10,... | collective-permute-start | bytes 5898248 | tf_op jit(solution)/shard_map/ppermute | solution.py:18
  285.1 43.8 %collective-permute-start.24 = (bf16[6,320,512]{2,1,0:T(8,128)(2,1)}, bf16[6,320,512]{2,1,0:T(8,128)(2,1)}, u32[]{:S(2)}, u32[]{:S(2)}) collective-permute-start(bf16[6,320,512]{2,1,0:T(8,128)(2,1)} %slice.38.refs_5_), channel_id=1, source_target_pairs={{0,1},{1,0},{2,3},{3,2},{4,5},{5,4},{6,7},{7,6},{8,9},{9,8},{10,11... | collective-permute-start | bytes 5898248 | tf_op jit(solution)/shard_map/ppermute | solution.py:18
  327.5 17.2 %collective-permute-start.33 = (bf16[2,320,512]{2,1,0:T(8,128)(2,1)S(1)}, bf16[2,320,512]{2,1,0:T(8,128)(2,1)S(1)}, u32[]{:S(2)}, u32[]{:S(2)}) collective-permute-start(bf16[2,320,512]{2,1,0:T(8,128)(2,1)S(1)} %slice.39.refs_9_), channel_id=1, source_target_pairs={{0,2},{1,3},{2,0},{3,1},{4,6},{5,7},{6,4},{7,5},{8,10},{9,11},{10,... | collective-permute-start | bytes 1966088 | tf_op jit(solution)/shard_map/ppermute | solution.py:18
  328.7 16.9 %collective-permute-start.32 = (bf16[2,320,512]{2,1,0:T(8,128)(2,1)S(1)}, bf16[2,320,512]{2,1,0:T(8,128)(2,1)}, u32[]{:S(2)}, u32[]{:S(2)}) collective-permute-start(bf16[2,320,512]{2,1,0:T(8,128)(2,1)S(1)} %slice.39.refs_9_), channel_id=1, source_target_pairs={{0,1},{1,0},{2,3},{3,2},{4,5},{5,4},{6,7},{7,6},{8,9},{9,8},{10,11... | collective-permute-start | bytes 1966088 | tf_op jit(solution)/shard_map/ppermute | solution.py:18
  (35 other events, 460.0 us)

commit v5 on v4

--- a/solution.py
+++ b/solution.py
@@ -191,6 +191,9 @@
     start_ref = refs.pop(0) if starts else None
     total_ref = refs.pop(0) if has_total else None
     out_ref = refs.pop(0)
+    if starts:
+        start_buffer, start_sem = refs[-2:]
+        del refs[-2:]
     if ends:
         integrals, amplitudes, remote_ref, sems = refs
     else:
@@ -229,6 +232,11 @@
                             def _():
                                 copy_of(ref, first, orbital * steps + position, t).start()
 
+    if starts:
+        @pl.when(step == 0)
+        def _():
+            pltpu.make_async_copy(start_ref, start_buffer, start_sem).start()
+
     def wait_for(t):
         for number in range(len(held_refs) * steps):
             copy_of(held_refs[0][0][2][0], t, number, t).wait()
@@ -252,7 +260,11 @@
 
         @pl.when(step == 0)
         def _():
-            integrals[...] = product + start_ref[...] if starts else product
+            if starts:
+                pltpu.make_async_copy(start_ref, start_buffer, start_sem).wait()
+                integrals[...] = product + start_buffer[...]
+            else:
+                integrals[...] = product
 
         @pl.when(step > 0)
         def _():
@@ -306,7 +318,7 @@
     in_specs += [ANY] * (len(operands) - len(in_specs))
     whole = pl.BlockSpec((rows, columns), lambda t, d: (0, 0))
     if start is not None:
-        in_specs.append(whole)
+        in_specs.append(ANY)
         operands.append(start)
     moved = 2 * (high - low) * aux_slice * rows + 2 * slices * aux_slice * columns
     scratch = [
@@ -328,6 +340,8 @@
         out_spec = whole
         out_shape = jax.ShapeDtypeStruct((rows, columns), jnp.float32)
     moved += out_shape.size * out_shape.dtype.itemsize
+    if start is not None:
+        scratch += [pltpu.VMEM((rows, columns), jnp.float32), pltpu.SemaphoreType.DMA]
     plan = (
         occ_width, steps, slices, low, high, ends,
         [[(first, last) for first, last, _ in parts] for parts in held],
@@ -386,18 +400,19 @@
 
     def share(blocks, after=None):
         if after is not None and len(blocks) > 1:
-            blocks = blocks[:-1] + [gate(blocks[-1], [after])]
+            blocks = blocks[:-1] + [gate(blocks[-1], after)]
         return [b for block in blocks for b in (block, swap(block, 1))]
 
-    first = []
-    for raw in spread(half[:, :1]):
-        own, other = transform(coeff_rows, raw, 0, pair_index, (0, 1))
-        first += [own, swap(other, 1)]
     distant = tuple(range(2, pair_count))
     parts = [
         transform(coeff_rows, half, orbital, pair_index, distant)
         for orbital in range(1, occ_width)
     ]
+    first = []
+    for raw in spread(half[:, :1]):
+        before = [] if first or not parts else [parts[0][-1]]
+        own, other = transform(coeff_rows, raw, 0, pair_index, (0, 1), before)
+        first += [own, swap(other, 1)]
     moved = [first] + [[swap(piece, d) for piece, d in zip(pieces, distant)] for pieces in parts]
     for orbital in range(1, occ_width):
         own, other = transform(coeff_rows, half, orbital, pair_index, (0, 1), moved[1][:1])
@@ -407,8 +422,7 @@
     final = occ_width - 1
     middle = aux_count * 3 // 4
     for orbital in range(occ_width):
-        early = [parts[0][-1]] if orbital == 0 and final else []
-        sent = assemble(moved[orbital], pair_index, early)
+        sent = assemble(moved[orbital], pair_index, [])
         after = []
         if 0 < orbital < final:
             after += moved[orbital + 1][1:]
@@ -420,7 +434,8 @@
         locals_.append(local)
         if orbital < occ_width - 1:
             far.append(spread(local))
-    halves = [spread(locals_[-1][:middle]), spread(locals_[-1][middle:])]
+    upper_rows = locals_[-1][middle:]
+    halves = [spread(locals_[-1][:middle]), spread(upper_rows)]
 
     distances = (sources ^ pair_index).astype(jnp.int32)
 
@@ -438,11 +453,11 @@
             locals_, held, distances, left_energy, right_of(first), everything, True
         )
     right_energy = right_of([occ_width - 1])
-    lower = (0, middle, share(halves[0], total))
+    lower = (0, middle, share(halves[0], [upper_rows] if total is None else [total, upper_rows]))
     start = add_density(
         locals_, [[lower]], distances, left_energy, right_energy, (0, middle), False
     )
-    upper = (middle, aux_count, share(halves[1], start))
+    upper = (middle, aux_count, share(halves[1], [start]))
     total = add_density(
         locals_, [[lower, upper]], distances, left_energy, right_energy, (middle, aux_count), True,
         start=start, total=total,

time: 366 us -> 361 us (0.986)
  transfers between devices with their start and end apart: 38 -> 38, of which waited for: 19 -> 19; matrix products, arithmetic and copies ran while one was open for 3% -> 3% of each run, Pallas kernels for 23% -> 24%
where the time goes in v5:
time: 361 us; the launch traced here: 360 us
  waiting for transfers between devices  191 us (53%)
  Pallas kernels  103 us (29%)
  starting transfers between devices  46.4 us (13%)
  local copies, waits for them, and re-layouts  13.8 us (4%)
    ppermute x29, waiting for transfers between devices, swap(): return lax.ppermute(value, axis, pairs)  107 us
    all_to_all x3, waiting for transfers between devices, per_device(): local = lax.all_to_all(sent, 'aux', split_axis=0, concat_axis=0, tiled=True)  62.7 us
    pallas_call x3, Pallas kernels, add_density(): pl.pallas_call(functools.partial(density_kernel, plan), grid_spec=pltpu.P...  59.1 us
    pallas_call x6, Pallas kernels, transform(): pl.pallas_call(functools.partial(transform_kernel, width, distances), gri...  31.4 us
    ppermute x6, waiting for transfers between devices, along(): return lax.ppermute(value, 'aux', pairs)  21.1 us
    ppermute x6, starting transfers between devices, along(): return lax.ppermute(value, 'aux', pairs)  17.8 us
    ppermute x29, starting transfers between devices, swap(): return lax.ppermute(value, axis, pairs)  16 us
    all_to_all x3, starting transfers between devices, per_device(): local = lax.all_to_all(sent, 'aux', split_axis=0, concat_axis=0, tiled=True)  12.6 us
  transfers between devices with their start and end apart: 38, of which 19 were waited for; matrix products, arithmetic and copies ran while one was open for 3% of the time, Pallas kernels for 24%

profile of v5, /device:TPU:0, one launch (start us, length us, event | category | flops | bytes accessed | tf_op | source)
XLA Modules:
  0.0 359.8 jit_solution(6193168029856394927)
XLA Ops:
  6.7 5.5 %collective-permute-done = bf16[80,1408]{1,0:T(8,128)(2,1)S(1)} collective-permute-done((bf16[80,1408]{1,0:T(8,128)(2,1)S(1)}, bf16[80,1408]{1,0:T(8,128)(2,1)S(1)}, u32[]{:S(2)}, u32[]{:S(2)}) %collective-permute-start) | collective-permute-done | bytes 225312 | tf_op jit(solution)/shard_map/ppermute | solution.py:18
  17.1 7.1 %collective-permute-done.1.refs_1_ = bf16[2,80,1408]{2,1,0:T(8,128)(2,1)S(1)} collective-permute-done((bf16[2,80,1408]{2,1,0:T(8,128)(2,1)S(1)}, bf16[2,80,1408]{2,1,0:T(8,128)(2,1)S(1)}, u32[]{:S(2)}, u32[]{:S(2)}) %collective-permute-start.1) | collective-permute-done | bytes 450592 | tf_op jit(solution)/shard_map/ppermute | solution.py:24
  24.2 5.2 %collective-permute-start.3 = (bf16[2,80,1408]{2,1,0:T(8,128)(2,1)S(1)}, bf16[2,80,1408]{2,1,0:T(8,128)(2,1)}, u32[]{:S(2)}, u32[]{:S(2)}) collective-permute-start(bf16[2,80,1408]{2,1,0:T(8,128)(2,1)S(1)} %collective-permute-done.1.refs_1_), channel_id=1, source_target_pairs={{0,8},{4,12},{8,16},{12,20},{16,24},{20,28},{1,9},{5,13},{9,17},{1... | collective-permute-start | bytes 1351688 | tf_op jit(solution)/shard_map/ppermute | solution.py:24
  31.3 4.9 %collective-permute-done.3.refs_3_ = bf16[2,80,1408]{2,1,0:T(8,128)(2,1)} collective-permute-done((bf16[2,80,1408]{2,1,0:T(8,128)(2,1)S(1)}, bf16[2,80,1408]{2,1,0:T(8,128)(2,1)}, u32[]{:S(2)}, u32[]{:S(2)}) %collective-permute-start.3) | collective-permute-done | bytes 450592 | tf_op jit(solution)/shard_map/ppermute | solution.py:24
  36.3 5.3 %collective-permute-start.5 = (bf16[2,80,1408]{2,1,0:T(8,128)(2,1)}, bf16[2,80,1408]{2,1,0:T(8,128)(2,1)}, u32[]{:S(2)}, u32[]{:S(2)}) collective-permute-start(bf16[2,80,1408]{2,1,0:T(8,128)(2,1)} %collective-permute-done.3.refs_3_), channel_id=1, source_target_pairs={{0,8},{4,12},{8,16},{12,20},{16,24},{20,28},{1,9},{5,13},{9,17},{1... | collective-permute-start | bytes 1351688 | tf_op jit(solution)/shard_map/ppermute | solution.py:24
  43.7 4.2 %collective-permute-done.5.refs_5_ = bf16[2,80,1408]{2,1,0:T(8,128)(2,1)} collective-permute-done((bf16[2,80,1408]{2,1,0:T(8,128)(2,1)}, bf16[2,80,1408]{2,1,0:T(8,128)(2,1)}, u32[]{:S(2)}, u32[]{:S(2)}) %collective-permute-start.5) | collective-permute-done | bytes 450592 | tf_op jit(solution)/shard_map/ppermute | solution.py:24
  47.8 4.9 %collective-permute-done.6.refs_6_ = bf16[2,80,1408]{2,1,0:T(8,128)(2,1)} collective-permute-done((bf16[2,80,1408]{2,1,0:T(8,128)(2,1)}, bf16[2,80,1408]{2,1,0:T(8,128)(2,1)}, u32[]{:S(2)}, u32[]{:S(2)}) %collective-permute-start.6) | collective-permute-done | bytes 450592 | tf_op jit(solution)/shard_map/ppermute | solution.py:24
  54.9 4.9 %place.1 = bf16[4,2,2,80,1408]{4,3,2,1,0:T(8,128)(2,1)} custom-call(s32[3]{0:T(128)} %pad_add_fusion.index_ref, bf16[2,80,1408]{2,1,0:T(8,128)(2,1)} %copy-done.9, bf16[2,80,1408]{2,1,0:T(8,128)(2,1)} %copy-done.13, bf16[2,80,1408]{2,1,0:T(8,128)(2,1)} %copy-done.14, bf16[2,80,1408]{2,1,0:T(8,128)(2,1)} %collective-permute-done.3.refs_3_, ...), custom_call_target="tpu_custom_call" | custom-call | bytes 7208960 | tf_op jit(solution)/shard_map/place/pallas_call | solution.py:58
  59.8 5.6 %transform.6 = (bf16[2,320,512]{2,1,0:T(8,128)(2,1)}, bf16[2,320,512]{2,1,0:T(8,128)(2,1)}) custom-call(s32[1]{0:T(128)} %bitcast.3.index_ref, bf16[1280,1408]{1,0:T(8,128)(2,1)} %bitcast.25, bf16[2,3,1408,512]{3,2,1,0:T(8,128)(2,1)} %bitcast.21), custom_call_target="tpu_custom_call" | custom-call | flops 1845493760 | bytes 7798784 | tf_op jit(solution)/shard_map/transform/pallas_call | solution.py:101
  65.4 5.1 %transform.7 = (bf16[2,320,512]{2,1,0:T(8,128)(2,1)}, bf16[2,320,512]{2,1,0:T(8,128)(2,1)}) custom-call(s32[1]{0:T(128)} %bitcast.3.index_ref, bf16[1280,1408]{1,0:T(8,128)(2,1)} %bitcast.26, bf16[2,1,1408,512]{3,2,1,0:T(8,128)(2,1)} %copy-done.2, bf16[2,320,512]{2,1,0:T(8,128)(2,1)} %get-tuple-element.17.refs_0_), custom_call_target="tpu_custom_call" | custom-call | flops 1845493760 | bytes 5996544 | tf_op jit(solution)/shard_map/transform/pallas_call | solution.py:101
  70.6 5.1 %transform.8 = (bf16[2,320,512]{2,1,0:T(8,128)(2,1)}, bf16[2,320,512]{2,1,0:T(8,128)(2,1)}) custom-call(s32[1]{0:T(128)} %bitcast.3.index_ref, bf16[1280,1408]{1,0:T(8,128)(2,1)} %bitcast.27, bf16[2,1,1408,512]{3,2,1,0:T(8,128)(2,1)} %collective-permute-done.15.half_ref), custom_call_target="tpu_custom_call" | custom-call | flops 1845493760 | bytes 5996544 | tf_op jit(solution)/shard_map/transform/pallas_call | solution.py:101
  87.0 5.6 %transform.11 = (bf16[2,320,512]{2,1,0:T(8,128)(2,1)}, bf16[2,320,512]{2,1,0:T(8,128)(2,1)}) custom-call(s32[1]{0:T(128)} %bitcast.3.index_ref, bf16[1280,1408]{1,0:T(8,128)(2,1)} %bitcast.28, bf16[2,3,1408,512]{3,2,1,0:T(8,128)(2,1)} %bitcast.22), custom_call_target="tpu_custom_call" | custom-call | flops 1845493760 | bytes 7798784 | tf_op jit(solution)/shard_map/transform/pallas_call | solution.py:101
  94.6 8.7 %collective-permute-done.17.refs_0_.refs_2_ = bf16[2,320,512]{2,1,0:T(8,128)(2,1)S(1)} collective-permute-done((bf16[2,320,512]{2,1,0:T(8,128)(2,1)}, bf16[2,320,512]{2,1,0:T(8,128)(2,1)S(1)}, u32[]{:S(2)}, u32[]{:S(2)}) %collective-permute-start.17) | collective-permute-done | bytes 655392 | tf_op jit(solution)/shard_map/ppermute | solution.py:18
  104.2 5.0 %transform.9 = (bf16[2,320,512]{2,1,0:T(8,128)(2,1)}, bf16[2,320,512]{2,1,0:T(8,128)(2,1)}) custom-call(s32[1]{0:T(128)} %bitcast.3.index_ref, bf16[1280,1408]{1,0:T(8,128)(2,1)} %bitcast.29, bf16[2,3,1408,512]{3,2,1,0:T(8,128)(2,1)} %bitcast.23, bf16[2,320,512]{2,1,0:T(8,128)(2,1)} %copy-done.6), custom_call_target="tpu_custom_call" | custom-call | flops 1845493760 | bytes 5996544 | tf_op jit(solution)/shard_map/transform/pallas_call | solution.py:101
  109.2 5.1 %transform.10 = (bf16[2,320,512]{2,1,0:T(8,128)(2,1)}, bf16[2,320,512]{2,1,0:T(8,128)(2,1)}) custom-call(s32[1]{0:T(128)} %bitcast.3.index_ref, bf16[1280,1408]{1,0:T(8,128)(2,1)} %bitcast.30, bf16[2,3,1408,512]{3,2,1,0:T(8,128)(2,1)} %bitcast.24, bf16[2,320,512]{2,1,0:T(8,128)(2,1)} %get-tuple-element.23.refs_0_), custom_call_target="tpu_custom_call" | custom-call | flops 1845493760 | bytes 5996544 | tf_op jit(solution)/shard_map/transform/pallas_call | solution.py:101
  118.4 13.1 %collective-permute-done.21.refs_2_ = bf16[2,320,512]{2,1,0:T(8,128)(2,1)} collective-permute-done((bf16[2,320,512]{2,1,0:T(8,128)(2,1)}, bf16[2,320,512]{2,1,0:T(8,128)(2,1)}, u32[]{:S(2)}, u32[]{:S(2)}) %collective-permute-start.21) | collective-permute-done | bytes 655392 | tf_op jit(solution)/shard_map/ppermute | solution.py:18
  131.5 12.3 %collective-permute-done.22.refs_3_ = bf16[2,320,512]{2,1,0:T(8,128)(2,1)} collective-permute-done((bf16[2,320,512]{2,1,0:T(8,128)(2,1)}, bf16[2,320,512]{2,1,0:T(8,128)(2,1)}, u32[]{:S(2)}, u32[]{:S(2)}) %collective-permute-start.22) | collective-permute-done | bytes 655392 | tf_op jit(solution)/shard_map/ppermute | solution.py:18
  145.5 4.6 %all-to-all-start.1 = ((bf16[8,320,512]{2,1,0:T(8,128)(2,1)}), bf16[8,320,512]{2,1,0:T(8,128)(2,1)}, u32[]{:S(2)}, u32[]{:S(2)}) async-start(bf16[8,320,512]{2,1,0:T(8,128)(2,1)} %gate.4), calls=%async_computation.1 | async-start | bytes 5242880 | tf_op jit(solution)/shard_map/all_to_all | solution.py:433
  150.9 60.0 %all-to-all-done.1.refs_3_.refs_9_ = bf16[8,320,512]{2,1,0:T(8,128)(2,1)} async-done(((bf16[8,320,512]{2,1,0:T(8,128)(2,1)}), bf16[8,320,512]{2,1,0:T(8,128)(2,1)}, u32[]{:S(2)}, u32[]{:S(2)}) %all-to-all-start.1) | async-done | bytes 2621472 | tf_op jit(solution)/shard_map/all_to_all | solution.py:433
  218.7 51.1 %collective-permute-done.29.refs_11_ = bf16[8,320,512]{2,1,0:T(8,128)(2,1)} collective-permute-done((bf16[8,320,512]{2,1,0:T(8,128)(2,1)}, bf16[8,320,512]{2,1,0:T(8,128)(2,1)}, u32[]{:S(2)}, u32[]{:S(2)}) %collective-permute-start.29) | collective-permute-done | bytes 2621472 | tf_op jit(solution)/shard_map/ppermute | solution.py:18
  283.1 31.7 %density.2.refs_1_.refs_14_ = bf16[960,4096]{1,0:T(8,128)(2,1)} custom-call(s32[2]{0:T(128)} %get-tuple-element.29.distance_ref, f32[960,1]{1,0:T(8,128)} %sub.71.refs_0_, f32[1,1280]{1,0:T(1,128)} %reshape.65.refs_1_, bf16[8,320,512]{2,1,0:T(8,128)(2,1)} %copy-done.1, bf16[8,320,512]{2,1,0:T(8,128)(2,1)} %all-to-all-done.1.refs_3_.refs_9_, ...), custom_call_target="tpu_custom_call" | custom-call | flops 20132659200 | bytes 26214400 | tf_op jit(solution)/shard_map/density/pallas_call | solution.py:350
  314.9 7.7 %collective-permute-done.25.refs_0_ = bf16[6,320,512]{2,1,0:T(8,128)(2,1)} collective-permute-done((bf16[6,320,512]{2,1,0:T(8,128)(2,1)}, bf16[6,320,512]{2,1,0:T(8,128)(2,1)}, u32[]{:S(2)}, u32[]{:S(2)}) %collective-permute-start.25) | collective-permute-done | bytes 1966112 | tf_op jit(solution)/shard_map/ppermute | solution.py:18
  328.1 11.5 %integrals.1.refs_1_.refs_13_ = f32[960,640]{1,0:T(8,128)} custom-call(s32[2]{0:T(128)} %get-tuple-element.29.distance_ref, f32[960,1]{1,0:T(8,128)} %sub.71.refs_0_, f32[1,640]{1,0:T(1,128)} %reshape.61.refs_1_, bf16[8,320,512]{2,1,0:T(8,128)(2,1)} %copy-done.1, bf16[8,320,512]{2,1,0:T(8,128)(2,1)} %all-to-all-done.1.refs_3_.refs_9_, ...), custom_call_target="tpu_custom_call" | custom-call | flops 3774873600 | bytes 13598720 | tf_op jit(solution)/shard_map/integrals/pallas_call | solution.py:350
  343.7 15.9 %density.3 = bf16[960,4096]{1,0:T(8,128)(2,1)} custom-call(s32[2]{0:T(128)} %get-tuple-element.29.distance_ref, f32[960,1]{1,0:T(8,128)} %sub.71.refs_0_, f32[1,640]{1,0:T(1,128)} %reshape.61.refs_1_, bf16[8,320,512]{2,1,0:T(8,128)(2,1)} %copy-done.1, bf16[8,320,512]{2,1,0:T(8,128)(2,1)} %all-to-all-done.1.refs_3_.refs_9_, bf16[8,320,512]{2,1,0:T(8,128)(2,1)} %copy-done, ...), custom_call_target="tpu_custom_call" | custom-call | flops 6291456000 | bytes 22937600 | tf_op jit(solution)/shard_map/density/pallas_call | solution.py:350
  (130 shorter events, 68.1 us)
Async XLA Ops:
  2.1 68.5 %collective-permute-start.15 = (bf16[2,1,1408,512]{3,2,1,0:T(8,128)(2,1)S(1)}, bf16[2,1,1408,512]{3,2,1,0:T(8,128)(2,1)}, u32[]{:S(2)}, u32[]{:S(2)}) collective-permute-start(bf16[2,1,1408,512]{3,2,1,0:T(8,128)(2,1)S(1)} %slice.37.half_ref), channel_id=1, source_target_pairs={{0,2},{1,3},{2,0},{3,1},{4,6},{5,7},{6,4},{7,5},{8,10},{9,11},{10,... | collective-permute-start | bytes 8650760 | tf_op jit(solution)/shard_map/ppermute | solution.py:18
  15.7 13.7 %collective-permute-start.2 = (bf16[2,80,1408]{2,1,0:T(8,128)(2,1)S(1)}, bf16[2,80,1408]{2,1,0:T(8,128)(2,1)S(1)}, u32[]{:S(2)}, u32[]{:S(2)}) collective-permute-start(bf16[2,80,1408]{2,1,0:T(8,128)(2,1)S(1)} %pad_maximum_fusion.refs_0_), channel_id=1, source_target_pairs={{8,0},{12,4},{16,8},{20,12},{24,16},{28,20},{9,1},{13,5},{17,9},{2... | collective-permute-start | bytes 1351688 | tf_op jit(solution)/shard_map/ppermute | solution.py:24
  17.0 13.7 %collective-permute-start.7 = (bf16[2,80,1408]{2,1,0:T(8,128)(2,1)S(1)}, bf16[2,80,1408]{2,1,0:T(8,128)(2,1)S(1)}, u32[]{:S(2)}, u32[]{:S(2)}) collective-permute-start(bf16[2,80,1408]{2,1,0:T(8,128)(2,1)S(1)} %pad_maximum_fusion.refs_0_), channel_id=1, source_target_pairs={{0,1},{1,0},{2,3},{3,2},{4,5},{5,4},{6,7},{7,6},{8,9},{9,8},{10,11... | collective-permute-start | bytes 1351688 | tf_op jit(solution)/shard_map/ppermute | solution.py:18
  29.4 12.2 %collective-permute-start.4 = (bf16[2,80,1408]{2,1,0:T(8,128)(2,1)S(1)}, bf16[2,80,1408]{2,1,0:T(8,128)(2,1)}, u32[]{:S(2)}, u32[]{:S(2)}) collective-permute-start(bf16[2,80,1408]{2,1,0:T(8,128)(2,1)S(1)} %collective-permute-done.2.refs_2_), channel_id=1, source_target_pairs={{8,0},{12,4},{16,8},{20,12},{24,16},{28,20},{9,1},{13,5},{17,9},{2... | collective-permute-start | bytes 1351688 | tf_op jit(solution)/shard_map/ppermute | solution.py:24
  30.7 12.2 %collective-permute-start.8 = (bf16[2,80,1408]{2,1,0:T(8,128)(2,1)S(1)}, bf16[2,80,1408]{2,1,0:T(8,128)(2,1)S(1)}, u32[]{:S(2)}, u32[]{:S(2)}) collective-permute-start(bf16[2,80,1408]{2,1,0:T(8,128)(2,1)S(1)} %collective-permute-done.1.refs_1_), channel_id=1, source_target_pairs={{0,1},{1,0},{2,3},{3,2},{4,5},{5,4},{6,7},{7,6},{8,9},{9,8},{10,11... | collective-permute-start | bytes 1351688 | tf_op jit(solution)/shard_map/ppermute | solution.py:18
  30.8 12.2 %collective-permute-start.9 = (bf16[2,80,1408]{2,1,0:T(8,128)(2,1)S(1)}, bf16[2,80,1408]{2,1,0:T(8,128)(2,1)S(1)}, u32[]{:S(2)}, u32[]{:S(2)}) collective-permute-start(bf16[2,80,1408]{2,1,0:T(8,128)(2,1)S(1)} %collective-permute-done.2.refs_2_), channel_id=1, source_target_pairs={{0,1},{1,0},{2,3},{3,2},{4,5},{5,4},{6,7},{7,6},{8,9},{9,8},{10,11... | collective-permute-start | bytes 1351688 | tf_op jit(solution)/shard_map/ppermute | solution.py:18
  81.5 64.1 %all-to-all-start = ((bf16[8,320,512]{2,1,0:T(8,128)(2,1)}), bf16[8,320,512]{2,1,0:T(8,128)(2,1)S(1)}, u32[]{:S(2)}, u32[]{:S(2)}) async-start(bf16[8,320,512]{2,1,0:T(8,128)(2,1)} %assemble.3), calls=%async_computation | async-start | bytes 5242880 | tf_op jit(solution)/shard_map/all_to_all | solution.py:433
  85.5 17.8 %collective-permute-start.17 = (bf16[2,320,512]{2,1,0:T(8,128)(2,1)}, bf16[2,320,512]{2,1,0:T(8,128)(2,1)S(1)}, u32[]{:S(2)}, u32[]{:S(2)}) collective-permute-start(bf16[2,320,512]{2,1,0:T(8,128)(2,1)} %get-tuple-element.22), channel_id=1, source_target_pairs={{0,2},{1,3},{2,0},{3,1},{4,6},{5,7},{6,4},{7,5},{8,10},{9,11},{10,... | collective-permute-start | bytes 1966088 | tf_op jit(solution)/shard_map/ppermute | solution.py:18
  86.1 29.6 %collective-permute-start.19 = (bf16[2,320,512]{2,1,0:T(8,128)(2,1)}, bf16[2,320,512]{2,1,0:T(8,128)(2,1)}, u32[]{:S(2)}, u32[]{:S(2)}) collective-permute-start(bf16[2,320,512]{2,1,0:T(8,128)(2,1)} %get-tuple-element.17.refs_0_), channel_id=1, source_target_pairs={{0,3},{1,2},{2,1},{3,0},{4,7},{5,6},{6,5},{7,4},{8,11},{9,10},{10,... | collective-permute-start | bytes 1966088 | tf_op jit(solution)/shard_map/ppermute | solution.py:18
  92.6 39.0 %collective-permute-start.21 = (bf16[2,320,512]{2,1,0:T(8,128)(2,1)}, bf16[2,320,512]{2,1,0:T(8,128)(2,1)}, u32[]{:S(2)}, u32[]{:S(2)}) collective-permute-start(bf16[2,320,512]{2,1,0:T(8,128)(2,1)} %get-tuple-element.26), channel_id=1, source_target_pairs={{0,2},{1,3},{2,0},{3,1},{4,6},{5,7},{6,4},{7,5},{8,10},{9,11},{10,... | collective-permute-start | bytes 1966088 | tf_op jit(solution)/shard_map/ppermute | solution.py:18
  93.2 50.6 %collective-permute-start.22 = (bf16[2,320,512]{2,1,0:T(8,128)(2,1)}, bf16[2,320,512]{2,1,0:T(8,128)(2,1)}, u32[]{:S(2)}, u32[]{:S(2)}) collective-permute-start(bf16[2,320,512]{2,1,0:T(8,128)(2,1)} %get-tuple-element.27), channel_id=1, source_target_pairs={{0,3},{1,2},{2,1},{3,0},{4,7},{5,6},{6,5},{7,4},{8,11},{9,10},{10,... | collective-permute-start | bytes 1966088 | tf_op jit(solution)/shard_map/ppermute | solution.py:18
  114.3 29.5 %collective-permute-start.20 = (bf16[2,320,512]{2,1,0:T(8,128)(2,1)}, bf16[2,320,512]{2,1,0:T(8,128)(2,1)S(1)}, u32[]{:S(2)}, u32[]{:S(2)}) collective-permute-start(bf16[2,320,512]{2,1,0:T(8,128)(2,1)} %get-tuple-element.25), channel_id=1, source_target_pairs={{0,1},{1,0},{2,3},{3,2},{4,5},{5,4},{6,7},{7,6},{8,9},{9,8},{10,11... | collective-permute-start | bytes 1966088 | tf_op jit(solution)/shard_map/ppermute | solution.py:18
  145.5 65.3 %all-to-all-start.1 = ((bf16[8,320,512]{2,1,0:T(8,128)(2,1)}), bf16[8,320,512]{2,1,0:T(8,128)(2,1)}, u32[]{:S(2)}, u32[]{:S(2)}) async-start(bf16[8,320,512]{2,1,0:T(8,128)(2,1)} %gate.4), calls=%async_computation.1 | async-start | bytes 5242880 | tf_op jit(solution)/shard_map/all_to_all | solution.py:433
  150.1 64.0 %collective-permute-start.23 = (bf16[8,320,512]{2,1,0:T(8,128)(2,1)S(1)}, bf16[8,320,512]{2,1,0:T(8,128)(2,1)}, u32[]{:S(2)}, u32[]{:S(2)}) collective-permute-start(bf16[8,320,512]{2,1,0:T(8,128)(2,1)S(1)} %all-to-all-done.refs_2_.refs_5_), channel_id=1, source_target_pairs={{0,2},{1,3},{2,0},{3,1},{4,6},{5,7},{6,4},{7,5},{8,10},{9,11},{10,... | collective-permute-start | bytes 7864328 | tf_op jit(solution)/shard_map/ppermute | solution.py:18
  210.9 59.0 %collective-permute-start.29 = (bf16[8,320,512]{2,1,0:T(8,128)(2,1)}, bf16[8,320,512]{2,1,0:T(8,128)(2,1)}, u32[]{:S(2)}, u32[]{:S(2)}) collective-permute-start(bf16[8,320,512]{2,1,0:T(8,128)(2,1)} %all-to-all-done.1.refs_3_.refs_9_), channel_id=1, source_target_pairs={{0,2},{1,3},{2,0},{3,1},{4,6},{5,7},{6,4},{7,5},{8,10},{9,11},{10,... | collective-permute-start | bytes 7864328 | tf_op jit(solution)/shard_map/ppermute | solution.py:18
  214.2 63.2 %all-to-all-start.2 = ((bf16[8,320,512]{2,1,0:T(8,128)(2,1)}), bf16[8,320,512]{2,1,0:T(8,128)(2,1)S(1)}, u32[]{:S(2)}, u32[]{:S(2)}) async-start(bf16[8,320,512]{2,1,0:T(8,128)(2,1)} %gate.5), calls=%async_computation.2 | async-start | bytes 5242880 | tf_op jit(solution)/shard_map/all_to_all | solution.py:433
  218.1 65.0 %collective-permute-start.28 = (bf16[8,320,512]{2,1,0:T(8,128)(2,1)}, bf16[8,320,512]{2,1,0:T(8,128)(2,1)}, u32[]{:S(2)}, u32[]{:S(2)}) collective-permute-start(bf16[8,320,512]{2,1,0:T(8,128)(2,1)} %all-to-all-done.1.refs_3_.refs_9_), channel_id=1, source_target_pairs={{0,1},{1,0},{2,3},{3,2},{4,5},{5,4},{6,7},{7,6},{8,9},{9,8},{10,11... | collective-permute-start | bytes 7864328 | tf_op jit(solution)/shard_map/ppermute | solution.py:18
  218.2 64.9 %collective-permute-start.26 = (bf16[8,320,512]{2,1,0:T(8,128)(2,1)}, bf16[8,320,512]{2,1,0:T(8,128)(2,1)}, u32[]{:S(2)}, u32[]{:S(2)}) collective-permute-start(bf16[8,320,512]{2,1,0:T(8,128)(2,1)} %copy-done.1), channel_id=1, source_target_pairs={{0,1},{1,0},{2,3},{3,2},{4,5},{5,4},{6,7},{7,6},{8,9},{9,8},{10,11... | collective-permute-start | bytes 7864328 | tf_op jit(solution)/shard_map/ppermute | solution.py:18
  269.8 13.3 %collective-permute-start.30 = (bf16[8,320,512]{2,1,0:T(8,128)(2,1)}, bf16[8,320,512]{2,1,0:T(8,128)(2,1)}, u32[]{:S(2)}, u32[]{:S(2)}) collective-permute-start(bf16[8,320,512]{2,1,0:T(8,128)(2,1)} %collective-permute-done.29.refs_11_), channel_id=1, source_target_pairs={{0,1},{1,0},{2,3},{3,2},{4,5},{5,4},{6,7},{7,6},{8,9},{9,8},{10,11... | collective-permute-start | bytes 7864328 | tf_op jit(solution)/shard_map/ppermute | solution.py:18
  269.9 13.3 %collective-permute-start.27 = (bf16[8,320,512]{2,1,0:T(8,128)(2,1)}, bf16[8,320,512]{2,1,0:T(8,128)(2,1)}, u32[]{:S(2)}, u32[]{:S(2)}) collective-permute-start(bf16[8,320,512]{2,1,0:T(8,128)(2,1)} %collective-permute-done.23.refs_1_.refs_7_), channel_id=1, source_target_pairs={{0,1},{1,0},{2,3},{3,2},{4,5},{5,4},{6,7},{7,6},{8,9},{9,8},{10,11... | collective-permute-start | bytes 7864328 | tf_op jit(solution)/shard_map/ppermute | solution.py:18
  278.9 43.7 %collective-permute-start.25 = (bf16[6,320,512]{2,1,0:T(8,128)(2,1)}, bf16[6,320,512]{2,1,0:T(8,128)(2,1)}, u32[]{:S(2)}, u32[]{:S(2)}) collective-permute-start(bf16[6,320,512]{2,1,0:T(8,128)(2,1)} %slice.38.refs_5_), channel_id=1, source_target_pairs={{0,2},{1,3},{2,0},{3,1},{4,6},{5,7},{6,4},{7,5},{8,10},{9,11},{10,... | collective-permute-start | bytes 5898248 | tf_op jit(solution)/shard_map/ppermute | solution.py:18
  283.1 41.8 %collective-permute-start.24 = (bf16[6,320,512]{2,1,0:T(8,128)(2,1)}, bf16[6,320,512]{2,1,0:T(8,128)(2,1)S(1)}, u32[]{:S(2)}, u32[]{:S(2)}) collective-permute-start(bf16[6,320,512]{2,1,0:T(8,128)(2,1)} %slice.38.refs_5_), channel_id=1, source_target_pairs={{0,1},{1,0},{2,3},{3,2},{4,5},{5,4},{6,7},{7,6},{8,9},{9,8},{10,11... | collective-permute-start | bytes 5898248 | tf_op jit(solution)/shard_map/ppermute | solution.py:18
  322.6 17.1 %collective-permute-start.33 = (bf16[2,320,512]{2,1,0:T(8,128)(2,1)S(1)}, bf16[2,320,512]{2,1,0:T(8,128)(2,1)S(1)}, u32[]{:S(2)}, u32[]{:S(2)}) collective-permute-start(bf16[2,320,512]{2,1,0:T(8,128)(2,1)S(1)} %copy-done.5), channel_id=1, source_target_pairs={{0,2},{1,3},{2,0},{3,1},{4,6},{5,7},{6,4},{7,5},{8,10},{9,11},{10,... | collective-permute-start | bytes 1966088 | tf_op jit(solution)/shard_map/ppermute | solution.py:18
  324.7 15.9 %collective-permute-start.32 = (bf16[2,320,512]{2,1,0:T(8,128)(2,1)S(1)}, bf16[2,320,512]{2,1,0:T(8,128)(2,1)}, u32[]{:S(2)}, u32[]{:S(2)}) collective-permute-start(bf16[2,320,512]{2,1,0:T(8,128)(2,1)S(1)} %copy-done.5), channel_id=1, source_target_pairs={{0,1},{1,0},{2,3},{3,2},{4,5},{5,4},{6,7},{7,6},{8,9},{9,8},{10,11... | collective-permute-start | bytes 1966088 | tf_op jit(solution)/shard_map/ppermute | solution.py:18
  (36 other events, 448.4 us)

commit v6 on v5

--- a/solution.py
+++ b/solution.py
@@ -195,7 +195,7 @@
         start_buffer, start_sem = refs[-2:]
         del refs[-2:]
     if ends:
-        integrals, amplitudes, remote_ref, sems = refs
+        integrals, amplitudes, factors, remote_ref, sems = refs
     else:
         remote_ref, sems = refs
         integrals = out_ref
@@ -237,6 +237,11 @@
         def _():
             pltpu.make_async_copy(start_ref, start_buffer, start_sem).start()
 
+    if ends:
+        @pl.when(step == 0)
+        def _():
+            factors[...] = spin_scale / (left_energy[...] + right_energy[...])
+
     def wait_for(t):
         for number in range(len(held_refs) * steps):
             copy_of(held_refs[0][0][2][0], t, number, t).wait()
@@ -273,8 +278,7 @@
         if ends:
             @pl.when(step == turns - 1)
             def _():
-                gap = left_energy[...] + right_energy[...]
-                amplitudes[...] = (spin_scale * integrals[...] / gap).astype(jnp.bfloat16)
+                amplitudes[...] = (integrals[...] * factors[...]).astype(jnp.bfloat16)
 
     if ends:
         @pl.when(step >= turns)
@@ -331,6 +335,7 @@
         scratch = [
             pltpu.VMEM((rows, columns), jnp.float32),
             pltpu.VMEM((rows, columns), jnp.bfloat16),
+            pltpu.VMEM((rows, columns), jnp.float32),
         ] + scratch
         if total is not None:
             in_specs.append(out_spec)
@@ -338,8 +343,8 @@
             moved += total.size * 2
     else:
         out_spec = whole
-        out_shape = jax.ShapeDtypeStruct((rows, columns), jnp.float32)
-    moved += out_shape.size * out_shape.dtype.itemsize
+        out_shape = pltpu.VMEM((rows, columns), jnp.float32)
+    moved += rows * max(columns * 4, slices * aux_slice * 2)
     if start is not None:
         scratch += [pltpu.VMEM((rows, columns), jnp.float32), pltpu.SemaphoreType.DMA]
     plan = (

time: 361 us -> 360 us (level)
  transfers between devices with their start and end apart: 38 -> 38, of which waited for: 19 -> 19; matrix products, arithmetic and copies ran while one was open for 3% -> 3% of each run, Pallas kernels for 24% -> 23%
where the time goes in v6:
time: 360 us
  waiting for transfers between devices  191 us (53%)
  Pallas kernels  101 us (28%)
  starting transfers between devices  46.5 us (13%)
  local copies, waits for them, and re-layouts  15.3 us (4%)
    ppermute x29, waiting for transfers between devices, swap(): return lax.ppermute(value, axis, pairs)  108 us
    all_to_all x3, waiting for transfers between devices, per_device(): local = lax.all_to_all(sent, 'aux', split_axis=0, concat_axis=0, tiled=True)  62.7 us
    pallas_call x3, Pallas kernels, add_density(): pl.pallas_call(functools.partial(density_kernel, plan), grid_spec=pltpu.P...  57.1 us
    pallas_call x6, Pallas kernels, transform(): pl.pallas_call(functools.partial(transform_kernel, width, distances), gri...  31.4 us
    ppermute x6, waiting for transfers between devices, along(): return lax.ppermute(value, 'aux', pairs)  21.1 us
    ppermute x6, starting transfers between devices, along(): return lax.ppermute(value, 'aux', pairs)  17.8 us
    ppermute x29, starting transfers between devices, swap(): return lax.ppermute(value, axis, pairs)  16.1 us
    all_to_all x3, starting transfers between devices, per_device(): local = lax.all_to_all(sent, 'aux', split_axis=0, concat_axis=0, tiled=True)  12.6 us
  transfers between devices with their start and end apart: 38, of which 19 were waited for; matrix products, arithmetic and copies ran while one was open for 3% of the time, Pallas kernels for 23%

profile of v6, /device:TPU:0, one launch (start us, length us, event | category | flops | bytes accessed | tf_op | source)
XLA Modules:
  0.0 359.6 jit_solution(9173466155703604635)
XLA Ops:
  6.7 5.5 %collective-permute-done = bf16[80,1408]{1,0:T(8,128)(2,1)S(1)} collective-permute-done((bf16[80,1408]{1,0:T(8,128)(2,1)S(1)}, bf16[80,1408]{1,0:T(8,128)(2,1)S(1)}, u32[]{:S(2)}, u32[]{:S(2)}) %collective-permute-start) | collective-permute-done | bytes 225312 | tf_op jit(solution)/shard_map/ppermute | solution.py:18
  17.1 7.1 %collective-permute-done.1.refs_1_ = bf16[2,80,1408]{2,1,0:T(8,128)(2,1)S(1)} collective-permute-done((bf16[2,80,1408]{2,1,0:T(8,128)(2,1)S(1)}, bf16[2,80,1408]{2,1,0:T(8,128)(2,1)S(1)}, u32[]{:S(2)}, u32[]{:S(2)}) %collective-permute-start.1) | collective-permute-done | bytes 450592 | tf_op jit(solution)/shard_map/ppermute | solution.py:24
  24.2 5.2 %collective-permute-start.3 = (bf16[2,80,1408]{2,1,0:T(8,128)(2,1)S(1)}, bf16[2,80,1408]{2,1,0:T(8,128)(2,1)}, u32[]{:S(2)}, u32[]{:S(2)}) collective-permute-start(bf16[2,80,1408]{2,1,0:T(8,128)(2,1)S(1)} %collective-permute-done.1.refs_1_), channel_id=1, source_target_pairs={{0,8},{4,12},{8,16},{12,20},{16,24},{20,28},{1,9},{5,13},{9,17},{1... | collective-permute-start | bytes 1351688 | tf_op jit(solution)/shard_map/ppermute | solution.py:24
  31.3 4.9 %collective-permute-done.3.refs_3_ = bf16[2,80,1408]{2,1,0:T(8,128)(2,1)} collective-permute-done((bf16[2,80,1408]{2,1,0:T(8,128)(2,1)S(1)}, bf16[2,80,1408]{2,1,0:T(8,128)(2,1)}, u32[]{:S(2)}, u32[]{:S(2)}) %collective-permute-start.3) | collective-permute-done | bytes 450592 | tf_op jit(solution)/shard_map/ppermute | solution.py:24
  36.3 5.3 %collective-permute-start.5 = (bf16[2,80,1408]{2,1,0:T(8,128)(2,1)}, bf16[2,80,1408]{2,1,0:T(8,128)(2,1)}, u32[]{:S(2)}, u32[]{:S(2)}) collective-permute-start(bf16[2,80,1408]{2,1,0:T(8,128)(2,1)} %collective-permute-done.3.refs_3_), channel_id=1, source_target_pairs={{0,8},{4,12},{8,16},{12,20},{16,24},{20,28},{1,9},{5,13},{9,17},{1... | collective-permute-start | bytes 1351688 | tf_op jit(solution)/shard_map/ppermute | solution.py:24
  43.7 4.2 %collective-permute-done.5.refs_5_ = bf16[2,80,1408]{2,1,0:T(8,128)(2,1)} collective-permute-done((bf16[2,80,1408]{2,1,0:T(8,128)(2,1)}, bf16[2,80,1408]{2,1,0:T(8,128)(2,1)}, u32[]{:S(2)}, u32[]{:S(2)}) %collective-permute-start.5) | collective-permute-done | bytes 450592 | tf_op jit(solution)/shard_map/ppermute | solution.py:24
  47.8 4.9 %collective-permute-done.6.refs_6_ = bf16[2,80,1408]{2,1,0:T(8,128)(2,1)} collective-permute-done((bf16[2,80,1408]{2,1,0:T(8,128)(2,1)}, bf16[2,80,1408]{2,1,0:T(8,128)(2,1)}, u32[]{:S(2)}, u32[]{:S(2)}) %collective-permute-start.6) | collective-permute-done | bytes 450592 | tf_op jit(solution)/shard_map/ppermute | solution.py:24
  54.9 4.9 %place.1 = bf16[4,2,2,80,1408]{4,3,2,1,0:T(8,128)(2,1)} custom-call(s32[3]{0:T(128)} %pad_add_fusion.index_ref, bf16[2,80,1408]{2,1,0:T(8,128)(2,1)} %copy-done.10, bf16[2,80,1408]{2,1,0:T(8,128)(2,1)} %copy-done.14, bf16[2,80,1408]{2,1,0:T(8,128)(2,1)} %copy-done.15, bf16[2,80,1408]{2,1,0:T(8,128)(2,1)} %collective-permute-done.3.refs_3_, ...), custom_call_target="tpu_custom_call" | custom-call | bytes 7208960 | tf_op jit(solution)/shard_map/place/pallas_call | solution.py:58
  59.8 5.6 %transform.6 = (bf16[2,320,512]{2,1,0:T(8,128)(2,1)}, bf16[2,320,512]{2,1,0:T(8,128)(2,1)}) custom-call(s32[1]{0:T(128)} %bitcast.3.index_ref, bf16[1280,1408]{1,0:T(8,128)(2,1)} %bitcast.25, bf16[2,3,1408,512]{3,2,1,0:T(8,128)(2,1)} %bitcast.21), custom_call_target="tpu_custom_call" | custom-call | flops 1845493760 | bytes 7798784 | tf_op jit(solution)/shard_map/transform/pallas_call | solution.py:101
  65.4 5.0 %transform.7 = (bf16[2,320,512]{2,1,0:T(8,128)(2,1)}, bf16[2,320,512]{2,1,0:T(8,128)(2,1)}) custom-call(s32[1]{0:T(128)} %bitcast.3.index_ref, bf16[1280,1408]{1,0:T(8,128)(2,1)} %bitcast.26, bf16[2,1,1408,512]{3,2,1,0:T(8,128)(2,1)} %copy-done.3, bf16[2,320,512]{2,1,0:T(8,128)(2,1)} %get-tuple-element.17.refs_0_), custom_call_target="tpu_custom_call" | custom-call | flops 1845493760 | bytes 5996544 | tf_op jit(solution)/shard_map/transform/pallas_call | solution.py:101
  70.6 5.1 %transform.8 = (bf16[2,320,512]{2,1,0:T(8,128)(2,1)}, bf16[2,320,512]{2,1,0:T(8,128)(2,1)}) custom-call(s32[1]{0:T(128)} %bitcast.3.index_ref, bf16[1280,1408]{1,0:T(8,128)(2,1)} %bitcast.27, bf16[2,1,1408,512]{3,2,1,0:T(8,128)(2,1)} %collective-permute-done.15.half_ref), custom_call_target="tpu_custom_call" | custom-call | flops 1845493760 | bytes 5996544 | tf_op jit(solution)/shard_map/transform/pallas_call | solution.py:101
  87.0 5.6 %transform.11 = (bf16[2,320,512]{2,1,0:T(8,128)(2,1)}, bf16[2,320,512]{2,1,0:T(8,128)(2,1)}) custom-call(s32[1]{0:T(128)} %bitcast.3.index_ref, bf16[1280,1408]{1,0:T(8,128)(2,1)} %bitcast.28, bf16[2,3,1408,512]{3,2,1,0:T(8,128)(2,1)} %bitcast.22), custom_call_target="tpu_custom_call" | custom-call | flops 1845493760 | bytes 7798784 | tf_op jit(solution)/shard_map/transform/pallas_call | solution.py:101
  94.6 8.7 %collective-permute-done.17.refs_0_.refs_2_ = bf16[2,320,512]{2,1,0:T(8,128)(2,1)S(1)} collective-permute-done((bf16[2,320,512]{2,1,0:T(8,128)(2,1)}, bf16[2,320,512]{2,1,0:T(8,128)(2,1)S(1)}, u32[]{:S(2)}, u32[]{:S(2)}) %collective-permute-start.17) | collective-permute-done | bytes 655392 | tf_op jit(solution)/shard_map/ppermute | solution.py:18
  104.2 5.0 %transform.9 = (bf16[2,320,512]{2,1,0:T(8,128)(2,1)}, bf16[2,320,512]{2,1,0:T(8,128)(2,1)}) custom-call(s32[1]{0:T(128)} %bitcast.3.index_ref, bf16[1280,1408]{1,0:T(8,128)(2,1)} %bitcast.29, bf16[2,3,1408,512]{3,2,1,0:T(8,128)(2,1)} %bitcast.23, bf16[2,320,512]{2,1,0:T(8,128)(2,1)} %copy-done.7), custom_call_target="tpu_custom_call" | custom-call | flops 1845493760 | bytes 5996544 | tf_op jit(solution)/shard_map/transform/pallas_call | solution.py:101
  109.3 5.1 %transform.10 = (bf16[2,320,512]{2,1,0:T(8,128)(2,1)}, bf16[2,320,512]{2,1,0:T(8,128)(2,1)}) custom-call(s32[1]{0:T(128)} %bitcast.3.index_ref, bf16[1280,1408]{1,0:T(8,128)(2,1)} %bitcast.30, bf16[2,3,1408,512]{3,2,1,0:T(8,128)(2,1)} %bitcast.24, bf16[2,320,512]{2,1,0:T(8,128)(2,1)} %get-tuple-element.23.refs_0_), custom_call_target="tpu_custom_call" | custom-call | flops 1845493760 | bytes 5996544 | tf_op jit(solution)/shard_map/transform/pallas_call | solution.py:101
  118.4 13.2 %collective-permute-done.21.refs_2_ = bf16[2,320,512]{2,1,0:T(8,128)(2,1)} collective-permute-done((bf16[2,320,512]{2,1,0:T(8,128)(2,1)}, bf16[2,320,512]{2,1,0:T(8,128)(2,1)}, u32[]{:S(2)}, u32[]{:S(2)}) %collective-permute-start.21) | collective-permute-done | bytes 655392 | tf_op jit(solution)/shard_map/ppermute | solution.py:18
  131.5 12.3 %collective-permute-done.22.refs_3_ = bf16[2,320,512]{2,1,0:T(8,128)(2,1)} collective-permute-done((bf16[2,320,512]{2,1,0:T(8,128)(2,1)}, bf16[2,320,512]{2,1,0:T(8,128)(2,1)}, u32[]{:S(2)}, u32[]{:S(2)}) %collective-permute-start.22) | collective-permute-done | bytes 655392 | tf_op jit(solution)/shard_map/ppermute | solution.py:18
  145.5 4.5 %all-to-all-start.1 = ((bf16[8,320,512]{2,1,0:T(8,128)(2,1)}), bf16[8,320,512]{2,1,0:T(8,128)(2,1)}, u32[]{:S(2)}, u32[]{:S(2)}) async-start(bf16[8,320,512]{2,1,0:T(8,128)(2,1)} %gate.4), calls=%async_computation.1 | async-start | bytes 5242880 | tf_op jit(solution)/shard_map/all_to_all | solution.py:438
  150.9 60.0 %all-to-all-done.1.refs_3_.refs_9_ = bf16[8,320,512]{2,1,0:T(8,128)(2,1)} async-done(((bf16[8,320,512]{2,1,0:T(8,128)(2,1)}), bf16[8,320,512]{2,1,0:T(8,128)(2,1)}, u32[]{:S(2)}, u32[]{:S(2)}) %all-to-all-start.1) | async-done | bytes 2621472 | tf_op jit(solution)/shard_map/all_to_all | solution.py:438
  218.7 51.2 %collective-permute-done.29.refs_11_ = bf16[8,320,512]{2,1,0:T(8,128)(2,1)} collective-permute-done((bf16[8,320,512]{2,1,0:T(8,128)(2,1)}, bf16[8,320,512]{2,1,0:T(8,128)(2,1)}, u32[]{:S(2)}, u32[]{:S(2)}) %collective-permute-start.29) | collective-permute-done | bytes 2621472 | tf_op jit(solution)/shard_map/ppermute | solution.py:18
  283.1 31.4 %density.2.refs_1_.refs_14_ = bf16[960,4096]{1,0:T(8,128)(2,1)} custom-call(s32[2]{0:T(128)} %get-tuple-element.29.distance_ref, f32[960,1]{1,0:T(8,128)} %sub.71.refs_0_, f32[1,1280]{1,0:T(1,128)} %reshape.65.refs_1_, bf16[8,320,512]{2,1,0:T(8,128)(2,1)} %copy-done.2, bf16[8,320,512]{2,1,0:T(8,128)(2,1)} %all-to-all-done.1.refs_3_.refs_9_, ...), custom_call_target="tpu_custom_call" | custom-call | flops 20132659200 | bytes 26214400 | tf_op jit(solution)/shard_map/density/pallas_call | solution.py:355
  314.5 8.0 %collective-permute-done.25.refs_0_ = bf16[6,320,512]{2,1,0:T(8,128)(2,1)} collective-permute-done((bf16[6,320,512]{2,1,0:T(8,128)(2,1)}, bf16[6,320,512]{2,1,0:T(8,128)(2,1)}, u32[]{:S(2)}, u32[]{:S(2)}) %collective-permute-start.25) | collective-permute-done | bytes 1966112 | tf_op jit(solution)/shard_map/ppermute | solution.py:18
  328.0 10.0 %integrals.1.refs_1_.refs_13_ = f32[960,640]{1,0:T(8,128)S(1)} custom-call(s32[2]{0:T(128)} %get-tuple-element.29.distance_ref, f32[960,1]{1,0:T(8,128)} %sub.71.refs_0_, f32[1,640]{1,0:T(1,128)} %reshape.61.refs_1_, bf16[8,320,512]{2,1,0:T(8,128)(2,1)} %copy-done.2, bf16[8,320,512]{2,1,0:T(8,128)(2,1)} %all-to-all-done.1.refs_3_.refs_9_, ...), custom_call_target="tpu_custom_call" | custom-call | flops 3774873600 | bytes 19005440 | tf_op jit(solution)/shard_map/integrals/pallas_call | solution.py:355
  343.7 15.7 %density.3 = bf16[960,4096]{1,0:T(8,128)(2,1)} custom-call(s32[2]{0:T(128)} %get-tuple-element.29.distance_ref, f32[960,1]{1,0:T(8,128)} %sub.71.refs_0_, f32[1,640]{1,0:T(1,128)} %reshape.61.refs_1_, bf16[8,320,512]{2,1,0:T(8,128)(2,1)} %copy-done.2, bf16[8,320,512]{2,1,0:T(8,128)(2,1)} %all-to-all-done.1.refs_3_.refs_9_, bf16[8,320,512]{2,1,0:T(8,128)(2,1)} %copy-done.1, ...), custom_call_target="tpu_custom_call" | custom-call | flops 6291456000 | bytes 22937600 | tf_op jit(solution)/shard_map/density/pallas_call | solution.py:355
  (132 shorter events, 69.5 us)
Async XLA Ops:
  2.1 68.5 %collective-permute-start.15 = (bf16[2,1,1408,512]{3,2,1,0:T(8,128)(2,1)S(1)}, bf16[2,1,1408,512]{3,2,1,0:T(8,128)(2,1)}, u32[]{:S(2)}, u32[]{:S(2)}) collective-permute-start(bf16[2,1,1408,512]{3,2,1,0:T(8,128)(2,1)S(1)} %slice.37.half_ref), channel_id=1, source_target_pairs={{0,2},{1,3},{2,0},{3,1},{4,6},{5,7},{6,4},{7,5},{8,10},{9,11},{10,... | collective-permute-start | bytes 8650760 | tf_op jit(solution)/shard_map/ppermute | solution.py:18
  15.7 13.7 %collective-permute-start.2 = (bf16[2,80,1408]{2,1,0:T(8,128)(2,1)S(1)}, bf16[2,80,1408]{2,1,0:T(8,128)(2,1)S(1)}, u32[]{:S(2)}, u32[]{:S(2)}) collective-permute-start(bf16[2,80,1408]{2,1,0:T(8,128)(2,1)S(1)} %pad_maximum_fusion.refs_0_), channel_id=1, source_target_pairs={{8,0},{12,4},{16,8},{20,12},{24,16},{28,20},{9,1},{13,5},{17,9},{2... | collective-permute-start | bytes 1351688 | tf_op jit(solution)/shard_map/ppermute | solution.py:24
  17.0 13.7 %collective-permute-start.7 = (bf16[2,80,1408]{2,1,0:T(8,128)(2,1)S(1)}, bf16[2,80,1408]{2,1,0:T(8,128)(2,1)S(1)}, u32[]{:S(2)}, u32[]{:S(2)}) collective-permute-start(bf16[2,80,1408]{2,1,0:T(8,128)(2,1)S(1)} %pad_maximum_fusion.refs_0_), channel_id=1, source_target_pairs={{0,1},{1,0},{2,3},{3,2},{4,5},{5,4},{6,7},{7,6},{8,9},{9,8},{10,11... | collective-permute-start | bytes 1351688 | tf_op jit(solution)/shard_map/ppermute | solution.py:18
  29.4 12.1 %collective-permute-start.4 = (bf16[2,80,1408]{2,1,0:T(8,128)(2,1)S(1)}, bf16[2,80,1408]{2,1,0:T(8,128)(2,1)}, u32[]{:S(2)}, u32[]{:S(2)}) collective-permute-start(bf16[2,80,1408]{2,1,0:T(8,128)(2,1)S(1)} %collective-permute-done.2.refs_2_), channel_id=1, source_target_pairs={{8,0},{12,4},{16,8},{20,12},{24,16},{28,20},{9,1},{13,5},{17,9},{2... | collective-permute-start | bytes 1351688 | tf_op jit(solution)/shard_map/ppermute | solution.py:24
  30.7 12.2 %collective-permute-start.8 = (bf16[2,80,1408]{2,1,0:T(8,128)(2,1)S(1)}, bf16[2,80,1408]{2,1,0:T(8,128)(2,1)S(1)}, u32[]{:S(2)}, u32[]{:S(2)}) collective-permute-start(bf16[2,80,1408]{2,1,0:T(8,128)(2,1)S(1)} %collective-permute-done.1.refs_1_), channel_id=1, source_target_pairs={{0,1},{1,0},{2,3},{3,2},{4,5},{5,4},{6,7},{7,6},{8,9},{9,8},{10,11... | collective-permute-start | bytes 1351688 | tf_op jit(solution)/shard_map/ppermute | solution.py:18
  30.8 12.2 %collective-permute-start.9 = (bf16[2,80,1408]{2,1,0:T(8,128)(2,1)S(1)}, bf16[2,80,1408]{2,1,0:T(8,128)(2,1)S(1)}, u32[]{:S(2)}, u32[]{:S(2)}) collective-permute-start(bf16[2,80,1408]{2,1,0:T(8,128)(2,1)S(1)} %collective-permute-done.2.refs_2_), channel_id=1, source_target_pairs={{0,1},{1,0},{2,3},{3,2},{4,5},{5,4},{6,7},{7,6},{8,9},{9,8},{10,11... | collective-permute-start | bytes 1351688 | tf_op jit(solution)/shard_map/ppermute | solution.py:18
  81.4 64.1 %all-to-all-start = ((bf16[8,320,512]{2,1,0:T(8,128)(2,1)}), bf16[8,320,512]{2,1,0:T(8,128)(2,1)S(1)}, u32[]{:S(2)}, u32[]{:S(2)}) async-start(bf16[8,320,512]{2,1,0:T(8,128)(2,1)} %assemble.3), calls=%async_computation | async-start | bytes 5242880 | tf_op jit(solution)/shard_map/all_to_all | solution.py:438
  85.5 17.8 %collective-permute-start.17 = (bf16[2,320,512]{2,1,0:T(8,128)(2,1)}, bf16[2,320,512]{2,1,0:T(8,128)(2,1)S(1)}, u32[]{:S(2)}, u32[]{:S(2)}) collective-permute-start(bf16[2,320,512]{2,1,0:T(8,128)(2,1)} %get-tuple-element.22), channel_id=1, source_target_pairs={{0,2},{1,3},{2,0},{3,1},{4,6},{5,7},{6,4},{7,5},{8,10},{9,11},{10,... | collective-permute-start | bytes 1966088 | tf_op jit(solution)/shard_map/ppermute | solution.py:18
  86.1 29.6 %collective-permute-start.19 = (bf16[2,320,512]{2,1,0:T(8,128)(2,1)}, bf16[2,320,512]{2,1,0:T(8,128)(2,1)}, u32[]{:S(2)}, u32[]{:S(2)}) collective-permute-start(bf16[2,320,512]{2,1,0:T(8,128)(2,1)} %get-tuple-element.17.refs_0_), channel_id=1, source_target_pairs={{0,3},{1,2},{2,1},{3,0},{4,7},{5,6},{6,5},{7,4},{8,11},{9,10},{10,... | collective-permute-start | bytes 1966088 | tf_op jit(solution)/shard_map/ppermute | solution.py:18
  92.5 39.0 %collective-permute-start.21 = (bf16[2,320,512]{2,1,0:T(8,128)(2,1)}, bf16[2,320,512]{2,1,0:T(8,128)(2,1)}, u32[]{:S(2)}, u32[]{:S(2)}) collective-permute-start(bf16[2,320,512]{2,1,0:T(8,128)(2,1)} %get-tuple-element.26), channel_id=1, source_target_pairs={{0,2},{1,3},{2,0},{3,1},{4,6},{5,7},{6,4},{7,5},{8,10},{9,11},{10,... | collective-permute-start | bytes 1966088 | tf_op jit(solution)/shard_map/ppermute | solution.py:18
  93.2 50.7 %collective-permute-start.22 = (bf16[2,320,512]{2,1,0:T(8,128)(2,1)}, bf16[2,320,512]{2,1,0:T(8,128)(2,1)}, u32[]{:S(2)}, u32[]{:S(2)}) collective-permute-start(bf16[2,320,512]{2,1,0:T(8,128)(2,1)} %get-tuple-element.27), channel_id=1, source_target_pairs={{0,3},{1,2},{2,1},{3,0},{4,7},{5,6},{6,5},{7,4},{8,11},{9,10},{10,... | collective-permute-start | bytes 1966088 | tf_op jit(solution)/shard_map/ppermute | solution.py:18
  114.3 29.5 %collective-permute-start.20 = (bf16[2,320,512]{2,1,0:T(8,128)(2,1)}, bf16[2,320,512]{2,1,0:T(8,128)(2,1)S(1)}, u32[]{:S(2)}, u32[]{:S(2)}) collective-permute-start(bf16[2,320,512]{2,1,0:T(8,128)(2,1)} %get-tuple-element.25), channel_id=1, source_target_pairs={{0,1},{1,0},{2,3},{3,2},{4,5},{5,4},{6,7},{7,6},{8,9},{9,8},{10,11... | collective-permute-start | bytes 1966088 | tf_op jit(solution)/shard_map/ppermute | solution.py:18
  145.5 65.3 %all-to-all-start.1 = ((bf16[8,320,512]{2,1,0:T(8,128)(2,1)}), bf16[8,320,512]{2,1,0:T(8,128)(2,1)}, u32[]{:S(2)}, u32[]{:S(2)}) async-start(bf16[8,320,512]{2,1,0:T(8,128)(2,1)} %gate.4), calls=%async_computation.1 | async-start | bytes 5242880 | tf_op jit(solution)/shard_map/all_to_all | solution.py:438
  150.1 64.0 %collective-permute-start.23 = (bf16[8,320,512]{2,1,0:T(8,128)(2,1)S(1)}, bf16[8,320,512]{2,1,0:T(8,128)(2,1)}, u32[]{:S(2)}, u32[]{:S(2)}) collective-permute-start(bf16[8,320,512]{2,1,0:T(8,128)(2,1)S(1)} %all-to-all-done.refs_2_.refs_5_), channel_id=1, source_target_pairs={{0,2},{1,3},{2,0},{3,1},{4,6},{5,7},{6,4},{7,5},{8,10},{9,11},{10,... | collective-permute-start | bytes 7864328 | tf_op jit(solution)/shard_map/ppermute | solution.py:18
  210.9 59.0 %collective-permute-start.29 = (bf16[8,320,512]{2,1,0:T(8,128)(2,1)}, bf16[8,320,512]{2,1,0:T(8,128)(2,1)}, u32[]{:S(2)}, u32[]{:S(2)}) collective-permute-start(bf16[8,320,512]{2,1,0:T(8,128)(2,1)} %all-to-all-done.1.refs_3_.refs_9_), channel_id=1, source_target_pairs={{0,2},{1,3},{2,0},{3,1},{4,6},{5,7},{6,4},{7,5},{8,10},{9,11},{10,... | collective-permute-start | bytes 7864328 | tf_op jit(solution)/shard_map/ppermute | solution.py:18
  214.1 63.2 %all-to-all-start.2 = ((bf16[8,320,512]{2,1,0:T(8,128)(2,1)}), bf16[8,320,512]{2,1,0:T(8,128)(2,1)S(1)}, u32[]{:S(2)}, u32[]{:S(2)}) async-start(bf16[8,320,512]{2,1,0:T(8,128)(2,1)} %gate.5), calls=%async_computation.2 | async-start | bytes 5242880 | tf_op jit(solution)/shard_map/all_to_all | solution.py:438
  218.1 65.0 %collective-permute-start.28 = (bf16[8,320,512]{2,1,0:T(8,128)(2,1)}, bf16[8,320,512]{2,1,0:T(8,128)(2,1)}, u32[]{:S(2)}, u32[]{:S(2)}) collective-permute-start(bf16[8,320,512]{2,1,0:T(8,128)(2,1)} %all-to-all-done.1.refs_3_.refs_9_), channel_id=1, source_target_pairs={{0,1},{1,0},{2,3},{3,2},{4,5},{5,4},{6,7},{7,6},{8,9},{9,8},{10,11... | collective-permute-start | bytes 7864328 | tf_op jit(solution)/shard_map/ppermute | solution.py:18
  218.2 64.9 %collective-permute-start.26 = (bf16[8,320,512]{2,1,0:T(8,128)(2,1)}, bf16[8,320,512]{2,1,0:T(8,128)(2,1)}, u32[]{:S(2)}, u32[]{:S(2)}) collective-permute-start(bf16[8,320,512]{2,1,0:T(8,128)(2,1)} %copy-done.2), channel_id=1, source_target_pairs={{0,1},{1,0},{2,3},{3,2},{4,5},{5,4},{6,7},{7,6},{8,9},{9,8},{10,11... | collective-permute-start | bytes 7864328 | tf_op jit(solution)/shard_map/ppermute | solution.py:18
  269.8 13.3 %collective-permute-start.30 = (bf16[8,320,512]{2,1,0:T(8,128)(2,1)}, bf16[8,320,512]{2,1,0:T(8,128)(2,1)}, u32[]{:S(2)}, u32[]{:S(2)}) collective-permute-start(bf16[8,320,512]{2,1,0:T(8,128)(2,1)} %collective-permute-done.29.refs_11_), channel_id=1, source_target_pairs={{0,1},{1,0},{2,3},{3,2},{4,5},{5,4},{6,7},{7,6},{8,9},{9,8},{10,11... | collective-permute-start | bytes 7864328 | tf_op jit(solution)/shard_map/ppermute | solution.py:18
  269.8 13.3 %collective-permute-start.27 = (bf16[8,320,512]{2,1,0:T(8,128)(2,1)}, bf16[8,320,512]{2,1,0:T(8,128)(2,1)}, u32[]{:S(2)}, u32[]{:S(2)}) collective-permute-start(bf16[8,320,512]{2,1,0:T(8,128)(2,1)} %collective-permute-done.23.refs_1_.refs_7_), channel_id=1, source_target_pairs={{0,1},{1,0},{2,3},{3,2},{4,5},{5,4},{6,7},{7,6},{8,9},{9,8},{10,11... | collective-permute-start | bytes 7864328 | tf_op jit(solution)/shard_map/ppermute | solution.py:18
  278.8 43.7 %collective-permute-start.25 = (bf16[6,320,512]{2,1,0:T(8,128)(2,1)}, bf16[6,320,512]{2,1,0:T(8,128)(2,1)}, u32[]{:S(2)}, u32[]{:S(2)}) collective-permute-start(bf16[6,320,512]{2,1,0:T(8,128)(2,1)} %slice.38.refs_5_), channel_id=1, source_target_pairs={{0,2},{1,3},{2,0},{3,1},{4,6},{5,7},{6,4},{7,5},{8,10},{9,11},{10,... | collective-permute-start | bytes 5898248 | tf_op jit(solution)/shard_map/ppermute | solution.py:18
  283.1 41.8 %collective-permute-start.24 = (bf16[6,320,512]{2,1,0:T(8,128)(2,1)}, bf16[6,320,512]{2,1,0:T(8,128)(2,1)S(1)}, u32[]{:S(2)}, u32[]{:S(2)}) collective-permute-start(bf16[6,320,512]{2,1,0:T(8,128)(2,1)} %slice.38.refs_5_), channel_id=1, source_target_pairs={{0,1},{1,0},{2,3},{3,2},{4,5},{5,4},{6,7},{7,6},{8,9},{9,8},{10,11... | collective-permute-start | bytes 5898248 | tf_op jit(solution)/shard_map/ppermute | solution.py:18
  322.5 17.1 %collective-permute-start.33 = (bf16[2,320,512]{2,1,0:T(8,128)(2,1)S(1)}, bf16[2,320,512]{2,1,0:T(8,128)(2,1)S(1)}, u32[]{:S(2)}, u32[]{:S(2)}) collective-permute-start(bf16[2,320,512]{2,1,0:T(8,128)(2,1)S(1)} %copy-done.6), channel_id=1, source_target_pairs={{0,2},{1,3},{2,0},{3,1},{4,6},{5,7},{6,4},{7,5},{8,10},{9,11},{10,... | collective-permute-start | bytes 1966088 | tf_op jit(solution)/shard_map/ppermute | solution.py:18
  324.7 15.8 %collective-permute-start.32 = (bf16[2,320,512]{2,1,0:T(8,128)(2,1)S(1)}, bf16[2,320,512]{2,1,0:T(8,128)(2,1)}, u32[]{:S(2)}, u32[]{:S(2)}) collective-permute-start(bf16[2,320,512]{2,1,0:T(8,128)(2,1)S(1)} %copy-done.6), channel_id=1, source_target_pairs={{0,1},{1,0},{2,3},{3,2},{4,5},{5,4},{6,7},{7,6},{8,9},{9,8},{10,11... | collective-permute-start | bytes 1966088 | tf_op jit(solution)/shard_map/ppermute | solution.py:18
  (37 other events, 450.0 us)

commit v7 on v5

--- a/solution.py
+++ b/solution.py
@@ -26,17 +26,28 @@
 
 def place_kernel(line, index_ref, *refs):
     count = 2 * line - 1
-    own_refs, mate_refs, out_ref = refs[:count], refs[count:-1], refs[-1]
+    own_refs, mate_refs, out_ref, sems = refs[:count], refs[count:-2], refs[-2], refs[-1]
     here, side, core = index_ref[0], index_ref[1], index_ref[2]
-    for half, piece_refs in ((core, own_refs), (1 - core, mate_refs)):
-        for number, ref in enumerate(piece_refs):
-            shift = (number + 1) // 2
-            row = here - shift if number % 2 else here + shift
-
-            @pl.when((row >= 0) & (row < line))
-            def _():
-                for slot in range(2):
-                    out_ref[row, side ^ slot, half] = ref[slot]
+
+    def each(action):
+        for which, (half, piece_refs) in enumerate(((core, own_refs), (1 - core, mate_refs))):
+            for number, ref in enumerate(piece_refs):
+                shift = (number + 1) // 2
+                row = here - shift if number % 2 else here + shift
+
+                @pl.when((row >= 0) & (row < line))
+                def _():
+                    for slot in range(2):
+                        action(
+                            pltpu.make_async_copy(
+                                ref.at[slot],
+                                out_ref.at[row, side ^ slot, half],
+                                sems.at[which, number, slot],
+                            )
+                        )
+
+    each(lambda copy: copy.start())
+    each(lambda copy: copy.wait())
 
 
 def gather_coefficients(vir_coeffs):
@@ -58,9 +69,10 @@
     placed = pl.pallas_call(
         functools.partial(place_kernel, line),
         in_specs=[pl.BlockSpec(memory_space=pltpu.SMEM)]
-        + [pl.BlockSpec(memory_space=pltpu.VMEM)] * (len(own) + len(mate)),
+        + [ANY] * (len(own) + len(mate)),
         out_specs=pl.BlockSpec(memory_space=pltpu.VMEM),
-        out_shape=jax.ShapeDtypeStruct((line, 2, 2, part, depth), rows.dtype),
+        out_shape=pltpu.VMEM((line, 2, 2, part, depth), rows.dtype),
+        scratch_shapes=[pltpu.SemaphoreType.DMA((2, len(own), 2))],
         compiler_params=pltpu.CompilerParams(vmem_limit_bytes=VMEM_LIMIT),
         cost_estimate=pl.CostEstimate(
             flops=0, bytes_accessed=4 * line * 4 * part * depth, transcendentals=0
@@ -102,7 +114,7 @@
         functools.partial(transform_kernel, width, distances),
         grid_spec=grid_spec,
         out_shape=[jax.ShapeDtypeStruct((blocks, width, aux_slice), jnp.bfloat16)] * count,
-        compiler_params=pltpu.CompilerParams(vmem_limit_bytes=VMEM_LIMIT),
+        compiler_params=pltpu.CompilerParams(vmem_limit_bytes=VMEM_LIMIT - 2 * 1024 * 1024),
         cost_estimate=pl.CostEstimate(
             flops=2 * blocks * count * width * depth * aux_slice,
             bytes_accessed=2 * (near * width * depth + blocks * (depth + count * width) * aux_slice),

time: 361 us -> 360 us (level)
    unnamed x44 -> x46, local copies, waits for them, and re-layouts: 5.74 us -> 7.55 us
  transfers between devices with their start and end apart: 38 -> 38, of which waited for: 19 -> 19; matrix products, arithmetic and copies ran while one was open for 3% -> 3% of each run, Pallas kernels for 24% -> 23%
where the time goes in v7:
time: 360 us
  waiting for transfers between devices  191 us (53%)
  Pallas kernels  101 us (28%)
  starting transfers between devices  46.5 us (13%)
  local copies, waits for them, and re-layouts  15.7 us (4%)
    ppermute x29, waiting for transfers between devices, swap(): return lax.ppermute(value, axis, pairs)  107 us
    all_to_all x3, waiting for transfers between devices, per_device(): local = lax.all_to_all(sent, 'aux', split_axis=0, concat_axis=0, tiled=True)  62.7 us
    pallas_call x3, Pallas kernels, add_density(): pl.pallas_call(functools.partial(density_kernel, plan), grid_spec=pltpu.P...  59.1 us
    pallas_call x6, Pallas kernels, transform(): pl.pallas_call(functools.partial(transform_kernel, width, distances), gri...  31.4 us
    ppermute x6, waiting for transfers between devices, along(): return lax.ppermute(value, 'aux', pairs)  21.2 us
    ppermute x6, starting transfers between devices, along(): return lax.ppermute(value, 'aux', pairs)  17.8 us
    ppermute x29, starting transfers between devices, swap(): return lax.ppermute(value, axis, pairs)  16.1 us
    all_to_all x3, starting transfers between devices, per_device(): local = lax.all_to_all(sent, 'aux', split_axis=0, concat_axis=0, tiled=True)  12.6 us
  transfers between devices with their start and end apart: 38, of which 19 were waited for; matrix products, arithmetic and copies ran while one was open for 3% of the time, Pallas kernels for 23%

profile of v7, /device:TPU:0, one launch (start us, length us, event | category | flops | bytes accessed | tf_op | source)
XLA Modules:
  0.0 359.7 jit_solution(15069294930012957870)
XLA Ops:
  6.7 5.5 %collective-permute-done = bf16[80,1408]{1,0:T(8,128)(2,1)S(1)} collective-permute-done((bf16[80,1408]{1,0:T(8,128)(2,1)S(1)}, bf16[80,1408]{1,0:T(8,128)(2,1)S(1)}, u32[]{:S(2)}, u32[]{:S(2)}) %collective-permute-start) | collective-permute-done | bytes 225312 | tf_op jit(solution)/shard_map/ppermute | solution.py:18
  17.1 7.1 %collective-permute-done.1.refs_1_ = bf16[2,80,1408]{2,1,0:T(8,128)(2,1)S(1)} collective-permute-done((bf16[2,80,1408]{2,1,0:T(8,128)(2,1)S(1)}, bf16[2,80,1408]{2,1,0:T(8,128)(2,1)S(1)}, u32[]{:S(2)}, u32[]{:S(2)}) %collective-permute-start.1) | collective-permute-done | bytes 450592 | tf_op jit(solution)/shard_map/ppermute | solution.py:24
  24.2 5.2 %collective-permute-start.3 = (bf16[2,80,1408]{2,1,0:T(8,128)(2,1)S(1)}, bf16[2,80,1408]{2,1,0:T(8,128)(2,1)}, u32[]{:S(2)}, u32[]{:S(2)}) collective-permute-start(bf16[2,80,1408]{2,1,0:T(8,128)(2,1)S(1)} %collective-permute-done.1.refs_1_), channel_id=1, source_target_pairs={{0,8},{4,12},{8,16},{12,20},{16,24},{20,28},{1,9},{5,13},{9,17},{1... | collective-permute-start | bytes 1351688 | tf_op jit(solution)/shard_map/ppermute | solution.py:24
  31.3 5.0 %collective-permute-done.3.refs_3_ = bf16[2,80,1408]{2,1,0:T(8,128)(2,1)} collective-permute-done((bf16[2,80,1408]{2,1,0:T(8,128)(2,1)S(1)}, bf16[2,80,1408]{2,1,0:T(8,128)(2,1)}, u32[]{:S(2)}, u32[]{:S(2)}) %collective-permute-start.3) | collective-permute-done | bytes 450592 | tf_op jit(solution)/shard_map/ppermute | solution.py:24
  36.3 5.3 %collective-permute-start.5 = (bf16[2,80,1408]{2,1,0:T(8,128)(2,1)}, bf16[2,80,1408]{2,1,0:T(8,128)(2,1)}, u32[]{:S(2)}, u32[]{:S(2)}) collective-permute-start(bf16[2,80,1408]{2,1,0:T(8,128)(2,1)} %collective-permute-done.3.refs_3_), channel_id=1, source_target_pairs={{0,8},{4,12},{8,16},{12,20},{16,24},{20,28},{1,9},{5,13},{9,17},{1... | collective-permute-start | bytes 1351688 | tf_op jit(solution)/shard_map/ppermute | solution.py:24
  43.7 4.2 %collective-permute-done.5.refs_5_ = bf16[2,80,1408]{2,1,0:T(8,128)(2,1)} collective-permute-done((bf16[2,80,1408]{2,1,0:T(8,128)(2,1)}, bf16[2,80,1408]{2,1,0:T(8,128)(2,1)}, u32[]{:S(2)}, u32[]{:S(2)}) %collective-permute-start.5) | collective-permute-done | bytes 450592 | tf_op jit(solution)/shard_map/ppermute | solution.py:24
  47.8 4.9 %collective-permute-done.6.refs_6_ = bf16[2,80,1408]{2,1,0:T(8,128)(2,1)} collective-permute-done((bf16[2,80,1408]{2,1,0:T(8,128)(2,1)}, bf16[2,80,1408]{2,1,0:T(8,128)(2,1)}, u32[]{:S(2)}, u32[]{:S(2)}) %collective-permute-start.6) | collective-permute-done | bytes 450592 | tf_op jit(solution)/shard_map/ppermute | solution.py:24
  59.8 5.6 %transform.6 = (bf16[2,320,512]{2,1,0:T(8,128)(2,1)}, bf16[2,320,512]{2,1,0:T(8,128)(2,1)}) custom-call(s32[1]{0:T(128)} %bitcast.3.index_ref, bf16[1280,1408]{1,0:T(8,128)(2,1)} %bitcast.20, bf16[2,3,1408,512]{3,2,1,0:T(8,128)(2,1)} %bitcast.27), custom_call_target="tpu_custom_call" | custom-call | flops 1845493760 | bytes 7798784 | tf_op jit(solution)/shard_map/transform/pallas_call | solution.py:113
  65.3 5.0 %transform.7 = (bf16[2,320,512]{2,1,0:T(8,128)(2,1)}, bf16[2,320,512]{2,1,0:T(8,128)(2,1)}) custom-call(s32[1]{0:T(128)} %bitcast.3.index_ref, bf16[1280,1408]{1,0:T(8,128)(2,1)} %bitcast.21, bf16[2,1,1408,512]{3,2,1,0:T(8,128)(2,1)} %copy-done.3, bf16[2,320,512]{2,1,0:T(8,128)(2,1)} %get-tuple-element.17.refs_0_), custom_call_target="tpu_custom_call" | custom-call | flops 1845493760 | bytes 5996544 | tf_op jit(solution)/shard_map/transform/pallas_call | solution.py:113
  70.5 5.1 %transform.8 = (bf16[2,320,512]{2,1,0:T(8,128)(2,1)}, bf16[2,320,512]{2,1,0:T(8,128)(2,1)}) custom-call(s32[1]{0:T(128)} %bitcast.3.index_ref, bf16[1280,1408]{1,0:T(8,128)(2,1)} %bitcast.22, bf16[2,1,1408,512]{3,2,1,0:T(8,128)(2,1)} %collective-permute-done.15.half_ref), custom_call_target="tpu_custom_call" | custom-call | flops 1845493760 | bytes 5996544 | tf_op jit(solution)/shard_map/transform/pallas_call | solution.py:113
  81.4 4.1 %all-to-all-start = ((bf16[8,320,512]{2,1,0:T(8,128)(2,1)}), bf16[8,320,512]{2,1,0:T(8,128)(2,1)S(1)}, u32[]{:S(2)}, u32[]{:S(2)}) async-start(bf16[8,320,512]{2,1,0:T(8,128)(2,1)} %assemble.3), calls=%async_computation | async-start | bytes 5242880 | tf_op jit(solution)/shard_map/all_to_all | solution.py:445
  86.9 5.6 %transform.11 = (bf16[2,320,512]{2,1,0:T(8,128)(2,1)}, bf16[2,320,512]{2,1,0:T(8,128)(2,1)}) custom-call(s32[1]{0:T(128)} %bitcast.3.index_ref, bf16[1280,1408]{1,0:T(8,128)(2,1)} %bitcast.23, bf16[2,3,1408,512]{3,2,1,0:T(8,128)(2,1)} %bitcast.28), custom_call_target="tpu_custom_call" | custom-call | flops 1845493760 | bytes 7798784 | tf_op jit(solution)/shard_map/transform/pallas_call | solution.py:113
  94.5 8.7 %collective-permute-done.17.refs_0_.refs_2_ = bf16[2,320,512]{2,1,0:T(8,128)(2,1)S(1)} collective-permute-done((bf16[2,320,512]{2,1,0:T(8,128)(2,1)}, bf16[2,320,512]{2,1,0:T(8,128)(2,1)S(1)}, u32[]{:S(2)}, u32[]{:S(2)}) %collective-permute-start.17) | collective-permute-done | bytes 655392 | tf_op jit(solution)/shard_map/ppermute | solution.py:18
  104.1 5.0 %transform.9 = (bf16[2,320,512]{2,1,0:T(8,128)(2,1)}, bf16[2,320,512]{2,1,0:T(8,128)(2,1)}) custom-call(s32[1]{0:T(128)} %bitcast.3.index_ref, bf16[1280,1408]{1,0:T(8,128)(2,1)} %bitcast.24, bf16[2,3,1408,512]{3,2,1,0:T(8,128)(2,1)} %bitcast.29, bf16[2,320,512]{2,1,0:T(8,128)(2,1)} %copy-done.7), custom_call_target="tpu_custom_call" | custom-call | flops 1845493760 | bytes 5996544 | tf_op jit(solution)/shard_map/transform/pallas_call | solution.py:113
  109.1 5.1 %transform.10 = (bf16[2,320,512]{2,1,0:T(8,128)(2,1)}, bf16[2,320,512]{2,1,0:T(8,128)(2,1)}) custom-call(s32[1]{0:T(128)} %bitcast.3.index_ref, bf16[1280,1408]{1,0:T(8,128)(2,1)} %bitcast.25, bf16[2,3,1408,512]{3,2,1,0:T(8,128)(2,1)} %bitcast.30, bf16[2,320,512]{2,1,0:T(8,128)(2,1)} %get-tuple-element.23.refs_0_), custom_call_target="tpu_custom_call" | custom-call | flops 1845493760 | bytes 5996544 | tf_op jit(solution)/shard_map/transform/pallas_call | solution.py:113
  118.3 13.2 %collective-permute-done.21.refs_2_ = bf16[2,320,512]{2,1,0:T(8,128)(2,1)} collective-permute-done((bf16[2,320,512]{2,1,0:T(8,128)(2,1)}, bf16[2,320,512]{2,1,0:T(8,128)(2,1)}, u32[]{:S(2)}, u32[]{:S(2)}) %collective-permute-start.21) | collective-permute-done | bytes 655392 | tf_op jit(solution)/shard_map/ppermute | solution.py:18
  131.4 12.3 %collective-permute-done.22.refs_3_ = bf16[2,320,512]{2,1,0:T(8,128)(2,1)} collective-permute-done((bf16[2,320,512]{2,1,0:T(8,128)(2,1)}, bf16[2,320,512]{2,1,0:T(8,128)(2,1)}, u32[]{:S(2)}, u32[]{:S(2)}) %collective-permute-start.22) | collective-permute-done | bytes 655392 | tf_op jit(solution)/shard_map/ppermute | solution.py:18
  145.4 4.5 %all-to-all-start.1 = ((bf16[8,320,512]{2,1,0:T(8,128)(2,1)}), bf16[8,320,512]{2,1,0:T(8,128)(2,1)}, u32[]{:S(2)}, u32[]{:S(2)}) async-start(bf16[8,320,512]{2,1,0:T(8,128)(2,1)} %gate.4), calls=%async_computation.1 | async-start | bytes 5242880 | tf_op jit(solution)/shard_map/all_to_all | solution.py:445
  150.8 60.0 %all-to-all-done.1.refs_3_.refs_9_ = bf16[8,320,512]{2,1,0:T(8,128)(2,1)} async-done(((bf16[8,320,512]{2,1,0:T(8,128)(2,1)}), bf16[8,320,512]{2,1,0:T(8,128)(2,1)}, u32[]{:S(2)}, u32[]{:S(2)}) %all-to-all-start.1) | async-done | bytes 2621472 | tf_op jit(solution)/shard_map/all_to_all | solution.py:445
  218.6 51.2 %collective-permute-done.29.refs_11_ = bf16[8,320,512]{2,1,0:T(8,128)(2,1)} collective-permute-done((bf16[8,320,512]{2,1,0:T(8,128)(2,1)}, bf16[8,320,512]{2,1,0:T(8,128)(2,1)}, u32[]{:S(2)}, u32[]{:S(2)}) %collective-permute-start.29) | collective-permute-done | bytes 2621472 | tf_op jit(solution)/shard_map/ppermute | solution.py:18
  283.0 31.7 %density.2.refs_1_.refs_14_ = bf16[960,4096]{1,0:T(8,128)(2,1)} custom-call(s32[2]{0:T(128)} %get-tuple-element.29.distance_ref, f32[960,1]{1,0:T(8,128)} %sub.71.refs_0_, f32[1,1280]{1,0:T(1,128)} %reshape.65.refs_1_, bf16[8,320,512]{2,1,0:T(8,128)(2,1)} %copy-done.2, bf16[8,320,512]{2,1,0:T(8,128)(2,1)} %all-to-all-done.1.refs_3_.refs_9_, ...), custom_call_target="tpu_custom_call" | custom-call | flops 20132659200 | bytes 26214400 | tf_op jit(solution)/shard_map/density/pallas_call | solution.py:362
  314.7 7.6 %collective-permute-done.25.refs_0_ = bf16[6,320,512]{2,1,0:T(8,128)(2,1)} collective-permute-done((bf16[6,320,512]{2,1,0:T(8,128)(2,1)}, bf16[6,320,512]{2,1,0:T(8,128)(2,1)}, u32[]{:S(2)}, u32[]{:S(2)}) %collective-permute-start.25) | collective-permute-done | bytes 1966112 | tf_op jit(solution)/shard_map/ppermute | solution.py:18
  327.9 11.5 %integrals.1.refs_1_.refs_13_ = f32[960,640]{1,0:T(8,128)} custom-call(s32[2]{0:T(128)} %get-tuple-element.29.distance_ref, f32[960,1]{1,0:T(8,128)} %sub.71.refs_0_, f32[1,640]{1,0:T(1,128)} %reshape.61.refs_1_, bf16[8,320,512]{2,1,0:T(8,128)(2,1)} %copy-done.2, bf16[8,320,512]{2,1,0:T(8,128)(2,1)} %all-to-all-done.1.refs_3_.refs_9_, ...), custom_call_target="tpu_custom_call" | custom-call | flops 3774873600 | bytes 13598720 | tf_op jit(solution)/shard_map/integrals/pallas_call | solution.py:362
  343.6 15.9 %density.3 = bf16[960,4096]{1,0:T(8,128)(2,1)} custom-call(s32[2]{0:T(128)} %get-tuple-element.29.distance_ref, f32[960,1]{1,0:T(8,128)} %sub.71.refs_0_, f32[1,640]{1,0:T(1,128)} %reshape.61.refs_1_, bf16[8,320,512]{2,1,0:T(8,128)(2,1)} %copy-done.2, bf16[8,320,512]{2,1,0:T(8,128)(2,1)} %all-to-all-done.1.refs_3_.refs_9_, bf16[8,320,512]{2,1,0:T(8,128)(2,1)} %copy-done.1, ...), custom_call_target="tpu_custom_call" | custom-call | flops 6291456000 | bytes 22937600 | tf_op jit(solution)/shard_map/density/pallas_call | solution.py:362
  (132 shorter events, 68.8 us)
Async XLA Ops:
  2.1 68.4 %collective-permute-start.15 = (bf16[2,1,1408,512]{3,2,1,0:T(8,128)(2,1)S(1)}, bf16[2,1,1408,512]{3,2,1,0:T(8,128)(2,1)}, u32[]{:S(2)}, u32[]{:S(2)}) collective-permute-start(bf16[2,1,1408,512]{3,2,1,0:T(8,128)(2,1)S(1)} %slice.37.half_ref), channel_id=1, source_target_pairs={{0,2},{1,3},{2,0},{3,1},{4,6},{5,7},{6,4},{7,5},{8,10},{9,11},{10,... | collective-permute-start | bytes 8650760 | tf_op jit(solution)/shard_map/ppermute | solution.py:18
  15.7 13.6 %collective-permute-start.2 = (bf16[2,80,1408]{2,1,0:T(8,128)(2,1)S(1)}, bf16[2,80,1408]{2,1,0:T(8,128)(2,1)S(1)}, u32[]{:S(2)}, u32[]{:S(2)}) collective-permute-start(bf16[2,80,1408]{2,1,0:T(8,128)(2,1)S(1)} %pad_maximum_fusion.refs_0_), channel_id=1, source_target_pairs={{8,0},{12,4},{16,8},{20,12},{24,16},{28,20},{9,1},{13,5},{17,9},{2... | collective-permute-start | bytes 1351688 | tf_op jit(solution)/shard_map/ppermute | solution.py:24
  17.0 13.7 %collective-permute-start.7 = (bf16[2,80,1408]{2,1,0:T(8,128)(2,1)S(1)}, bf16[2,80,1408]{2,1,0:T(8,128)(2,1)S(1)}, u32[]{:S(2)}, u32[]{:S(2)}) collective-permute-start(bf16[2,80,1408]{2,1,0:T(8,128)(2,1)S(1)} %pad_maximum_fusion.refs_0_), channel_id=1, source_target_pairs={{0,1},{1,0},{2,3},{3,2},{4,5},{5,4},{6,7},{7,6},{8,9},{9,8},{10,11... | collective-permute-start | bytes 1351688 | tf_op jit(solution)/shard_map/ppermute | solution.py:18
  29.4 12.2 %collective-permute-start.4 = (bf16[2,80,1408]{2,1,0:T(8,128)(2,1)S(1)}, bf16[2,80,1408]{2,1,0:T(8,128)(2,1)}, u32[]{:S(2)}, u32[]{:S(2)}) collective-permute-start(bf16[2,80,1408]{2,1,0:T(8,128)(2,1)S(1)} %collective-permute-done.2.refs_2_), channel_id=1, source_target_pairs={{8,0},{12,4},{16,8},{20,12},{24,16},{28,20},{9,1},{13,5},{17,9},{2... | collective-permute-start | bytes 1351688 | tf_op jit(solution)/shard_map/ppermute | solution.py:24
  30.7 12.2 %collective-permute-start.8 = (bf16[2,80,1408]{2,1,0:T(8,128)(2,1)S(1)}, bf16[2,80,1408]{2,1,0:T(8,128)(2,1)S(1)}, u32[]{:S(2)}, u32[]{:S(2)}) collective-permute-start(bf16[2,80,1408]{2,1,0:T(8,128)(2,1)S(1)} %collective-permute-done.1.refs_1_), channel_id=1, source_target_pairs={{0,1},{1,0},{2,3},{3,2},{4,5},{5,4},{6,7},{7,6},{8,9},{9,8},{10,11... | collective-permute-start | bytes 1351688 | tf_op jit(solution)/shard_map/ppermute | solution.py:18
  30.8 12.2 %collective-permute-start.9 = (bf16[2,80,1408]{2,1,0:T(8,128)(2,1)S(1)}, bf16[2,80,1408]{2,1,0:T(8,128)(2,1)S(1)}, u32[]{:S(2)}, u32[]{:S(2)}) collective-permute-start(bf16[2,80,1408]{2,1,0:T(8,128)(2,1)S(1)} %collective-permute-done.2.refs_2_), channel_id=1, source_target_pairs={{0,1},{1,0},{2,3},{3,2},{4,5},{5,4},{6,7},{7,6},{8,9},{9,8},{10,11... | collective-permute-start | bytes 1351688 | tf_op jit(solution)/shard_map/ppermute | solution.py:18
  81.4 64.1 %all-to-all-start = ((bf16[8,320,512]{2,1,0:T(8,128)(2,1)}), bf16[8,320,512]{2,1,0:T(8,128)(2,1)S(1)}, u32[]{:S(2)}, u32[]{:S(2)}) async-start(bf16[8,320,512]{2,1,0:T(8,128)(2,1)} %assemble.3), calls=%async_computation | async-start | bytes 5242880 | tf_op jit(solution)/shard_map/all_to_all | solution.py:445
  85.4 17.8 %collective-permute-start.17 = (bf16[2,320,512]{2,1,0:T(8,128)(2,1)}, bf16[2,320,512]{2,1,0:T(8,128)(2,1)S(1)}, u32[]{:S(2)}, u32[]{:S(2)}) collective-permute-start(bf16[2,320,512]{2,1,0:T(8,128)(2,1)} %get-tuple-element.22), channel_id=1, source_target_pairs={{0,2},{1,3},{2,0},{3,1},{4,6},{5,7},{6,4},{7,5},{8,10},{9,11},{10,... | collective-permute-start | bytes 1966088 | tf_op jit(solution)/shard_map/ppermute | solution.py:18
  86.1 29.5 %collective-permute-start.19 = (bf16[2,320,512]{2,1,0:T(8,128)(2,1)}, bf16[2,320,512]{2,1,0:T(8,128)(2,1)}, u32[]{:S(2)}, u32[]{:S(2)}) collective-permute-start(bf16[2,320,512]{2,1,0:T(8,128)(2,1)} %get-tuple-element.17.refs_0_), channel_id=1, source_target_pairs={{0,3},{1,2},{2,1},{3,0},{4,7},{5,6},{6,5},{7,4},{8,11},{9,10},{10,... | collective-permute-start | bytes 1966088 | tf_op jit(solution)/shard_map/ppermute | solution.py:18
  92.5 39.0 %collective-permute-start.21 = (bf16[2,320,512]{2,1,0:T(8,128)(2,1)}, bf16[2,320,512]{2,1,0:T(8,128)(2,1)}, u32[]{:S(2)}, u32[]{:S(2)}) collective-permute-start(bf16[2,320,512]{2,1,0:T(8,128)(2,1)} %get-tuple-element.26), channel_id=1, source_target_pairs={{0,2},{1,3},{2,0},{3,1},{4,6},{5,7},{6,4},{7,5},{8,10},{9,11},{10,... | collective-permute-start | bytes 1966088 | tf_op jit(solution)/shard_map/ppermute | solution.py:18
  93.1 50.7 %collective-permute-start.22 = (bf16[2,320,512]{2,1,0:T(8,128)(2,1)}, bf16[2,320,512]{2,1,0:T(8,128)(2,1)}, u32[]{:S(2)}, u32[]{:S(2)}) collective-permute-start(bf16[2,320,512]{2,1,0:T(8,128)(2,1)} %get-tuple-element.27), channel_id=1, source_target_pairs={{0,3},{1,2},{2,1},{3,0},{4,7},{5,6},{6,5},{7,4},{8,11},{9,10},{10,... | collective-permute-start | bytes 1966088 | tf_op jit(solution)/shard_map/ppermute | solution.py:18
  114.2 29.5 %collective-permute-start.20 = (bf16[2,320,512]{2,1,0:T(8,128)(2,1)}, bf16[2,320,512]{2,1,0:T(8,128)(2,1)S(1)}, u32[]{:S(2)}, u32[]{:S(2)}) collective-permute-start(bf16[2,320,512]{2,1,0:T(8,128)(2,1)} %get-tuple-element.25), channel_id=1, source_target_pairs={{0,1},{1,0},{2,3},{3,2},{4,5},{5,4},{6,7},{7,6},{8,9},{9,8},{10,11... | collective-permute-start | bytes 1966088 | tf_op jit(solution)/shard_map/ppermute | solution.py:18
  145.4 65.3 %all-to-all-start.1 = ((bf16[8,320,512]{2,1,0:T(8,128)(2,1)}), bf16[8,320,512]{2,1,0:T(8,128)(2,1)}, u32[]{:S(2)}, u32[]{:S(2)}) async-start(bf16[8,320,512]{2,1,0:T(8,128)(2,1)} %gate.4), calls=%async_computation.1 | async-start | bytes 5242880 | tf_op jit(solution)/shard_map/all_to_all | solution.py:445
  150.0 64.0 %collective-permute-start.23 = (bf16[8,320,512]{2,1,0:T(8,128)(2,1)S(1)}, bf16[8,320,512]{2,1,0:T(8,128)(2,1)}, u32[]{:S(2)}, u32[]{:S(2)}) collective-permute-start(bf16[8,320,512]{2,1,0:T(8,128)(2,1)S(1)} %all-to-all-done.refs_2_.refs_5_), channel_id=1, source_target_pairs={{0,2},{1,3},{2,0},{3,1},{4,6},{5,7},{6,4},{7,5},{8,10},{9,11},{10,... | collective-permute-start | bytes 7864328 | tf_op jit(solution)/shard_map/ppermute | solution.py:18
  210.8 59.0 %collective-permute-start.29 = (bf16[8,320,512]{2,1,0:T(8,128)(2,1)}, bf16[8,320,512]{2,1,0:T(8,128)(2,1)}, u32[]{:S(2)}, u32[]{:S(2)}) collective-permute-start(bf16[8,320,512]{2,1,0:T(8,128)(2,1)} %all-to-all-done.1.refs_3_.refs_9_), channel_id=1, source_target_pairs={{0,2},{1,3},{2,0},{3,1},{4,6},{5,7},{6,4},{7,5},{8,10},{9,11},{10,... | collective-permute-start | bytes 7864328 | tf_op jit(solution)/shard_map/ppermute | solution.py:18
  214.0 63.2 %all-to-all-start.2 = ((bf16[8,320,512]{2,1,0:T(8,128)(2,1)}), bf16[8,320,512]{2,1,0:T(8,128)(2,1)S(1)}, u32[]{:S(2)}, u32[]{:S(2)}) async-start(bf16[8,320,512]{2,1,0:T(8,128)(2,1)} %gate.5), calls=%async_computation.2 | async-start | bytes 5242880 | tf_op jit(solution)/shard_map/all_to_all | solution.py:445
  218.0 65.0 %collective-permute-start.28 = (bf16[8,320,512]{2,1,0:T(8,128)(2,1)}, bf16[8,320,512]{2,1,0:T(8,128)(2,1)}, u32[]{:S(2)}, u32[]{:S(2)}) collective-permute-start(bf16[8,320,512]{2,1,0:T(8,128)(2,1)} %all-to-all-done.1.refs_3_.refs_9_), channel_id=1, source_target_pairs={{0,1},{1,0},{2,3},{3,2},{4,5},{5,4},{6,7},{7,6},{8,9},{9,8},{10,11... | collective-permute-start | bytes 7864328 | tf_op jit(solution)/shard_map/ppermute | solution.py:18
  218.1 64.9 %collective-permute-start.26 = (bf16[8,320,512]{2,1,0:T(8,128)(2,1)}, bf16[8,320,512]{2,1,0:T(8,128)(2,1)}, u32[]{:S(2)}, u32[]{:S(2)}) collective-permute-start(bf16[8,320,512]{2,1,0:T(8,128)(2,1)} %copy-done.2), channel_id=1, source_target_pairs={{0,1},{1,0},{2,3},{3,2},{4,5},{5,4},{6,7},{7,6},{8,9},{9,8},{10,11... | collective-permute-start | bytes 7864328 | tf_op jit(solution)/shard_map/ppermute | solution.py:18
  269.7 13.3 %collective-permute-start.30 = (bf16[8,320,512]{2,1,0:T(8,128)(2,1)}, bf16[8,320,512]{2,1,0:T(8,128)(2,1)}, u32[]{:S(2)}, u32[]{:S(2)}) collective-permute-start(bf16[8,320,512]{2,1,0:T(8,128)(2,1)} %collective-permute-done.29.refs_11_), channel_id=1, source_target_pairs={{0,1},{1,0},{2,3},{3,2},{4,5},{5,4},{6,7},{7,6},{8,9},{9,8},{10,11... | collective-permute-start | bytes 7864328 | tf_op jit(solution)/shard_map/ppermute | solution.py:18
  269.7 13.3 %collective-permute-start.27 = (bf16[8,320,512]{2,1,0:T(8,128)(2,1)}, bf16[8,320,512]{2,1,0:T(8,128)(2,1)}, u32[]{:S(2)}, u32[]{:S(2)}) collective-permute-start(bf16[8,320,512]{2,1,0:T(8,128)(2,1)} %collective-permute-done.23.refs_1_.refs_7_), channel_id=1, source_target_pairs={{0,1},{1,0},{2,3},{3,2},{4,5},{5,4},{6,7},{7,6},{8,9},{9,8},{10,11... | collective-permute-start | bytes 7864328 | tf_op jit(solution)/shard_map/ppermute | solution.py:18
  278.7 43.7 %collective-permute-start.25 = (bf16[6,320,512]{2,1,0:T(8,128)(2,1)}, bf16[6,320,512]{2,1,0:T(8,128)(2,1)}, u32[]{:S(2)}, u32[]{:S(2)}) collective-permute-start(bf16[6,320,512]{2,1,0:T(8,128)(2,1)} %slice.38.refs_5_), channel_id=1, source_target_pairs={{0,2},{1,3},{2,0},{3,1},{4,6},{5,7},{6,4},{7,5},{8,10},{9,11},{10,... | collective-permute-start | bytes 5898248 | tf_op jit(solution)/shard_map/ppermute | solution.py:18
  283.0 41.8 %collective-permute-start.24 = (bf16[6,320,512]{2,1,0:T(8,128)(2,1)}, bf16[6,320,512]{2,1,0:T(8,128)(2,1)S(1)}, u32[]{:S(2)}, u32[]{:S(2)}) collective-permute-start(bf16[6,320,512]{2,1,0:T(8,128)(2,1)} %slice.38.refs_5_), channel_id=1, source_target_pairs={{0,1},{1,0},{2,3},{3,2},{4,5},{5,4},{6,7},{7,6},{8,9},{9,8},{10,11... | collective-permute-start | bytes 5898248 | tf_op jit(solution)/shard_map/ppermute | solution.py:18
  322.4 17.1 %collective-permute-start.33 = (bf16[2,320,512]{2,1,0:T(8,128)(2,1)S(1)}, bf16[2,320,512]{2,1,0:T(8,128)(2,1)S(1)}, u32[]{:S(2)}, u32[]{:S(2)}) collective-permute-start(bf16[2,320,512]{2,1,0:T(8,128)(2,1)S(1)} %copy-done.6), channel_id=1, source_target_pairs={{0,2},{1,3},{2,0},{3,1},{4,6},{5,7},{6,4},{7,5},{8,10},{9,11},{10,... | collective-permute-start | bytes 1966088 | tf_op jit(solution)/shard_map/ppermute | solution.py:18
  324.6 15.8 %collective-permute-start.32 = (bf16[2,320,512]{2,1,0:T(8,128)(2,1)S(1)}, bf16[2,320,512]{2,1,0:T(8,128)(2,1)}, u32[]{:S(2)}, u32[]{:S(2)}) collective-permute-start(bf16[2,320,512]{2,1,0:T(8,128)(2,1)S(1)} %copy-done.6), channel_id=1, source_target_pairs={{0,1},{1,0},{2,3},{3,2},{4,5},{5,4},{6,7},{7,6},{8,9},{9,8},{10,11... | collective-permute-start | bytes 1966088 | tf_op jit(solution)/shard_map/ppermute | solution.py:18
  (37 other events, 448.3 us)
